TPU v7x, 32 devices: a whole 2x2x4 slice. The times are simulated.
32 devices in a mesh: blk: 8 (over z, core), rep: 4 (over y, x).
Axes of the slice: x: 2, y: 2, z: 4, core: 2. Of those that a mesh axis runs over, the one named last changes fastest.
Arguments:
- t_slab: bfloat16 [4, 1024, 8, 1024], P('rep', 'blk'), may hold values from -12 to 12
- w_cycle: bfloat16 [4, 1, 1024, 1024], P('rep'), may hold values from -0.75 to 0.75
- k_irrep: int32 [4], P('rep'), may hold values from 0 to 7
- i_irrep: int32 [8], replicated, may hold values from 0 to 7, as said below
- j_irrep: int32 [1], replicated, may hold values from 0 to 7
- tile_irrep: int32 [8], replicated, may hold values from 0 to 7, each once
- i_energy: float32 [8], replicated, may hold values from -2.5 to -0.5
- j_energy: float32 [1], replicated, may hold values from -2.5 to -0.5
- vir_energy: float32 [1024], replicated, may hold values from 0.3 to 3
Outputs:
- amplitude_update: float32 [1, 8, 1024, 1024], P(None, None, 'blk', 'rep')
Inputs may be any that keep to these rules, and one draw needn't show every extreme that they name: tile_irrep holds each of the 8 irreps exactly once. The orbitals i come in 8 runs of 1 consecutive orbitals; i_irrep is the same within a run, and each irrep labels exactly one run.
All inputs are finite; a program needn't handle non-finite values.
Results may differ from a plain program's by a relative error of at most 0.0003.
Values may be sent and summed in bfloat16 or wider, within the bound.
No kernel may reach another device: no remote copies, remote signals or barrier semaphores. Data moves between devices by JAX's collectives and lax.ppermute only.
A program may use at most 64 MiB of HBM per device.

v0:
```python
import jax
import jax.numpy as jnp
from jax import lax
from jax.sharding import PartitionSpec as P

TILE = 128


def label_virtual(tile_irrep, count):
    tile_of = jnp.arange(count, dtype=jnp.int32) // TILE
    tiles = jnp.arange(tile_irrep.shape[0], dtype=jnp.int32)
    return jnp.sum(jnp.where(tile_of[:, None] == tiles[None, :], tile_irrep[None, :], 0), axis=1)


def masked(block, first_label, second_label, third_label, fourth_label):
    first = jnp.bitwise_xor(first_label[:, None, None, None], second_label[None, :, None, None])
    second = jnp.bitwise_xor(third_label[None, None, :, None], fourth_label[None, None, None, :])
    keep = jnp.bitwise_xor(first, second) == 0
    return jnp.where(keep, block, jnp.zeros((), block.dtype))


def shards(t_slab, w_cycle, k_irrep, i_irrep, j_irrep, tile_irrep, i_energy, j_energy, vir_energy):
    blk_count = lax.axis_size("blk")
    rep_count = lax.axis_size("rep")
    k_rows, c_width, rows_i, full_width = t_slab.shape
    rows_j = w_cycle.shape[1]
    vir_irrep = label_virtual(tile_irrep, full_width)
    a_width = full_width // blk_count
    b_width = full_width // rep_count
    a_start = lax.axis_index("blk") * a_width
    b_start = lax.axis_index("rep") * b_width
    c_label = lax.dynamic_slice_in_dim(vir_irrep, lax.axis_index("blk") * c_width, c_width, 0)
    held = masked(t_slab, k_irrep, c_label, i_irrep, vir_irrep)
    outgoing = held.reshape(k_rows, c_width, rows_i, blk_count, a_width).transpose(3, 0, 1, 2, 4)
    outgoing = outgoing.reshape(blk_count, k_rows * c_width, rows_i * a_width)
    arrived = lax.all_to_all(outgoing, "blk", split_axis=0, concat_axis=0, tiled=True)
    left_side = arrived.reshape(blk_count, k_rows, c_width, rows_i * a_width).transpose(1, 0, 2, 3)
    left_side = left_side.reshape(k_rows, full_width, rows_i * a_width)
    right_side = masked(w_cycle, k_irrep, j_irrep, vir_irrep, vir_irrep)
    right_side = right_side.transpose(0, 2, 1, 3).reshape(k_rows, full_width, rows_j * full_width)
    partial_value = lax.dot_general(
        left_side, right_side, (((0, 1), (0, 1)), ((), ())), preferred_element_type=jnp.float32
    )
    arranged = partial_value.reshape(rows_i * a_width, rows_j, rep_count, b_width).transpose(
        0, 2, 1, 3
    )
    arranged = arranged.reshape(rows_i * a_width, rep_count * rows_j * b_width)
    summed = lax.psum_scatter(arranged, "rep", scatter_dimension=1, tiled=True)
    result = summed.reshape(rows_i, a_width, rows_j, b_width)
    result = result.transpose(2, 0, 1, 3)
    b_energy = lax.dynamic_slice_in_dim(vir_energy, b_start, b_width, 0)
    a_energy = lax.dynamic_slice_in_dim(vir_energy, a_start, a_width, 0)
    denom = (
        a_energy[None, None, :, None]
        + b_energy[None, None, None, :]
        - i_energy[None, :, None, None]
        - j_energy[:, None, None, None]
    )
    return result / denom


def solution(mesh):
    in_specs = (
        P("rep", "blk", None, None),
        P("rep", None, None, None),
        P("rep"),
        P(),
        P(),
        P(),
        P(),
        P(),
        P(),
    )
    out_specs = P(None, None, "blk", "rep")
    return jax.shard_map(shards, mesh=mesh, in_specs=in_specs, out_specs=out_specs, check_vma=False)
```

profile of v0, /device:TPU:0, one launch (start us, length us, event | category | flops | bytes accessed | tf_op | source)
XLA Modules:
  0.0 136.1 jit_solution(11329956933410268085)
XLA Ops:
  7.2 0.7 select_reduce_fusion
  7.9 0.7 broadcast_xor_fusion
  8.7 0.1 dynamic-slice_xor_fusion
  8.7 2.3 %copy_bitcast_fusion = bf16[8,1,128,8,128]{4,3,2,0,1:T(8,128)(2,1)S(1)} fusion(bf16[1,128,8,1024]{3,2,1,0:T(8,128)(2,1)} %param.9, s32[8,1024]{1,0:T(8,128)S(1)} %broadcast_xor_fusion, s32[128]{0:T(128)S(1)} %dynamic-slice_xor_fusion), kind=kLoop, calls=%fused_computation.7 | loop fusion | flops 3145728 | bytes 4227584 | tf_op jit(solution)/shard_map/transpose | solution.py:34
  11.1 2.3 %reshape.197 = bf16[8,128,1024]{2,1,0:T(8,128)(2,1)} reshape(bf16[8,1,128,8,128]{4,3,2,0,1:T(8,128)(2,1)S(1)} %copy_bitcast_fusion) | data formatting | bytes 4194304 | tf_op jit(solution)/shard_map/reshape | solution.py:35
  13.4 6.3 %all-to-all-start = ((bf16[8,128,1024]{2,1,0:T(8,128)(2,1)}), bf16[8,128,1024]{2,1,0:T(8,128)(2,1)S(1)}, u32[]{:S(2)}, u32[]{:S(2)}) async-start(bf16[8,128,1024]{2,1,0:T(8,128)(2,1)} %reshape.197), calls=%async_computation | async-start | bytes 4194304 | tf_op jit(solution)/shard_map/all_to_all | solution.py:36
  19.7 0.0 reduce-scatter.2.cloned.1.call-start
  20.4 48.4 %all-to-all-done = bf16[8,128,1024]{2,1,0:T(8,128)(2,1)S(1)} async-done(((bf16[8,128,1024]{2,1,0:T(8,128)(2,1)}), bf16[8,128,1024]{2,1,0:T(8,128)(2,1)S(1)}, u32[]{:S(2)}, u32[]{:S(2)}) %all-to-all-start) | async-done | bytes 2097184 | tf_op jit(solution)/shard_map/all_to_all | solution.py:36
  68.8 6.3 %fusion.4 = f32[1024,1024]{1,0:T(8,128)} fusion(bf16[1024,1024]{1,0:T(8,128)(2,1)S(1)} %bitcast.20, bf16[1,1,1024,1024]{3,2,1,0:T(8,128)(2,1)} %param.10, s32[1024]{0:T(1024)S(1)} %select_reduce_fusion, s32[]{:T(128)} %bitcast.4), kind=kOutput, calls=%fused_computation.6 | convolution fusion | flops 2151677952 | bytes 8392708 | tf_op jit(solution)/shard_map/dot_general | solution.py:41
  75.1 0.0 copy-start
  75.1 0.0 reduce-scatter.2.cloned.1.call-update
  75.8 0.8 dynamic_slice.10
  76.6 0.8 dynamic_slice.11
  77.3 0.1 broadcast_add_fusion
  77.4 49.5 %reduce-scatter.2.cloned.1.call-done = f32[1024,256]{1,0:T(8,128)} async-done(((f32[1024,1024]{1,0:T(8,128)}), f32[1024,256]{1,0:T(8,128)}) %reduce-scatter.2.cloned.1.call-update) | async-done | bytes 1048592 | tf_op jit(solution)/shard_map/reduce_scatter | solution.py:48
  126.9 0.0 copy-done
  126.9 2.4 %subtract_divide_fusion = f32[1,8,128,256]{3,2,1,0:T(8,128)} fusion(f32[1,8,128,256]{3,2,1,0:T(8,128)} %bitcast.21, f32[]{:T(128)} %bitcast.19, f32[8]{0:T(128)S(1)} %copy-done, f32[128,256]{1,0:T(8,128)S(1)} %broadcast_add_fusion), kind=kLoop, calls=%fused_computation.12 | loop fusion | flops 786432 | bytes 2228260 | tf_op jit(solution)/shard_map/div | solution.py:59
  (1 shorter events, 0.0 us)
Async XLA Ops:
  13.4 55.4 %all-to-all-start = ((bf16[8,128,1024]{2,1,0:T(8,128)(2,1)}), bf16[8,128,1024]{2,1,0:T(8,128)(2,1)S(1)}, u32[]{:S(2)}, u32[]{:S(2)}) async-start(bf16[8,128,1024]{2,1,0:T(8,128)(2,1)} %reshape.197), calls=%async_computation | async-start | bytes 4194304 | tf_op jit(solution)/shard_map/all_to_all | solution.py:36
  19.7 107.2 %reduce-scatter.2.cloned.1.call-start = ((), (), s32[]{:S(2)}) async-start(), calls=%async_computation.2 | async-start | bytes 5242880 | tf_op jit(solution)/shard_map/reduce_scatter | solution.py:48
  75.1 51.8 %copy-start = (f32[8]{0:T(128)S(1)}, f32[8]{0:T(128)}, u32[]{:S(2)}) copy-start(f32[8]{0:T(128)} %param.15) | copy-start | bytes 100
Sparse Core Ops, SparseCore 0:
  75.3 51.5 reduce-scatter.1
where the time goes:
time: 137 us; the launch traced here: 136 us
  waiting for transfers between devices  97.9 us (71%)
  between operations  15.4 us (11%)
  other arithmetic  6.38 us (5%)
  starting transfers between devices  6.36 us (5%)
  matrix products  6.32 us (5%)
  local copies, waits for them, and re-layouts  3.85 us (3%)
    reduce_scatter x1, waiting for transfers between devices, shards(): summed = lax.psum_scatter(arranged, 'rep', scatter_dimension=1, tiled=True)  49.5 us
    all_to_all x1, waiting for transfers between devices, shards(): lax.all_to_all(outgoing, 'blk', split_axis=0, concat_axis=0, tiled=True)  48.4 us
    all_to_all x1, starting transfers between devices, shards(): lax.all_to_all(outgoing, 'blk', split_axis=0, concat_axis=0, tiled=True)  6.33 us
    dot_general x1, matrix products, shards(): lax.dot_general(left_side, right_side, (((0, 1), (0, 1)), ((), ())), pref...  6.32 us
  transfers between devices with their start and end apart: 2, of which 2 were waited for; matrix products, arithmetic and copies ran while one was open for 1% of the time, Pallas kernels for 0%

commit v1 on v0

v1 whole, which is shorter than its diff:
```python
import jax
import jax.numpy as jnp
from jax import lax
from jax.experimental import pallas as pl
from jax.experimental.pallas import tpu as pltpu
from jax.sharding import PartitionSpec as P

TILE = 128
CHUNK = 256
HALVES = 2
POWER = 17
TOP = 128.0
LEAST = 2.0**-100
SMALLEST = 2.0**-126
SPARE = 16


def vmem():
    return pl.BlockSpec(memory_space=pltpu.VMEM)


def hbm():
    return pl.BlockSpec(memory_space=pltpu.HBM)


def small(array):
    return pltpu.SMEM(array.shape, array.dtype)


def limit(mebibytes):
    return pltpu.CompilerParams(vmem_limit_bytes=mebibytes * 2**20)


def place_of(ref, stride, label):
    found = jnp.int32(0)
    for n in range(ref.shape[0] // stride):
        found = jnp.where(ref[n * stride] == label, jnp.int32(n), found)
    return found


def start_all(sources, targets, sems):
    copies = []
    for n, (source, target) in enumerate(zip(sources, targets)):
        copies.append(pltpu.make_async_copy(source, target, sems.at[n]))
        copies[-1].start()
    return copies


def pack_kernel(plan, *refs):
    rows_i, run, c_width, by_partner, tiles_b, groups, steps = plan
    if steps:
        k_hbm, i_hbm, tile_hbm, t_hbm, j_hbm, w_hbm, *refs = refs
        *refs, j_ref, w_sems = refs
    else:
        k_hbm, i_hbm, tile_hbm, t_hbm, *refs = refs
        outs_hbm, refs = refs[: len(groups)], refs[len(groups) :]
        *refs, out_sems = refs
    *refs, k_ref, i_ref, tile_ref, t_ref, small_sems, t_sems = refs
    out_refs = refs[: len(groups)]
    runs = rows_i // run
    rows = CHUNK // runs
    sources, targets = [k_hbm, i_hbm, tile_hbm], [k_ref, i_ref, tile_ref]
    if steps:
        sources.append(j_hbm)
        targets.append(j_ref)
    small_copies = start_all(sources, targets, small_sems)
    me = lax.axis_index("blk") if by_partner else 0
    places = {
        step: (out_ref, spot)
        for out_ref, group in zip(out_refs, groups)
        for spot, step in enumerate(group)
    }
    pairs = [step for step in places if step % 2 == 0]
    columns = [
        pl.ds(pl.multiple_of(((me ^ step) | 1) * TILE - TILE, 2 * TILE), 2 * TILE)
        for step in pairs
    ]
    depth = t_ref.shape[1] // HALVES
    spans = [(n, pl.ds(half * depth, depth)) for n in range(len(pairs)) for half in range(HALVES)]
    t_copies = start_all(
        [t_hbm.at[span, columns[n]] for n, span in spans],
        [t_ref.at[n, span] for n, span in spans],
        t_sems,
    )
    row = lax.broadcasted_iota(jnp.int32, (rows, CHUNK), 0)
    col = lax.broadcasted_iota(jnp.int32, (rows, CHUNK), 1)
    run_bits = run.bit_length() - 1
    same_c = (row >> run_bits) == (col >> (rows_i.bit_length() - 1))
    same_m = (row & (run - 1)) == (col & (run - 1))
    of_run = jnp.where(same_c & same_m, (col >> run_bits) & (runs - 1), -1)
    own_tile = lax.axis_index("blk") * c_width // TILE
    for copy in small_copies:
        copy.wait()
    w_copies = []
    if steps:
        w_ref, choice_ref = refs[len(groups) :]
        side = lax.axis_index("rep") * tiles_b if by_partner else 0
        flip = len(steps) - tiles_b if by_partner else 0
        label_w = k_ref[0] ^ j_ref[0]
        spot_row = lax.broadcasted_iota(jnp.int32, choice_ref.shape[1:], 0)
        for n in range(len(steps)):
            b_tile = n ^ flip ^ side
            c_tile = place_of(tile_ref, 1, label_w ^ tile_ref[b_tile])
            source = w_hbm.at[
                pl.ds(pl.multiple_of(c_tile * TILE, TILE), TILE),
                pl.ds(pl.multiple_of(b_tile * TILE, TILE), TILE),
            ]
            target = w_ref.at[:, pl.ds(n * TILE, TILE)]
            w_copies.append(pltpu.make_async_copy(source, target, w_sems.at[n]))
            w_copies[-1].start()
            spot = jnp.int32(0)
            for where, step in enumerate(steps):
                spot = jnp.where((c_tile ^ me) == step, jnp.int32(where), spot)
            choice_ref[n] = jnp.where(spot_row == spot, 1.0, 0.0)
    label = k_ref[0] ^ tile_ref[own_tile]
    picks = []
    for step in pairs:
        rows_of_pair = []
        for own in (step, step + 1):
            chosen = place_of(i_ref, run, label ^ tile_ref[me ^ own])
            rows_of_pair.append(jnp.where(of_run == chosen, 1.0, 0.0).astype(jnp.bfloat16))
        picks.append(jnp.concatenate(rows_of_pair, axis=0))
    swapped = (me & 1) == 1
    out_copies = []
    for n, step in enumerate(pairs):
        for chunk in range(t_ref.shape[1] // CHUNK):
            if chunk * CHUNK % depth == 0:
                t_copies[n * HALVES + chunk * CHUNK // depth].wait()
            block = t_ref[n, chunk * CHUNK : (chunk + 1) * CHUNK, :]
            kept = jnp.dot(picks[n], block, preferred_element_type=jnp.float32)
            low, high = kept[:, :TILE], kept[:, TILE:]
            for own, here, other in ((step, low, high), (step + 1, high, low)):
                half = slice((own - step) * rows, (own - step + 1) * rows)
                out_ref, spot = places[own]
                value = jnp.where(swapped, other[half], here[half])
                out_ref[spot, chunk * rows : (chunk + 1) * rows, :] = value.astype(out_ref.dtype)
        if not steps:
            out_copies.append(pltpu.make_async_copy(out_ref, outs_hbm[n], out_sems.at[n]))
            out_copies[-1].start()
    for copy in w_copies + out_copies:
        copy.wait()


def write_coded(out_ref, value):
    rows, width = value.shape
    largest = jnp.max(jnp.max(jnp.abs(value), axis=0, keepdims=True), axis=1, keepdims=True)
    exponent = jnp.ceil(jnp.log2(jnp.maximum(largest, LEAST)))
    scaled = value * (TOP * jnp.exp2(-exponent))
    power = scaled
    for _ in range(POWER.bit_length() - 1):
        power = power * power
    out_ref[:rows, :] = (power * scaled).astype(out_ref.dtype)
    out_ref[rows:, :] = jnp.broadcast_to(exponent, (SPARE, width)).astype(out_ref.dtype)


def read_coded(ref):
    rows = ref.shape[0] - SPARE
    power = ref[:rows, :].astype(jnp.float32)
    exponent = ref[rows:, :].astype(jnp.float32)[:1, :]
    size = jnp.exp2(jnp.log2(jnp.maximum(jnp.abs(power), SMALLEST)) * (1.0 / POWER))
    size = jnp.where(power < 0, -size, size) * (jnp.exp2(exponent) * (1.0 / TOP))
    return jnp.where(power == 0, 0.0, size)


def multiply_kernel(spots, out_count, w_ref, choice_ref, *refs):
    out_refs = refs[-out_count:]
    blocks = [refs[n][spot] for n, spot in spots]
    tiles = choice_ref.shape[0]
    each = tiles // out_count
    for n, out_ref in enumerate(out_refs):
        products = []
        for tile in range(n * each, (n + 1) * each):
            left = jnp.zeros_like(blocks[0])
            for spot, block in enumerate(blocks):
                left = jnp.where(choice_ref[tile, spot : spot + 1, :] > 0.5, block, left)
            products.append(
                lax.dot_general(
                    left,
                    w_ref[:, tile * TILE : (tile + 1) * TILE],
                    (((0,), (0,)), ((), ())),
                    preferred_element_type=jnp.float32,
                )
            )
        value = jnp.concatenate(products, axis=1)
        if out_ref.dtype == jnp.float32:
            out_ref[...] = value
        else:
            write_coded(out_ref, value)


def scale_kernel(
    a_width, i_hbm, j_hbm, tile_hbm, ei_hbm, ej_hbm, ev_ref, after_hbm, denom_ref, run_ref,
    zero_hbm, i_ref, j_ref, tile_ref, ei_ref, ej_ref, column_ref, zero_ref, sems, zero_sems,
):
    copies = start_all(
        (i_hbm, j_hbm, tile_hbm, ei_hbm, ej_hbm), (i_ref, j_ref, tile_ref, ei_ref, ej_ref), sems
    )
    rows_i, b_width = i_ref.shape[0], run_ref.shape[1]
    run = rows_i // tile_ref.shape[0]
    zero_ref[...] = jnp.zeros_like(zero_ref)
    count = zero_ref.shape[0]
    zero_copies = start_all(
        [zero_ref] * (rows_i // count),
        [zero_hbm.at[pl.ds(n * count, count)] for n in range(rows_i // count)],
        zero_sems,
    )
    a_start = lax.axis_index("blk") * a_width
    b_start = lax.axis_index("rep") * b_width
    a_tile = a_start // TILE
    column_ref[...] = jnp.broadcast_to(ev_ref[pl.ds(a_tile, 1), :], (TILE, TILE)).T
    a_energy = column_ref[pl.ds(pl.multiple_of(a_start % TILE, a_width), a_width), :]
    width = min(TILE, b_width)
    for copy in copies:
        copy.wait()
    for part in range(b_width // width):
        b_tile = b_start // TILE + part
        b_tile_row = ev_ref[pl.ds(b_tile, 1), :]
        b_row = b_tile_row[:, :width]
        for n in range(1, TILE // width):
            piece = b_tile_row[:, n * width : (n + 1) * width]
            b_row = jnp.where(b_start % TILE == n * width, piece, b_row)
        chosen = place_of(i_ref, run, j_ref[0] ^ tile_ref[a_tile] ^ tile_ref[b_tile])
        columns = slice(part * width, (part + 1) * width)
        run_ref[:, columns] = jnp.full((run_ref.shape[0], width), chosen.astype(jnp.float32))
        sum_ab = a_energy[:, :width] + b_row
        for m in range(run):
            denom_ref[m * a_width : (m + 1) * a_width, columns] = (
                sum_ab - ei_ref[chosen * run + m] - ej_ref[0]
            )
    for copy in zero_copies:
        copy.wait()


def place_kernel(run, denom_ref, run_ref, zero_hbm, *refs):
    parts_refs, out_hbm, block_ref, sems = refs[:-3], refs[-3], refs[-2], refs[-1]
    a_width, width = block_ref.shape[2:]
    total = parts_refs[-1][...]
    for parts_ref in parts_refs[:-1]:
        coded = parts_ref.dtype != jnp.float32
        total = total + (read_coded(parts_ref) if coded else parts_ref[...])
    scaled = total / denom_ref[...]
    copies = []
    for part in range(block_ref.shape[0]):
        columns = slice(part * width, (part + 1) * width)
        chosen = jnp.max(run_ref[:, columns]).astype(jnp.int32)
        for m in range(run):
            block_ref[part, m] = scaled[m * a_width : (m + 1) * a_width, columns]
        target = out_hbm.at[pl.ds(chosen * run, run), :, pl.ds(part * width, width)]
        copies.append(pltpu.make_async_copy(block_ref.at[part], target, sems.at[part]))
        copies[-1].start()
    for copy in copies:
        copy.wait()


def swap(block, axis, step):
    return lax.ppermute(block, axis, [(n, n ^ step) for n in range(lax.axis_size(axis))])


def shards(t_slab, w_cycle, k_irrep, i_irrep, j_irrep, tile_irrep, i_energy, j_energy, vir_energy):
    blk_count = lax.axis_size("blk")
    rep_count = lax.axis_size("rep")
    k_rows, c_width, rows_i, full_width = t_slab.shape
    rows_j = w_cycle.shape[1]
    assert k_rows == 1 and rows_j == 1
    tiles = tile_irrep.shape[0]
    run = rows_i // tiles
    a_width = full_width // blk_count
    b_width = full_width // rep_count
    deep = c_width * run
    wide = run * a_width
    by_partner = a_width == TILE and b_width % TILE == 0
    steps = list(reversed(range(tiles))) if by_partner else list(range(tiles))
    groups = [[step] for step in steps]
    if by_partner:
        far = [4, 6, 2] if tiles == 8 else range(tiles - 2, 0, -2)
        groups = [[step, step + 1] for step in far] + [[1], [0]]
        steps = [step for group in groups for step in group]

    t_rows = t_slab.reshape(c_width * rows_i, full_width)

    def pack(some_groups, last):
        pairs = sum(len(group) for group in some_groups) // 2
        plan = (rows_i, run, c_width, by_partner, b_width // TILE, some_groups, steps * last)
        arguments = [k_irrep, i_irrep, tile_irrep, t_rows]
        shapes = [
            jax.ShapeDtypeStruct((len(group), deep, TILE), t_slab.dtype) for group in some_groups
        ]
        scratch = [
            small(k_irrep),
            small(i_irrep),
            small(tile_irrep),
            pltpu.VMEM((pairs, t_rows.shape[0], 2 * TILE), t_slab.dtype),
            pltpu.SemaphoreType.DMA((3 + last,)),
            pltpu.SemaphoreType.DMA((pairs * HALVES,)),
        ]
        if not last:
            packed_here = [pltpu.VMEM(shape.shape, shape.dtype) for shape in shapes]
            scratch = packed_here + scratch + [pltpu.SemaphoreType.DMA((len(shapes),))]
        if last:
            arguments += [j_irrep, w_cycle.reshape(full_width, full_width)]
            shapes += [
                jax.ShapeDtypeStruct((TILE, full_width), w_cycle.dtype),
                jax.ShapeDtypeStruct((tiles, tiles, TILE), jnp.float32),
            ]
            scratch += [small(j_irrep), pltpu.SemaphoreType.DMA((tiles,))]
        return pl.pallas_call(
            lambda *refs: pack_kernel(plan, *refs),
            in_specs=[hbm()] * len(arguments),
            out_specs=[vmem() if last else hbm()] * len(shapes),
            out_shape=shapes,
            scratch_shapes=scratch,
            compiler_params=limit(52 if last else 62),
            name="pack_near" if last else "pack_far",
        )(*arguments)

    packed = list(pack(groups[:3], False)) if by_partner else []
    *near, chosen_w, choice = pack(groups[len(packed) :], True)
    packed += near

    if by_partner:
        *far, beside, own = packed
        left = [swap(pair, "blk", group[0]) for pair, group in zip(far, groups)]
        left += [swap(beside, "blk", 1), own]
        left[0], left[-2], choice = lax.optimization_barrier((left[0], left[-2], choice))
        handed = [swap(pair, "blk", 1) for pair in left[: len(far)]]
        spots = []
        for n in range(len(far)):
            spots += [(n, 0), (len(left) + n, 1)]
        spots += [(len(far), 0), (len(far) + 1, 0)]
        left += handed
        part_shapes = [
            jax.ShapeDtypeStruct((wide + SPARE, b_width), jnp.bfloat16)
        ] * (rep_count - 1) + [jax.ShapeDtypeStruct((wide, b_width), jnp.float32)]
    else:
        stacked = jnp.concatenate(packed).reshape(tiles, c_width, run, TILE // a_width, a_width)
        outgoing = stacked.transpose(0, 3, 1, 2, 4).reshape(blk_count, c_width, wide)
        arrived = lax.all_to_all(outgoing, "blk", split_axis=0, concat_axis=0, tiled=True)
        left = [arrived.reshape(tiles, TILE, wide)]
        spots = [(0, n) for n in range(tiles)]
        part_shapes = [jax.ShapeDtypeStruct((wide, full_width), jnp.float32)]

    partials = pl.pallas_call(
        lambda *refs: multiply_kernel(spots, len(part_shapes), *refs),
        in_specs=[vmem()] * (2 + len(left)),
        out_specs=[vmem()] * len(part_shapes),
        out_shape=part_shapes,
        compiler_params=limit(16),
        name="multiply",
    )(chosen_w, choice, *left)

    out_shape = jax.ShapeDtypeStruct((rows_i, a_width, b_width), jnp.float32)
    denom, run_row, zeros = pl.pallas_call(
        lambda *refs: scale_kernel(a_width, *refs),
        in_specs=[hbm()] * 5 + [vmem(), pl.BlockSpec(memory_space=pl.ANY)],
        out_specs=[vmem(), vmem(), hbm()],
        out_shape=[
            jax.ShapeDtypeStruct((wide, b_width), jnp.float32),
            jax.ShapeDtypeStruct((8, b_width), jnp.float32),
            out_shape,
        ],
        scratch_shapes=[
            small(i_irrep),
            small(j_irrep),
            small(tile_irrep),
            small(i_energy),
            small(j_energy),
            pltpu.VMEM((TILE, TILE), jnp.float32),
            pltpu.VMEM((run, a_width, b_width), jnp.float32),
            pltpu.SemaphoreType.DMA((5,)),
            pltpu.SemaphoreType.DMA((tiles,)),
        ],
        compiler_params=limit(8),
        name="scale",
    )(
        i_irrep, j_irrep, tile_irrep, i_energy, j_energy,
        vir_energy.reshape(full_width // TILE, TILE), partials[-1],
    )

    if by_partner:
        gathered = [
            swap(part, "rep", rep_count - 1 - n) for n, part in enumerate(partials[:-1])
        ] + [partials[-1]]
    else:
        outgoing = partials[0].reshape(wide, rep_count, b_width).transpose(1, 0, 2)
        arrived = lax.all_to_all(outgoing, "rep", split_axis=0, concat_axis=0, tiled=True)
        gathered = [arrived[n] for n in range(rep_count)]

    part_width = min(TILE, b_width)
    result = pl.pallas_call(
        lambda *refs: place_kernel(run, *refs),
        in_specs=[vmem(), vmem(), hbm()] + [vmem()] * rep_count,
        out_specs=hbm(),
        out_shape=out_shape,
        input_output_aliases={2: 0},
        scratch_shapes=[
            pltpu.VMEM((b_width // part_width, run, a_width, part_width), jnp.float32),
            pltpu.SemaphoreType.DMA((b_width // part_width,)),
        ],
        compiler_params=limit(16),
        name="place",
    )(denom, run_row, zeros, *gathered)
    return result.reshape(rows_j, rows_i, a_width, b_width)


def solution(mesh):
    in_specs = (
        P("rep", "blk", None, None),
        P("rep", None, None, None),
        P("rep"),
        P(),
        P(),
        P(),
        P(),
        P(),
        P(),
    )
    out_specs = P(None, None, "blk", "rep")
    return jax.shard_map(shards, mesh=mesh, in_specs=in_specs, out_specs=out_specs, check_vma=False)
```

time: 137 us -> 24.7 us (0.18)
  waiting for transfers between devices: 97.9 us -> 5.75 us
  between operations: 15.4 us -> 2.08 us
  Pallas kernels: 0 us -> 6.83 us
  other arithmetic: 6.38 us -> 0 us
  matrix products: 6.32 us -> 0 us
  local copies, waits for them, and re-layouts: 3.85 us -> 0.02 us
  starting transfers between devices: 6.36 us -> 9.82 us
    reduce_scatter x1 -> x0, waiting for transfers between devices: 49.5 us -> none  [shards(): summed = lax.psum_scatter(arranged, 'rep', scatter_dimension=1, tiled=True)]
    all_to_all x1 -> x0, waiting for transfers between devices: 48.4 us -> none  [shards(): lax.all_to_all(outgoing, 'blk', split_axis=0, concat_axis=0, tiled=True)]
    ppermute x0 -> x10, starting transfers between devices: none -> 9.82 us  [swap(): lax.ppermute(block, axis, [(n, n ^ step) for n in range(lax.axis_size(axi...]
    pallas_call x0 -> x5, Pallas kernels: none -> 6.83 us  [the longest x2 4.38 us: pack(): pl.pallas_call(lambda *refs: pack_kernel(plan, *refs), in_specs=[hbm()] *...]
    all_to_all x1 -> x0, starting transfers between devices: 6.33 us -> none  [shards(): lax.all_to_all(outgoing, 'blk', split_axis=0, concat_axis=0, tiled=True)]
    dot_general x1 -> x0, matrix products: 6.32 us -> none  [shards(): lax.dot_general(left_side, right_side, (((0, 1), (0, 1)), ((), ())), pref...]
    ppermute x0 -> x10, waiting for transfers between devices: none -> 5.75 us  [swap(): lax.ppermute(block, axis, [(n, n ^ step) for n in range(lax.axis_size(axi...]
    div x1 -> x0, other arithmetic: 2.41 us -> none  [shards(): return result / denom]
  transfers between devices with their start and end apart: 2 -> 10, of which waited for: 2 -> 8; matrix products, arithmetic and copies ran while one was open for 1% -> 0% of each run, Pallas kernels for 0% -> 11%
where the time goes in v1:
time: 24.7 us; the launch traced here: 24.5 us
  starting transfers between devices  9.82 us (40%)
  Pallas kernels  6.83 us (28%)
  waiting for transfers between devices  5.75 us (23%)
  between operations  2.08 us (8%)
    ppermute x10, starting transfers between devices, swap(): lax.ppermute(block, axis, [(n, n ^ step) for n in range(lax.axis_size(axi...  9.82 us
    ppermute x10, waiting for transfers between devices, swap(): lax.ppermute(block, axis, [(n, n ^ step) for n in range(lax.axis_size(axi...  5.75 us
    pallas_call x2, Pallas kernels, pack(): pl.pallas_call(lambda *refs: pack_kernel(plan, *refs), in_specs=[hbm()] *...  4.38 us
    pallas_call x1, Pallas kernels, shards(): pl.pallas_call(lambda *refs: scale_kernel(a_width, *refs), in_specs=[hbm(...  1.09 us
    pallas_call x1, Pallas kernels, shards(): pl.pallas_call(lambda *refs: place_kernel(run, *refs), in_specs=[vmem(),...  0.86 us
    pallas_call x1, Pallas kernels, shards(): pl.pallas_call(lambda *refs: multiply_kernel(spots, len(part_shapes), *re...  0.51 us
  transfers between devices with their start and end apart: 10, of which 8 were waited for; matrix products, arithmetic and copies ran while one was open for 0% of the time, Pallas kernels for 11%

profile of v1, /device:TPU:0, one launch (start us, length us, event | category | flops | bytes accessed | tf_op | source)
XLA Modules:
  0.0 24.5 jit_solution(4209951949633179349)
XLA Ops:
  0.7 2.8 %pack_far.1 = (bf16[2,128,128]{2,1,0:T(8,128)(2,1)}, bf16[2,128,128]{2,1,0:T(8,128)(2,1)}, bf16[2,128,128]{2,1,0:T(8,128)(2,1)}) custom-call(s32[1]{0:T(128)S(6)} %copy.12.refs_0_, s32[8]{0:T(128)} %refs_0_.3, s32[8]{0:T(128)} %refs_2_.5, bf16[1024,1024]{1,0:T(8,128)(2,1)} %bitcast.5), custom_call_target="tpu_custom_call" | custom-call | tf_op jit(solution)/shard_map/pack_far/pallas_call | solution.py:306
  3.4 4.1 %collective-permute-start = (bf16[2,128,128]{2,1,0:T(8,128)(2,1)}, bf16[2,128,128]{2,1,0:T(8,128)(2,1)S(1)}, u32[]{:S(2)}, u32[]{:S(2)}) collective-permute-start(bf16[2,128,128]{2,1,0:T(8,128)(2,1)} %get-tuple-element.23), channel_id=1, source_target_pairs={{0,16},{4,20},{8,24},{12,28},{16,0},{20,4},{24,8},{28,12},{1,17},{... | collective-permute-start | bytes 196616 | tf_op jit(solution)/shard_map/ppermute | solution.py:256
  7.5 1.3 %collective-permute-start.2 = (bf16[2,128,128]{2,1,0:T(8,128)(2,1)}, bf16[2,128,128]{2,1,0:T(8,128)(2,1)S(1)}, u32[]{:S(2)}, u32[]{:S(2)}) collective-permute-start(bf16[2,128,128]{2,1,0:T(8,128)(2,1)} %get-tuple-element.28), channel_id=1, source_target_pairs={{0,24},{4,28},{8,16},{12,20},{16,8},{20,12},{24,0},{28,4},{1,25},{... | collective-permute-start | bytes 196616 | tf_op jit(solution)/shard_map/ppermute | solution.py:256
  8.9 0.2 collective-permute-start.3
  9.8 0.0 copy-start.2
  9.8 1.6 %pack_near.1 = (bf16[1,128,128]{2,1,0:T(8,128)(2,1)S(1)}, bf16[1,128,128]{2,1,0:T(8,128)(2,1)S(1)}, bf16[128,1024]{1,0:T(8,128)(2,1)S(1)}, f32[8,8,128]{2,1,0:T(8,128)S(1)}) custom-call(s32[1]{0:T(128)S(6)} %copy.12.refs_0_, s32[8]{0:T(128)S(1)} %copy-done, s32[8]{0:T(128)S(1)} %copy-done.1, bf16[1024,1024]{1,0:T(8,128)(2,1)} %bitcast.6, ...), custom_call_target="tpu_custom_call" | custom-call | tf_op jit(solution)/shard_map/pack_near/pallas_call | solution.py:306
  11.5 0.1 collective-permute-start.1
  11.5 1.2 %collective-permute-done.1.refs_5_ = bf16[1,128,128]{2,1,0:T(8,128)(2,1)S(1)} collective-permute-done((bf16[1,128,128]{2,1,0:T(8,128)(2,1)S(1)}, bf16[1,128,128]{2,1,0:T(8,128)(2,1)S(1)}, u32[]{:S(2)}, u32[]{:S(2)}) %collective-permute-start.1) | collective-permute-done | bytes 32800 | tf_op jit(solution)/shard_map/ppermute | solution.py:256
  12.7 1.2 %collective-permute-done.2.refs_3_ = bf16[2,128,128]{2,1,0:T(8,128)(2,1)S(1)} collective-permute-done((bf16[2,128,128]{2,1,0:T(8,128)(2,1)}, bf16[2,128,128]{2,1,0:T(8,128)(2,1)S(1)}, u32[]{:S(2)}, u32[]{:S(2)}) %collective-permute-start.2) | collective-permute-done | bytes 65568 | tf_op jit(solution)/shard_map/ppermute | solution.py:256
  14.0 0.1 collective-permute-done.3.refs_4_
  14.1 0.4 %collective-permute-start.6 = (bf16[2,128,128]{2,1,0:T(8,128)(2,1)S(1)}, bf16[2,128,128]{2,1,0:T(8,128)(2,1)S(1)}, u32[]{:S(2)}, u32[]{:S(2)}) collective-permute-start(bf16[2,128,128]{2,1,0:T(8,128)(2,1)S(1)} %collective-permute-done.3.refs_4_), channel_id=1, source_target_pairs={{0,4},{4,0},{8,12},{12,8},{16,20},{20,16},{24,28},{28,24},{1,5},{5... | collective-permute-start | bytes 196616 | tf_op jit(solution)/shard_map/ppermute | solution.py:256
  14.5 0.1 collective-permute-start.4
  14.6 0.7 %collective-permute-done.5.refs_8_ = bf16[2,128,128]{2,1,0:T(8,128)(2,1)S(1)} collective-permute-done((bf16[2,128,128]{2,1,0:T(8,128)(2,1)S(1)}, bf16[2,128,128]{2,1,0:T(8,128)(2,1)S(1)}, u32[]{:S(2)}, u32[]{:S(2)}) %collective-permute-start.5) | collective-permute-done | bytes 65568 | tf_op jit(solution)/shard_map/ppermute | solution.py:256
  15.2 0.2 collective-permute-done.6.refs_9_
  15.4 0.4 %collective-permute-done.4.refs_7_ = bf16[2,128,128]{2,1,0:T(8,128)(2,1)S(1)} collective-permute-done((bf16[2,128,128]{2,1,0:T(8,128)(2,1)S(1)}, bf16[2,128,128]{2,1,0:T(8,128)(2,1)S(1)}, u32[]{:S(2)}, u32[]{:S(2)}) %collective-permute-start.4) | collective-permute-done | bytes 65568 | tf_op jit(solution)/shard_map/ppermute | solution.py:256
  15.7 0.5 %multiply.1 = (bf16[144,256]{1,0:T(8,128)(2,1)S(1)}, bf16[144,256]{1,0:T(8,128)(2,1)S(1)}, bf16[144,256]{1,0:T(8,128)(2,1)S(1)}, f32[128,256]{1,0:T(8,128)S(1)}) custom-call(bf16[128,1024]{1,0:T(8,128)(2,1)S(1)} %get-tuple-element.22.refs_0_, f32[8,8,128]{2,1,0:T(8,128)S(1)} %get-tuple-element.26.refs_1_, ...), custom_call_target="tpu_custom_call" | custom-call | tf_op jit(solution)/shard_map/multiply/pallas_call | solution.py:342
  16.3 2.5 %collective-permute-start.7 = (bf16[144,256]{1,0:T(8,128)(2,1)S(1)}, bf16[144,256]{1,0:T(8,128)(2,1)S(1)}, u32[]{:S(2)}, u32[]{:S(2)}) collective-permute-start(bf16[144,256]{1,0:T(8,128)(2,1)S(1)} %get-tuple-element.36), channel_id=1, source_target_pairs={{0,3},{1,2},{2,1},{3,0},{4,7},{5,6},{6,5},{7,4},{8,11},{9,10},{10,... | collective-permute-start | bytes 221192 | tf_op jit(solution)/shard_map/ppermute | solution.py:256
  18.8 0.5 %collective-permute-start.8 = (bf16[144,256]{1,0:T(8,128)(2,1)S(1)}, bf16[144,256]{1,0:T(8,128)(2,1)S(1)}, u32[]{:S(2)}, u32[]{:S(2)}) collective-permute-start(bf16[144,256]{1,0:T(8,128)(2,1)S(1)} %get-tuple-element.37), channel_id=1, source_target_pairs={{0,2},{1,3},{2,0},{3,1},{4,6},{5,7},{6,4},{7,5},{8,10},{9,11},{10,... | collective-permute-start | bytes 221192 | tf_op jit(solution)/shard_map/ppermute | solution.py:256
  19.3 0.5 %collective-permute-start.9 = (bf16[144,256]{1,0:T(8,128)(2,1)S(1)}, bf16[144,256]{1,0:T(8,128)(2,1)S(1)}, u32[]{:S(2)}, u32[]{:S(2)}) collective-permute-start(bf16[144,256]{1,0:T(8,128)(2,1)S(1)} %get-tuple-element.38), channel_id=1, source_target_pairs={{0,1},{1,0},{2,3},{3,2},{4,5},{5,4},{6,7},{7,6},{8,9},{9,8},{10,11... | collective-permute-start | bytes 221192 | tf_op jit(solution)/shard_map/ppermute | solution.py:256
  20.5 1.1 %scale.1 = (f32[128,256]{1,0:T(8,128)S(1)}, f32[8,256]{1,0:T(8,128)S(1)}, f32[8,128,256]{2,1,0:T(8,128)}) custom-call(s32[8]{0:T(128)S(1)} %copy-done, s32[1]{0:T(128)S(6)} %copy.13.refs_4_.refs_1_, s32[8]{0:T(128)S(1)} %copy-done.1, f32[8]{0:T(128)S(1)} %copy-done.3, f32[1]{0:T(128)S(6)} %copy.14.refs_4_, f32[8,128]{1,0:T(8,128)S(1)} %bitcast.4, ...), custom_call_target="tpu_custom_call" | custom-call | tf_op jit(solution)/shard_map/scale/pallas_call | solution.py:352
  21.6 0.0 collective-permute-done.7.refs_3_
  21.6 1.5 %collective-permute-done.8.refs_4_ = bf16[144,256]{1,0:T(8,128)(2,1)S(1)} collective-permute-done((bf16[144,256]{1,0:T(8,128)(2,1)S(1)}, bf16[144,256]{1,0:T(8,128)(2,1)S(1)}, u32[]{:S(2)}, u32[]{:S(2)}) %collective-permute-start.8) | collective-permute-done | bytes 73760 | tf_op jit(solution)/shard_map/ppermute | solution.py:256
  23.2 0.5 %collective-permute-done.9.refs_5_ = bf16[144,256]{1,0:T(8,128)(2,1)S(1)} collective-permute-done((bf16[144,256]{1,0:T(8,128)(2,1)S(1)}, bf16[144,256]{1,0:T(8,128)(2,1)S(1)}, u32[]{:S(2)}, u32[]{:S(2)}) %collective-permute-start.9) | collective-permute-done | bytes 73760 | tf_op jit(solution)/shard_map/ppermute | solution.py:256
  23.6 0.9 %place.1 = f32[8,128,256]{2,1,0:T(8,128)} custom-call(f32[128,256]{1,0:T(8,128)S(1)} %get-tuple-element.33.refs_0_, f32[8,256]{1,0:T(8,128)S(1)} %get-tuple-element.34.refs_1_, f32[8,128,256]{2,1,0:T(8,128)} %get-tuple-element.35.refs_2_, bf16[144,256]{1,0:T(8,128)(2,1)S(1)} %collective-permute-done.7.refs_3_, ...), custom_call_target="tpu_custom_call", output_to_operand_aliasing={{}: (2, {})} | custom-call | tf_op jit(solution)/shard_map/place/pallas_call | solution.py:389
  (9 shorter events, 0.0 us)
Async XLA Ops:
  0.0 9.8 %copy-start.1 = (s32[8]{0:T(128)S(1)}, s32[8]{0:T(128)}, u32[]{:S(2)}) copy-start(s32[8]{0:T(128)} %refs_2_.5) | copy-start | bytes 100
  0.0 9.8 %copy-start = (s32[8]{0:T(128)S(1)}, s32[8]{0:T(128)}, u32[]{:S(2)}) copy-start(s32[8]{0:T(128)} %refs_0_.3) | copy-start | bytes 100
  3.4 9.3 %collective-permute-start = (bf16[2,128,128]{2,1,0:T(8,128)(2,1)}, bf16[2,128,128]{2,1,0:T(8,128)(2,1)S(1)}, u32[]{:S(2)}, u32[]{:S(2)}) collective-permute-start(bf16[2,128,128]{2,1,0:T(8,128)(2,1)} %get-tuple-element.23), channel_id=1, source_target_pairs={{0,16},{4,20},{8,24},{12,28},{16,0},{20,4},{24,8},{28,12},{1,17},{... | collective-permute-start | bytes 196616 | tf_op jit(solution)/shard_map/ppermute | solution.py:256
  7.5 6.4 %collective-permute-start.2 = (bf16[2,128,128]{2,1,0:T(8,128)(2,1)}, bf16[2,128,128]{2,1,0:T(8,128)(2,1)S(1)}, u32[]{:S(2)}, u32[]{:S(2)}) collective-permute-start(bf16[2,128,128]{2,1,0:T(8,128)(2,1)} %get-tuple-element.28), channel_id=1, source_target_pairs={{0,24},{4,28},{8,16},{12,20},{16,8},{20,12},{24,0},{28,4},{1,25},{... | collective-permute-start | bytes 196616 | tf_op jit(solution)/shard_map/ppermute | solution.py:256
  8.9 5.2 %collective-permute-start.3 = (bf16[2,128,128]{2,1,0:T(8,128)(2,1)}, bf16[2,128,128]{2,1,0:T(8,128)(2,1)S(1)}, u32[]{:S(2)}, u32[]{:S(2)}) collective-permute-start(bf16[2,128,128]{2,1,0:T(8,128)(2,1)} %get-tuple-element.29), channel_id=1, source_target_pairs={{0,8},{4,12},{8,0},{12,4},{16,24},{20,28},{24,16},{28,20},{1,9},{5... | collective-permute-start | bytes 196616 | tf_op jit(solution)/shard_map/ppermute | solution.py:256
  9.8 10.7 %copy-start.2 = (f32[1024]{0:T(1024)S(1)}, f32[1024]{0:T(1024)}, u32[]{:S(2)}) copy-start(f32[1024]{0:T(1024)} %param.17) | copy-start | bytes 12292
  9.8 10.7 %copy-start.3 = (f32[8]{0:T(128)S(1)}, f32[8]{0:T(128)}, u32[]{:S(2)}) copy-start(f32[8]{0:T(128)} %refs_3_.1) | copy-start | bytes 100
  11.5 1.3 %collective-permute-start.1 = (bf16[1,128,128]{2,1,0:T(8,128)(2,1)S(1)}, bf16[1,128,128]{2,1,0:T(8,128)(2,1)S(1)}, u32[]{:S(2)}, u32[]{:S(2)}) collective-permute-start(bf16[1,128,128]{2,1,0:T(8,128)(2,1)S(1)} %get-tuple-element.24), channel_id=1, source_target_pairs={{0,4},{4,0},{8,12},{12,8},{16,20},{20,16},{24,28},{28,24},{1,5},{5... | collective-permute-start | bytes 98312 | tf_op jit(solution)/shard_map/ppermute | solution.py:256
  14.0 1.3 %collective-permute-start.5 = (bf16[2,128,128]{2,1,0:T(8,128)(2,1)S(1)}, bf16[2,128,128]{2,1,0:T(8,128)(2,1)S(1)}, u32[]{:S(2)}, u32[]{:S(2)}) collective-permute-start(bf16[2,128,128]{2,1,0:T(8,128)(2,1)S(1)} %collective-permute-done.2.refs_3_), channel_id=1, source_target_pairs={{0,4},{4,0},{8,12},{12,8},{16,20},{20,16},{24,28},{28,24},{1,5},{5... | collective-permute-start | bytes 196616 | tf_op jit(solution)/shard_map/ppermute | solution.py:256
  14.1 1.3 %collective-permute-start.6 = (bf16[2,128,128]{2,1,0:T(8,128)(2,1)S(1)}, bf16[2,128,128]{2,1,0:T(8,128)(2,1)S(1)}, u32[]{:S(2)}, u32[]{:S(2)}) collective-permute-start(bf16[2,128,128]{2,1,0:T(8,128)(2,1)S(1)} %collective-permute-done.3.refs_4_), channel_id=1, source_target_pairs={{0,4},{4,0},{8,12},{12,8},{16,20},{20,16},{24,28},{28,24},{1,5},{5... | collective-permute-start | bytes 196616 | tf_op jit(solution)/shard_map/ppermute | solution.py:256
  14.5 1.3 %collective-permute-start.4 = (bf16[2,128,128]{2,1,0:T(8,128)(2,1)S(1)}, bf16[2,128,128]{2,1,0:T(8,128)(2,1)S(1)}, u32[]{:S(2)}, u32[]{:S(2)}) collective-permute-start(bf16[2,128,128]{2,1,0:T(8,128)(2,1)S(1)} %collective-permute-done.refs_2_), channel_id=1, source_target_pairs={{0,4},{4,0},{8,12},{12,8},{16,20},{20,16},{24,28},{28,24},{1,5},{5... | collective-permute-start | bytes 196616 | tf_op jit(solution)/shard_map/ppermute | solution.py:256
  16.3 5.4 %collective-permute-start.7 = (bf16[144,256]{1,0:T(8,128)(2,1)S(1)}, bf16[144,256]{1,0:T(8,128)(2,1)S(1)}, u32[]{:S(2)}, u32[]{:S(2)}) collective-permute-start(bf16[144,256]{1,0:T(8,128)(2,1)S(1)} %get-tuple-element.36), channel_id=1, source_target_pairs={{0,3},{1,2},{2,1},{3,0},{4,7},{5,6},{6,5},{7,4},{8,11},{9,10},{10,... | collective-permute-start | bytes 221192 | tf_op jit(solution)/shard_map/ppermute | solution.py:256
  18.8 4.4 %collective-permute-start.8 = (bf16[144,256]{1,0:T(8,128)(2,1)S(1)}, bf16[144,256]{1,0:T(8,128)(2,1)S(1)}, u32[]{:S(2)}, u32[]{:S(2)}) collective-permute-start(bf16[144,256]{1,0:T(8,128)(2,1)S(1)} %get-tuple-element.37), channel_id=1, source_target_pairs={{0,2},{1,3},{2,0},{3,1},{4,6},{5,7},{6,4},{7,5},{8,10},{9,11},{10,... | collective-permute-start | bytes 221192 | tf_op jit(solution)/shard_map/ppermute | solution.py:256
  19.3 4.4 %collective-permute-start.9 = (bf16[144,256]{1,0:T(8,128)(2,1)S(1)}, bf16[144,256]{1,0:T(8,128)(2,1)S(1)}, u32[]{:S(2)}, u32[]{:S(2)}) collective-permute-start(bf16[144,256]{1,0:T(8,128)(2,1)S(1)} %get-tuple-element.38), channel_id=1, source_target_pairs={{0,1},{1,0},{2,3},{3,2},{4,5},{5,4},{6,7},{7,6},{8,9},{9,8},{10,11... | collective-permute-start | bytes 221192 | tf_op jit(solution)/shard_map/ppermute | solution.py:256

commit v2 on v1

--- a/solution.py
+++ b/solution.py
@@ -7,12 +7,11 @@
 
 TILE = 128
 CHUNK = 256
-HALVES = 2
 POWER = 17
 TOP = 128.0
 LEAST = 2.0**-100
 SMALLEST = 2.0**-126
-SPARE = 16
+SPARE = 8
 
 
 def vmem():
@@ -53,8 +52,6 @@
         *refs, j_ref, w_sems = refs
     else:
         k_hbm, i_hbm, tile_hbm, t_hbm, *refs = refs
-        outs_hbm, refs = refs[: len(groups)], refs[len(groups) :]
-        *refs, out_sems = refs
     *refs, k_ref, i_ref, tile_ref, t_ref, small_sems, t_sems = refs
     out_refs = refs[: len(groups)]
     runs = rows_i // run
@@ -75,11 +72,9 @@
         pl.ds(pl.multiple_of(((me ^ step) | 1) * TILE - TILE, 2 * TILE), 2 * TILE)
         for step in pairs
     ]
-    depth = t_ref.shape[1] // HALVES
-    spans = [(n, pl.ds(half * depth, depth)) for n in range(len(pairs)) for half in range(HALVES)]
     t_copies = start_all(
-        [t_hbm.at[span, columns[n]] for n, span in spans],
-        [t_ref.at[n, span] for n, span in spans],
+        [t_hbm.at[:, span] for span in columns],
+        [t_ref.at[n] for n in range(len(pairs))],
         t_sems,
     )
     row = lax.broadcasted_iota(jnp.int32, (rows, CHUNK), 0)
@@ -121,11 +116,9 @@
             rows_of_pair.append(jnp.where(of_run == chosen, 1.0, 0.0).astype(jnp.bfloat16))
         picks.append(jnp.concatenate(rows_of_pair, axis=0))
     swapped = (me & 1) == 1
-    out_copies = []
     for n, step in enumerate(pairs):
+        t_copies[n].wait()
         for chunk in range(t_ref.shape[1] // CHUNK):
-            if chunk * CHUNK % depth == 0:
-                t_copies[n * HALVES + chunk * CHUNK // depth].wait()
             block = t_ref[n, chunk * CHUNK : (chunk + 1) * CHUNK, :]
             kept = jnp.dot(picks[n], block, preferred_element_type=jnp.float32)
             low, high = kept[:, :TILE], kept[:, TILE:]
@@ -134,10 +127,7 @@
                 out_ref, spot = places[own]
                 value = jnp.where(swapped, other[half], here[half])
                 out_ref[spot, chunk * rows : (chunk + 1) * rows, :] = value.astype(out_ref.dtype)
-        if not steps:
-            out_copies.append(pltpu.make_async_copy(out_ref, outs_hbm[n], out_sems.at[n]))
-            out_copies[-1].start()
-    for copy in w_copies + out_copies:
+    for copy in w_copies:
         copy.wait()
 
 
@@ -291,11 +281,8 @@
             small(tile_irrep),
             pltpu.VMEM((pairs, t_rows.shape[0], 2 * TILE), t_slab.dtype),
             pltpu.SemaphoreType.DMA((3 + last,)),
-            pltpu.SemaphoreType.DMA((pairs * HALVES,)),
+            pltpu.SemaphoreType.DMA((pairs,)),
         ]
-        if not last:
-            packed_here = [pltpu.VMEM(shape.shape, shape.dtype) for shape in shapes]
-            scratch = packed_here + scratch + [pltpu.SemaphoreType.DMA((len(shapes),))]
         if last:
             arguments += [j_irrep, w_cycle.reshape(full_width, full_width)]
             shapes += [
@@ -306,7 +293,7 @@
         return pl.pallas_call(
             lambda *refs: pack_kernel(plan, *refs),
             in_specs=[hbm()] * len(arguments),
-            out_specs=[vmem() if last else hbm()] * len(shapes),
+            out_specs=[vmem()] * len(shapes),
             out_shape=shapes,
             scratch_shapes=scratch,
             compiler_params=limit(52 if last else 62),

time: 24.7 us -> 24.3 us (0.984)
  Pallas kernels: 6.83 us -> 6.44 us
    pallas_call x2, Pallas kernels: 4.38 us -> 3.98 us  [pack(): pl.pallas_call(lambda *refs: pack_kernel(plan, *refs), in_specs=[hbm()] *...]
where the time goes in v2:
time: 24.3 us; the launch traced here: 24.1 us
  starting transfers between devices  9.82 us (40%)
  Pallas kernels  6.44 us (27%)
  waiting for transfers between devices  5.71 us (23%)
  between operations  2.09 us (9%)
    ppermute x10, starting transfers between devices, swap(): lax.ppermute(block, axis, [(n, n ^ step) for n in range(lax.axis_size(axi...  9.82 us
    ppermute x10, waiting for transfers between devices, swap(): lax.ppermute(block, axis, [(n, n ^ step) for n in range(lax.axis_size(axi...  5.71 us
    pallas_call x2, Pallas kernels, pack(): pl.pallas_call(lambda *refs: pack_kernel(plan, *refs), in_specs=[hbm()] *...  3.98 us
    pallas_call x1, Pallas kernels, shards(): pl.pallas_call(lambda *refs: scale_kernel(a_width, *refs), in_specs=[hbm(...  1.09 us
    pallas_call x1, Pallas kernels, shards(): pl.pallas_call(lambda *refs: place_kernel(run, *refs), in_specs=[vmem(),...  0.86 us
    pallas_call x1, Pallas kernels, shards(): pl.pallas_call(lambda *refs: multiply_kernel(spots, len(part_shapes), *re...  0.51 us
  transfers between devices with their start and end apart: 10, of which 8 were waited for; matrix products, arithmetic and copies ran while one was open for 0% of the time, Pallas kernels for 11%

profile of v2, /device:TPU:0, one launch (start us, length us, event | category | flops | bytes accessed | tf_op | source)
XLA Modules:
  0.0 24.1 jit_solution(1200963593865381145)
XLA Ops:
  0.7 2.4 %pack_far.1 = (bf16[2,128,128]{2,1,0:T(8,128)(2,1)}, bf16[2,128,128]{2,1,0:T(8,128)(2,1)}, bf16[2,128,128]{2,1,0:T(8,128)(2,1)}) custom-call(s32[1]{0:T(128)S(6)} %copy.12.refs_0_, s32[8]{0:T(128)} %refs_0_.3, s32[8]{0:T(128)} %refs_2_.5, bf16[1024,1024]{1,0:T(8,128)(2,1)} %bitcast.5), custom_call_target="tpu_custom_call" | custom-call | tf_op jit(solution)/shard_map/pack_far/pallas_call | solution.py:293
  3.1 4.1 %collective-permute-start = (bf16[2,128,128]{2,1,0:T(8,128)(2,1)}, bf16[2,128,128]{2,1,0:T(8,128)(2,1)S(1)}, u32[]{:S(2)}, u32[]{:S(2)}) collective-permute-start(bf16[2,128,128]{2,1,0:T(8,128)(2,1)} %get-tuple-element.23), channel_id=1, source_target_pairs={{0,16},{4,20},{8,24},{12,28},{16,0},{20,4},{24,8},{28,12},{1,17},{... | collective-permute-start | bytes 196616 | tf_op jit(solution)/shard_map/ppermute | solution.py:246
  7.2 1.3 %collective-permute-start.2 = (bf16[2,128,128]{2,1,0:T(8,128)(2,1)}, bf16[2,128,128]{2,1,0:T(8,128)(2,1)S(1)}, u32[]{:S(2)}, u32[]{:S(2)}) collective-permute-start(bf16[2,128,128]{2,1,0:T(8,128)(2,1)} %get-tuple-element.28), channel_id=1, source_target_pairs={{0,24},{4,28},{8,16},{12,20},{16,8},{20,12},{24,0},{28,4},{1,25},{... | collective-permute-start | bytes 196616 | tf_op jit(solution)/shard_map/ppermute | solution.py:246
  8.5 0.2 collective-permute-start.3
  9.4 0.0 copy-start.2
  9.4 0.0 copy-start.3
  9.4 1.6 %pack_near.1 = (bf16[1,128,128]{2,1,0:T(8,128)(2,1)S(1)}, bf16[1,128,128]{2,1,0:T(8,128)(2,1)S(1)}, bf16[128,1024]{1,0:T(8,128)(2,1)S(1)}, f32[8,8,128]{2,1,0:T(8,128)S(1)}) custom-call(s32[1]{0:T(128)S(6)} %copy.12.refs_0_, s32[8]{0:T(128)S(1)} %copy-done, s32[8]{0:T(128)S(1)} %copy-done.1, bf16[1024,1024]{1,0:T(8,128)(2,1)} %bitcast.6, ...), custom_call_target="tpu_custom_call" | custom-call | tf_op jit(solution)/shard_map/pack_near/pallas_call | solution.py:293
  11.1 0.1 collective-permute-start.1
  11.1 1.2 %collective-permute-done.1.refs_5_ = bf16[1,128,128]{2,1,0:T(8,128)(2,1)S(1)} collective-permute-done((bf16[1,128,128]{2,1,0:T(8,128)(2,1)S(1)}, bf16[1,128,128]{2,1,0:T(8,128)(2,1)S(1)}, u32[]{:S(2)}, u32[]{:S(2)}) %collective-permute-start.1) | collective-permute-done | bytes 32800 | tf_op jit(solution)/shard_map/ppermute | solution.py:246
  12.3 1.3 %collective-permute-done.2.refs_3_ = bf16[2,128,128]{2,1,0:T(8,128)(2,1)S(1)} collective-permute-done((bf16[2,128,128]{2,1,0:T(8,128)(2,1)}, bf16[2,128,128]{2,1,0:T(8,128)(2,1)S(1)}, u32[]{:S(2)}, u32[]{:S(2)}) %collective-permute-start.2) | collective-permute-done | bytes 65568 | tf_op jit(solution)/shard_map/ppermute | solution.py:246
  13.6 0.1 collective-permute-done.3.refs_4_
  13.7 0.4 %collective-permute-start.6 = (bf16[2,128,128]{2,1,0:T(8,128)(2,1)S(1)}, bf16[2,128,128]{2,1,0:T(8,128)(2,1)S(1)}, u32[]{:S(2)}, u32[]{:S(2)}) collective-permute-start(bf16[2,128,128]{2,1,0:T(8,128)(2,1)S(1)} %collective-permute-done.3.refs_4_), channel_id=1, source_target_pairs={{0,4},{4,0},{8,12},{12,8},{16,20},{20,16},{24,28},{28,24},{1,5},{5... | collective-permute-start | bytes 196616 | tf_op jit(solution)/shard_map/ppermute | solution.py:246
  14.1 0.1 collective-permute-start.4
  14.2 0.7 %collective-permute-done.5.refs_8_ = bf16[2,128,128]{2,1,0:T(8,128)(2,1)S(1)} collective-permute-done((bf16[2,128,128]{2,1,0:T(8,128)(2,1)S(1)}, bf16[2,128,128]{2,1,0:T(8,128)(2,1)S(1)}, u32[]{:S(2)}, u32[]{:S(2)}) %collective-permute-start.5) | collective-permute-done | bytes 65568 | tf_op jit(solution)/shard_map/ppermute | solution.py:246
  14.8 0.2 collective-permute-done.6.refs_9_
  15.0 0.4 %collective-permute-done.4.refs_7_ = bf16[2,128,128]{2,1,0:T(8,128)(2,1)S(1)} collective-permute-done((bf16[2,128,128]{2,1,0:T(8,128)(2,1)S(1)}, bf16[2,128,128]{2,1,0:T(8,128)(2,1)S(1)}, u32[]{:S(2)}, u32[]{:S(2)}) %collective-permute-start.4) | collective-permute-done | bytes 65568 | tf_op jit(solution)/shard_map/ppermute | solution.py:246
  15.4 0.5 %multiply.1 = (bf16[136,256]{1,0:T(8,128)(2,1)S(1)}, bf16[136,256]{1,0:T(8,128)(2,1)S(1)}, bf16[136,256]{1,0:T(8,128)(2,1)S(1)}, f32[128,256]{1,0:T(8,128)S(1)}) custom-call(bf16[128,1024]{1,0:T(8,128)(2,1)S(1)} %get-tuple-element.22.refs_0_, f32[8,8,128]{2,1,0:T(8,128)S(1)} %get-tuple-element.26.refs_1_, ...), custom_call_target="tpu_custom_call" | custom-call | tf_op jit(solution)/shard_map/multiply/pallas_call | solution.py:329
  15.9 2.5 %collective-permute-start.7 = (bf16[136,256]{1,0:T(8,128)(2,1)S(1)}, bf16[136,256]{1,0:T(8,128)(2,1)S(1)}, u32[]{:S(2)}, u32[]{:S(2)}) collective-permute-start(bf16[136,256]{1,0:T(8,128)(2,1)S(1)} %get-tuple-element.36), channel_id=1, source_target_pairs={{0,3},{1,2},{2,1},{3,0},{4,7},{5,6},{6,5},{7,4},{8,11},{9,10},{10,... | collective-permute-start | bytes 208904 | tf_op jit(solution)/shard_map/ppermute | solution.py:246
  18.4 0.5 %collective-permute-start.8 = (bf16[136,256]{1,0:T(8,128)(2,1)S(1)}, bf16[136,256]{1,0:T(8,128)(2,1)S(1)}, u32[]{:S(2)}, u32[]{:S(2)}) collective-permute-start(bf16[136,256]{1,0:T(8,128)(2,1)S(1)} %get-tuple-element.37), channel_id=1, source_target_pairs={{0,2},{1,3},{2,0},{3,1},{4,6},{5,7},{6,4},{7,5},{8,10},{9,11},{10,... | collective-permute-start | bytes 208904 | tf_op jit(solution)/shard_map/ppermute | solution.py:246
  18.9 0.5 %collective-permute-start.9 = (bf16[136,256]{1,0:T(8,128)(2,1)S(1)}, bf16[136,256]{1,0:T(8,128)(2,1)S(1)}, u32[]{:S(2)}, u32[]{:S(2)}) collective-permute-start(bf16[136,256]{1,0:T(8,128)(2,1)S(1)} %get-tuple-element.38), channel_id=1, source_target_pairs={{0,1},{1,0},{2,3},{3,2},{4,5},{5,4},{6,7},{7,6},{8,9},{9,8},{10,11... | collective-permute-start | bytes 208904 | tf_op jit(solution)/shard_map/ppermute | solution.py:246
  20.1 1.1 %scale.1 = (f32[128,256]{1,0:T(8,128)S(1)}, f32[8,256]{1,0:T(8,128)S(1)}, f32[8,128,256]{2,1,0:T(8,128)}) custom-call(s32[8]{0:T(128)S(1)} %copy-done, s32[1]{0:T(128)S(6)} %copy.13.refs_4_.refs_1_, s32[8]{0:T(128)S(1)} %copy-done.1, f32[8]{0:T(128)S(1)} %copy-done.3, f32[1]{0:T(128)S(6)} %copy.14.refs_4_, f32[8,128]{1,0:T(8,128)S(1)} %bitcast.4, ...), custom_call_target="tpu_custom_call" | custom-call | tf_op jit(solution)/shard_map/scale/pallas_call | solution.py:339
  21.2 1.5 %collective-permute-done.8.refs_4_ = bf16[136,256]{1,0:T(8,128)(2,1)S(1)} collective-permute-done((bf16[136,256]{1,0:T(8,128)(2,1)S(1)}, bf16[136,256]{1,0:T(8,128)(2,1)S(1)}, u32[]{:S(2)}, u32[]{:S(2)}) %collective-permute-start.8) | collective-permute-done | bytes 69664 | tf_op jit(solution)/shard_map/ppermute | solution.py:246
  22.7 0.5 %collective-permute-done.9.refs_5_ = bf16[136,256]{1,0:T(8,128)(2,1)S(1)} collective-permute-done((bf16[136,256]{1,0:T(8,128)(2,1)S(1)}, bf16[136,256]{1,0:T(8,128)(2,1)S(1)}, u32[]{:S(2)}, u32[]{:S(2)}) %collective-permute-start.9) | collective-permute-done | bytes 69664 | tf_op jit(solution)/shard_map/ppermute | solution.py:246
  23.2 0.9 %place.1 = f32[8,128,256]{2,1,0:T(8,128)} custom-call(f32[128,256]{1,0:T(8,128)S(1)} %get-tuple-element.33.refs_0_, f32[8,256]{1,0:T(8,128)S(1)} %get-tuple-element.34.refs_1_, f32[8,128,256]{2,1,0:T(8,128)} %get-tuple-element.35.refs_2_, bf16[136,256]{1,0:T(8,128)(2,1)S(1)} %collective-permute-done.7.refs_3_, ...), custom_call_target="tpu_custom_call", output_to_operand_aliasing={{}: (2, {})} | custom-call | tf_op jit(solution)/shard_map/place/pallas_call | solution.py:376
  (9 shorter events, 0.0 us)
Async XLA Ops:
  0.0 9.4 %copy-start.1 = (s32[8]{0:T(128)S(1)}, s32[8]{0:T(128)}, u32[]{:S(2)}) copy-start(s32[8]{0:T(128)} %refs_2_.5) | copy-start | bytes 100
  0.0 9.4 %copy-start = (s32[8]{0:T(128)S(1)}, s32[8]{0:T(128)}, u32[]{:S(2)}) copy-start(s32[8]{0:T(128)} %refs_0_.3) | copy-start | bytes 100
  3.1 9.3 %collective-permute-start = (bf16[2,128,128]{2,1,0:T(8,128)(2,1)}, bf16[2,128,128]{2,1,0:T(8,128)(2,1)S(1)}, u32[]{:S(2)}, u32[]{:S(2)}) collective-permute-start(bf16[2,128,128]{2,1,0:T(8,128)(2,1)} %get-tuple-element.23), channel_id=1, source_target_pairs={{0,16},{4,20},{8,24},{12,28},{16,0},{20,4},{24,8},{28,12},{1,17},{... | collective-permute-start | bytes 196616 | tf_op jit(solution)/shard_map/ppermute | solution.py:246
  7.2 6.4 %collective-permute-start.2 = (bf16[2,128,128]{2,1,0:T(8,128)(2,1)}, bf16[2,128,128]{2,1,0:T(8,128)(2,1)S(1)}, u32[]{:S(2)}, u32[]{:S(2)}) collective-permute-start(bf16[2,128,128]{2,1,0:T(8,128)(2,1)} %get-tuple-element.28), channel_id=1, source_target_pairs={{0,24},{4,28},{8,16},{12,20},{16,8},{20,12},{24,0},{28,4},{1,25},{... | collective-permute-start | bytes 196616 | tf_op jit(solution)/shard_map/ppermute | solution.py:246
  8.5 5.2 %collective-permute-start.3 = (bf16[2,128,128]{2,1,0:T(8,128)(2,1)}, bf16[2,128,128]{2,1,0:T(8,128)(2,1)S(1)}, u32[]{:S(2)}, u32[]{:S(2)}) collective-permute-start(bf16[2,128,128]{2,1,0:T(8,128)(2,1)} %get-tuple-element.29), channel_id=1, source_target_pairs={{0,8},{4,12},{8,0},{12,4},{16,24},{20,28},{24,16},{28,20},{1,9},{5... | collective-permute-start | bytes 196616 | tf_op jit(solution)/shard_map/ppermute | solution.py:246
  9.4 10.7 %copy-start.2 = (f32[1024]{0:T(1024)S(1)}, f32[1024]{0:T(1024)}, u32[]{:S(2)}) copy-start(f32[1024]{0:T(1024)} %param.17) | copy-start | bytes 12292
  9.4 10.7 %copy-start.3 = (f32[8]{0:T(128)S(1)}, f32[8]{0:T(128)}, u32[]{:S(2)}) copy-start(f32[8]{0:T(128)} %refs_3_.1) | copy-start | bytes 100
  11.1 1.3 %collective-permute-start.1 = (bf16[1,128,128]{2,1,0:T(8,128)(2,1)S(1)}, bf16[1,128,128]{2,1,0:T(8,128)(2,1)S(1)}, u32[]{:S(2)}, u32[]{:S(2)}) collective-permute-start(bf16[1,128,128]{2,1,0:T(8,128)(2,1)S(1)} %get-tuple-element.24), channel_id=1, source_target_pairs={{0,4},{4,0},{8,12},{12,8},{16,20},{20,16},{24,28},{28,24},{1,5},{5... | collective-permute-start | bytes 98312 | tf_op jit(solution)/shard_map/ppermute | solution.py:246
  13.6 1.3 %collective-permute-start.5 = (bf16[2,128,128]{2,1,0:T(8,128)(2,1)S(1)}, bf16[2,128,128]{2,1,0:T(8,128)(2,1)S(1)}, u32[]{:S(2)}, u32[]{:S(2)}) collective-permute-start(bf16[2,128,128]{2,1,0:T(8,128)(2,1)S(1)} %collective-permute-done.2.refs_3_), channel_id=1, source_target_pairs={{0,4},{4,0},{8,12},{12,8},{16,20},{20,16},{24,28},{28,24},{1,5},{5... | collective-permute-start | bytes 196616 | tf_op jit(solution)/shard_map/ppermute | solution.py:246
  13.7 1.3 %collective-permute-start.6 = (bf16[2,128,128]{2,1,0:T(8,128)(2,1)S(1)}, bf16[2,128,128]{2,1,0:T(8,128)(2,1)S(1)}, u32[]{:S(2)}, u32[]{:S(2)}) collective-permute-start(bf16[2,128,128]{2,1,0:T(8,128)(2,1)S(1)} %collective-permute-done.3.refs_4_), channel_id=1, source_target_pairs={{0,4},{4,0},{8,12},{12,8},{16,20},{20,16},{24,28},{28,24},{1,5},{5... | collective-permute-start | bytes 196616 | tf_op jit(solution)/shard_map/ppermute | solution.py:246
  14.1 1.3 %collective-permute-start.4 = (bf16[2,128,128]{2,1,0:T(8,128)(2,1)S(1)}, bf16[2,128,128]{2,1,0:T(8,128)(2,1)S(1)}, u32[]{:S(2)}, u32[]{:S(2)}) collective-permute-start(bf16[2,128,128]{2,1,0:T(8,128)(2,1)S(1)} %collective-permute-done.refs_2_), channel_id=1, source_target_pairs={{0,4},{4,0},{8,12},{12,8},{16,20},{20,16},{24,28},{28,24},{1,5},{5... | collective-permute-start | bytes 196616 | tf_op jit(solution)/shard_map/ppermute | solution.py:246
  15.9 5.3 %collective-permute-start.7 = (bf16[136,256]{1,0:T(8,128)(2,1)S(1)}, bf16[136,256]{1,0:T(8,128)(2,1)S(1)}, u32[]{:S(2)}, u32[]{:S(2)}) collective-permute-start(bf16[136,256]{1,0:T(8,128)(2,1)S(1)} %get-tuple-element.36), channel_id=1, source_target_pairs={{0,3},{1,2},{2,1},{3,0},{4,7},{5,6},{6,5},{7,4},{8,11},{9,10},{10,... | collective-permute-start | bytes 208904 | tf_op jit(solution)/shard_map/ppermute | solution.py:246
  18.4 4.3 %collective-permute-start.8 = (bf16[136,256]{1,0:T(8,128)(2,1)S(1)}, bf16[136,256]{1,0:T(8,128)(2,1)S(1)}, u32[]{:S(2)}, u32[]{:S(2)}) collective-permute-start(bf16[136,256]{1,0:T(8,128)(2,1)S(1)} %get-tuple-element.37), channel_id=1, source_target_pairs={{0,2},{1,3},{2,0},{3,1},{4,6},{5,7},{6,4},{7,5},{8,10},{9,11},{10,... | collective-permute-start | bytes 208904 | tf_op jit(solution)/shard_map/ppermute | solution.py:246
  18.9 4.3 %collective-permute-start.9 = (bf16[136,256]{1,0:T(8,128)(2,1)S(1)}, bf16[136,256]{1,0:T(8,128)(2,1)S(1)}, u32[]{:S(2)}, u32[]{:S(2)}) collective-permute-start(bf16[136,256]{1,0:T(8,128)(2,1)S(1)} %get-tuple-element.38), channel_id=1, source_target_pairs={{0,1},{1,0},{2,3},{3,2},{4,5},{5,4},{6,7},{7,6},{8,9},{9,8},{10,11... | collective-permute-start | bytes 208904 | tf_op jit(solution)/shard_map/ppermute | solution.py:246

commit v3 on v2

--- a/solution.py
+++ b/solution.py
@@ -11,7 +11,8 @@
 TOP = 128.0
 LEAST = 2.0**-100
 SMALLEST = 2.0**-126
-SPARE = 8
+SPARE = 16
+PACKED = 16
 
 
 def vmem():
@@ -92,7 +93,6 @@
         side = lax.axis_index("rep") * tiles_b if by_partner else 0
         flip = len(steps) - tiles_b if by_partner else 0
         label_w = k_ref[0] ^ j_ref[0]
-        spot_row = lax.broadcasted_iota(jnp.int32, choice_ref.shape[1:], 0)
         for n in range(len(steps)):
             b_tile = n ^ flip ^ side
             c_tile = place_of(tile_ref, 1, label_w ^ tile_ref[b_tile])
@@ -103,10 +103,9 @@
             target = w_ref.at[:, pl.ds(n * TILE, TILE)]
             w_copies.append(pltpu.make_async_copy(source, target, w_sems.at[n]))
             w_copies[-1].start()
-            spot = jnp.int32(0)
-            for where, step in enumerate(steps):
-                spot = jnp.where((c_tile ^ me) == step, jnp.int32(where), spot)
-            choice_ref[n] = jnp.where(spot_row == spot, 1.0, 0.0)
+            for spot, step in enumerate(steps):
+                hit = jnp.where((c_tile ^ me) == step, 1.0, 0.0)
+                choice_ref[n, spot] = jnp.full((PACKED, TILE), hit).astype(choice_ref.dtype)
     label = k_ref[0] ^ tile_ref[own_tile]
     picks = []
     for step in pairs:
@@ -133,7 +132,7 @@
 
 def write_coded(out_ref, value):
     rows, width = value.shape
-    largest = jnp.max(jnp.max(jnp.abs(value), axis=0, keepdims=True), axis=1, keepdims=True)
+    largest = jnp.max(jnp.abs(value), axis=0, keepdims=True)
     exponent = jnp.ceil(jnp.log2(jnp.maximum(largest, LEAST)))
     scaled = value * (TOP * jnp.exp2(-exponent))
     power = scaled
@@ -155,6 +154,7 @@
 def multiply_kernel(spots, out_count, w_ref, choice_ref, *refs):
     out_refs = refs[-out_count:]
     blocks = [refs[n][spot] for n, spot in spots]
+    blocks = [block.reshape(TILE // PACKED, PACKED, block.shape[-1]) for block in blocks]
     tiles = choice_ref.shape[0]
     each = tiles // out_count
     for n, out_ref in enumerate(out_refs):
@@ -162,7 +162,8 @@
         for tile in range(n * each, (n + 1) * each):
             left = jnp.zeros_like(blocks[0])
             for spot, block in enumerate(blocks):
-                left = jnp.where(choice_ref[tile, spot : spot + 1, :] > 0.5, block, left)
+                left = left + block * choice_ref[tile, spot]
+            left = left.reshape(TILE, left.shape[-1])
             products.append(
                 lax.dot_general(
                     left,
@@ -287,7 +288,7 @@
             arguments += [j_irrep, w_cycle.reshape(full_width, full_width)]
             shapes += [
                 jax.ShapeDtypeStruct((TILE, full_width), w_cycle.dtype),
-                jax.ShapeDtypeStruct((tiles, tiles, TILE), jnp.float32),
+                jax.ShapeDtypeStruct((tiles, tiles, PACKED, TILE), t_slab.dtype),
             ]
             scratch += [small(j_irrep), pltpu.SemaphoreType.DMA((tiles,))]
         return pl.pallas_call(

time: 24.3 us -> 24.4 us (level)
  no operation moved by 1% of the time
where the time goes in v3:
time: 24.4 us; the launch traced here: 24.2 us
  starting transfers between devices  9.82 us (40%)
  Pallas kernels  6.49 us (27%)
  waiting for transfers between devices  5.76 us (24%)
  between operations  2.08 us (9%)
    ppermute x10, starting transfers between devices, swap(): lax.ppermute(block, axis, [(n, n ^ step) for n in range(lax.axis_size(axi...  9.82 us
    ppermute x10, waiting for transfers between devices, swap(): lax.ppermute(block, axis, [(n, n ^ step) for n in range(lax.axis_size(axi...  5.76 us
    pallas_call x2, Pallas kernels, pack(): pl.pallas_call(lambda *refs: pack_kernel(plan, *refs), in_specs=[hbm()] *...  3.98 us
    pallas_call x1, Pallas kernels, shards(): pl.pallas_call(lambda *refs: scale_kernel(a_width, *refs), in_specs=[hbm(...  1.09 us
    pallas_call x1, Pallas kernels, shards(): pl.pallas_call(lambda *refs: place_kernel(run, *refs), in_specs=[vmem(),...  0.86 us
    pallas_call x1, Pallas kernels, shards(): pl.pallas_call(lambda *refs: multiply_kernel(spots, len(part_shapes), *re...  0.56 us
  transfers between devices with their start and end apart: 10, of which 8 were waited for; matrix products, arithmetic and copies ran while one was open for 0% of the time, Pallas kernels for 11%

profile of v3, /device:TPU:0, one launch (start us, length us, event | category | flops | bytes accessed | tf_op | source)
XLA Modules:
  0.0 24.2 jit_solution(16031574928864157325)
XLA Ops:
  0.7 2.4 %pack_far.1 = (bf16[2,128,128]{2,1,0:T(8,128)(2,1)}, bf16[2,128,128]{2,1,0:T(8,128)(2,1)}, bf16[2,128,128]{2,1,0:T(8,128)(2,1)}) custom-call(s32[1]{0:T(128)S(6)} %copy.12.refs_0_, s32[8]{0:T(128)} %refs_0_.3, s32[8]{0:T(128)} %refs_2_.5, bf16[1024,1024]{1,0:T(8,128)(2,1)} %bitcast.5), custom_call_target="tpu_custom_call" | custom-call | tf_op jit(solution)/shard_map/pack_far/pallas_call | solution.py:294
  3.1 4.1 %collective-permute-start = (bf16[2,128,128]{2,1,0:T(8,128)(2,1)}, bf16[2,128,128]{2,1,0:T(8,128)(2,1)S(1)}, u32[]{:S(2)}, u32[]{:S(2)}) collective-permute-start(bf16[2,128,128]{2,1,0:T(8,128)(2,1)} %get-tuple-element.23), channel_id=1, source_target_pairs={{0,16},{4,20},{8,24},{12,28},{16,0},{20,4},{24,8},{28,12},{1,17},{... | collective-permute-start | bytes 196616 | tf_op jit(solution)/shard_map/ppermute | solution.py:247
  7.2 1.3 %collective-permute-start.2 = (bf16[2,128,128]{2,1,0:T(8,128)(2,1)}, bf16[2,128,128]{2,1,0:T(8,128)(2,1)S(1)}, u32[]{:S(2)}, u32[]{:S(2)}) collective-permute-start(bf16[2,128,128]{2,1,0:T(8,128)(2,1)} %get-tuple-element.28), channel_id=1, source_target_pairs={{0,24},{4,28},{8,16},{12,20},{16,8},{20,12},{24,0},{28,4},{1,25},{... | collective-permute-start | bytes 196616 | tf_op jit(solution)/shard_map/ppermute | solution.py:247
  8.5 0.2 collective-permute-start.3
  9.4 0.0 copy-start.2
  9.4 1.6 %pack_near.1 = (bf16[1,128,128]{2,1,0:T(8,128)(2,1)S(1)}, bf16[1,128,128]{2,1,0:T(8,128)(2,1)S(1)}, bf16[128,1024]{1,0:T(8,128)(2,1)S(1)}, bf16[8,8,16,128]{3,2,1,0:T(8,128)(2,1)S(1)}) custom-call(s32[1]{0:T(128)S(6)} %copy.12.refs_0_, s32[8]{0:T(128)S(1)} %copy-done, s32[8]{0:T(128)S(1)} %copy-done.1, bf16[1024,1024]{1,0:T(8,128)(2,1)} %bitcast.6, ...), custom_call_target="tpu_custom_call" | custom-call | tf_op jit(solution)/shard_map/pack_near/pallas_call | solution.py:294
  11.1 0.1 collective-permute-start.1
  11.1 1.2 %collective-permute-done.1.refs_5_ = bf16[1,128,128]{2,1,0:T(8,128)(2,1)S(1)} collective-permute-done((bf16[1,128,128]{2,1,0:T(8,128)(2,1)S(1)}, bf16[1,128,128]{2,1,0:T(8,128)(2,1)S(1)}, u32[]{:S(2)}, u32[]{:S(2)}) %collective-permute-start.1) | collective-permute-done | bytes 32800 | tf_op jit(solution)/shard_map/ppermute | solution.py:247
  12.3 1.3 %collective-permute-done.2.refs_3_ = bf16[2,128,128]{2,1,0:T(8,128)(2,1)S(1)} collective-permute-done((bf16[2,128,128]{2,1,0:T(8,128)(2,1)}, bf16[2,128,128]{2,1,0:T(8,128)(2,1)S(1)}, u32[]{:S(2)}, u32[]{:S(2)}) %collective-permute-start.2) | collective-permute-done | bytes 65568 | tf_op jit(solution)/shard_map/ppermute | solution.py:247
  13.6 0.1 collective-permute-done.3.refs_4_
  13.7 0.4 %collective-permute-start.6 = (bf16[2,128,128]{2,1,0:T(8,128)(2,1)S(1)}, bf16[2,128,128]{2,1,0:T(8,128)(2,1)S(1)}, u32[]{:S(2)}, u32[]{:S(2)}) collective-permute-start(bf16[2,128,128]{2,1,0:T(8,128)(2,1)S(1)} %collective-permute-done.3.refs_4_), channel_id=1, source_target_pairs={{0,4},{4,0},{8,12},{12,8},{16,20},{20,16},{24,28},{28,24},{1,5},{5... | collective-permute-start | bytes 196616 | tf_op jit(solution)/shard_map/ppermute | solution.py:247
  14.1 0.1 collective-permute-start.4
  14.2 0.7 %collective-permute-done.5.refs_8_ = bf16[2,128,128]{2,1,0:T(8,128)(2,1)S(1)} collective-permute-done((bf16[2,128,128]{2,1,0:T(8,128)(2,1)S(1)}, bf16[2,128,128]{2,1,0:T(8,128)(2,1)S(1)}, u32[]{:S(2)}, u32[]{:S(2)}) %collective-permute-start.5) | collective-permute-done | bytes 65568 | tf_op jit(solution)/shard_map/ppermute | solution.py:247
  14.8 0.2 collective-permute-done.6.refs_9_
  15.0 0.4 %collective-permute-done.4.refs_7_ = bf16[2,128,128]{2,1,0:T(8,128)(2,1)S(1)} collective-permute-done((bf16[2,128,128]{2,1,0:T(8,128)(2,1)S(1)}, bf16[2,128,128]{2,1,0:T(8,128)(2,1)S(1)}, u32[]{:S(2)}, u32[]{:S(2)}) %collective-permute-start.4) | collective-permute-done | bytes 65568 | tf_op jit(solution)/shard_map/ppermute | solution.py:247
  15.4 0.6 %multiply.1 = (bf16[144,256]{1,0:T(8,128)(2,1)S(1)}, bf16[144,256]{1,0:T(8,128)(2,1)S(1)}, bf16[144,256]{1,0:T(8,128)(2,1)S(1)}, f32[128,256]{1,0:T(8,128)S(1)}) custom-call(bf16[128,1024]{1,0:T(8,128)(2,1)S(1)} %get-tuple-element.22.refs_0_, bf16[8,8,16,128]{3,2,1,0:T(8,128)(2,1)S(1)} %get-tuple-element.26.refs_1_, ...), custom_call_target="tpu_custom_call" | custom-call | tf_op jit(solution)/shard_map/multiply/pallas_call | solution.py:330
  15.9 2.5 %collective-permute-start.7 = (bf16[144,256]{1,0:T(8,128)(2,1)S(1)}, bf16[144,256]{1,0:T(8,128)(2,1)S(1)}, u32[]{:S(2)}, u32[]{:S(2)}) collective-permute-start(bf16[144,256]{1,0:T(8,128)(2,1)S(1)} %get-tuple-element.36), channel_id=1, source_target_pairs={{0,3},{1,2},{2,1},{3,0},{4,7},{5,6},{6,5},{7,4},{8,11},{9,10},{10,... | collective-permute-start | bytes 221192 | tf_op jit(solution)/shard_map/ppermute | solution.py:247
  18.4 0.5 %collective-permute-start.8 = (bf16[144,256]{1,0:T(8,128)(2,1)S(1)}, bf16[144,256]{1,0:T(8,128)(2,1)S(1)}, u32[]{:S(2)}, u32[]{:S(2)}) collective-permute-start(bf16[144,256]{1,0:T(8,128)(2,1)S(1)} %get-tuple-element.37), channel_id=1, source_target_pairs={{0,2},{1,3},{2,0},{3,1},{4,6},{5,7},{6,4},{7,5},{8,10},{9,11},{10,... | collective-permute-start | bytes 221192 | tf_op jit(solution)/shard_map/ppermute | solution.py:247
  19.0 0.5 %collective-permute-start.9 = (bf16[144,256]{1,0:T(8,128)(2,1)S(1)}, bf16[144,256]{1,0:T(8,128)(2,1)S(1)}, u32[]{:S(2)}, u32[]{:S(2)}) collective-permute-start(bf16[144,256]{1,0:T(8,128)(2,1)S(1)} %get-tuple-element.38), channel_id=1, source_target_pairs={{0,1},{1,0},{2,3},{3,2},{4,5},{5,4},{6,7},{7,6},{8,9},{9,8},{10,11... | collective-permute-start | bytes 221192 | tf_op jit(solution)/shard_map/ppermute | solution.py:247
  20.2 1.1 %scale.1 = (f32[128,256]{1,0:T(8,128)S(1)}, f32[8,256]{1,0:T(8,128)S(1)}, f32[8,128,256]{2,1,0:T(8,128)}) custom-call(s32[8]{0:T(128)S(1)} %copy-done, s32[1]{0:T(128)S(6)} %copy.13.refs_4_.refs_1_, s32[8]{0:T(128)S(1)} %copy-done.1, f32[8]{0:T(128)S(1)} %copy-done.3, f32[1]{0:T(128)S(6)} %copy.14.refs_4_, f32[8,128]{1,0:T(8,128)S(1)} %bitcast.4, ...), custom_call_target="tpu_custom_call" | custom-call | tf_op jit(solution)/shard_map/scale/pallas_call | solution.py:340
  21.3 0.0 collective-permute-done.7.refs_3_
  21.3 1.5 %collective-permute-done.8.refs_4_ = bf16[144,256]{1,0:T(8,128)(2,1)S(1)} collective-permute-done((bf16[144,256]{1,0:T(8,128)(2,1)S(1)}, bf16[144,256]{1,0:T(8,128)(2,1)S(1)}, u32[]{:S(2)}, u32[]{:S(2)}) %collective-permute-start.8) | collective-permute-done | bytes 73760 | tf_op jit(solution)/shard_map/ppermute | solution.py:247
  22.8 0.5 %collective-permute-done.9.refs_5_ = bf16[144,256]{1,0:T(8,128)(2,1)S(1)} collective-permute-done((bf16[144,256]{1,0:T(8,128)(2,1)S(1)}, bf16[144,256]{1,0:T(8,128)(2,1)S(1)}, u32[]{:S(2)}, u32[]{:S(2)}) %collective-permute-start.9) | collective-permute-done | bytes 73760 | tf_op jit(solution)/shard_map/ppermute | solution.py:247
  23.3 0.9 %place.1 = f32[8,128,256]{2,1,0:T(8,128)} custom-call(f32[128,256]{1,0:T(8,128)S(1)} %get-tuple-element.33.refs_0_, f32[8,256]{1,0:T(8,128)S(1)} %get-tuple-element.34.refs_1_, f32[8,128,256]{2,1,0:T(8,128)} %get-tuple-element.35.refs_2_, bf16[144,256]{1,0:T(8,128)(2,1)S(1)} %collective-permute-done.7.refs_3_, ...), custom_call_target="tpu_custom_call", output_to_operand_aliasing={{}: (2, {})} | custom-call | tf_op jit(solution)/shard_map/place/pallas_call | solution.py:377
  (9 shorter events, 0.0 us)
Async XLA Ops:
  0.0 9.4 %copy-start.1 = (s32[8]{0:T(128)S(1)}, s32[8]{0:T(128)}, u32[]{:S(2)}) copy-start(s32[8]{0:T(128)} %refs_2_.5) | copy-start | bytes 100
  0.0 9.4 %copy-start = (s32[8]{0:T(128)S(1)}, s32[8]{0:T(128)}, u32[]{:S(2)}) copy-start(s32[8]{0:T(128)} %refs_0_.3) | copy-start | bytes 100
  3.1 9.3 %collective-permute-start = (bf16[2,128,128]{2,1,0:T(8,128)(2,1)}, bf16[2,128,128]{2,1,0:T(8,128)(2,1)S(1)}, u32[]{:S(2)}, u32[]{:S(2)}) collective-permute-start(bf16[2,128,128]{2,1,0:T(8,128)(2,1)} %get-tuple-element.23), channel_id=1, source_target_pairs={{0,16},{4,20},{8,24},{12,28},{16,0},{20,4},{24,8},{28,12},{1,17},{... | collective-permute-start | bytes 196616 | tf_op jit(solution)/shard_map/ppermute | solution.py:247
  7.2 6.4 %collective-permute-start.2 = (bf16[2,128,128]{2,1,0:T(8,128)(2,1)}, bf16[2,128,128]{2,1,0:T(8,128)(2,1)S(1)}, u32[]{:S(2)}, u32[]{:S(2)}) collective-permute-start(bf16[2,128,128]{2,1,0:T(8,128)(2,1)} %get-tuple-element.28), channel_id=1, source_target_pairs={{0,24},{4,28},{8,16},{12,20},{16,8},{20,12},{24,0},{28,4},{1,25},{... | collective-permute-start | bytes 196616 | tf_op jit(solution)/shard_map/ppermute | solution.py:247
  8.5 5.2 %collective-permute-start.3 = (bf16[2,128,128]{2,1,0:T(8,128)(2,1)}, bf16[2,128,128]{2,1,0:T(8,128)(2,1)S(1)}, u32[]{:S(2)}, u32[]{:S(2)}) collective-permute-start(bf16[2,128,128]{2,1,0:T(8,128)(2,1)} %get-tuple-element.29), channel_id=1, source_target_pairs={{0,8},{4,12},{8,0},{12,4},{16,24},{20,28},{24,16},{28,20},{1,9},{5... | collective-permute-start | bytes 196616 | tf_op jit(solution)/shard_map/ppermute | solution.py:247
  9.4 10.7 %copy-start.2 = (f32[1024]{0:T(1024)S(1)}, f32[1024]{0:T(1024)}, u32[]{:S(2)}) copy-start(f32[1024]{0:T(1024)} %param.17) | copy-start | bytes 12292
  9.4 10.7 %copy-start.3 = (f32[8]{0:T(128)S(1)}, f32[8]{0:T(128)}, u32[]{:S(2)}) copy-start(f32[8]{0:T(128)} %refs_3_.1) | copy-start | bytes 100
  11.1 1.3 %collective-permute-start.1 = (bf16[1,128,128]{2,1,0:T(8,128)(2,1)S(1)}, bf16[1,128,128]{2,1,0:T(8,128)(2,1)S(1)}, u32[]{:S(2)}, u32[]{:S(2)}) collective-permute-start(bf16[1,128,128]{2,1,0:T(8,128)(2,1)S(1)} %get-tuple-element.24), channel_id=1, source_target_pairs={{0,4},{4,0},{8,12},{12,8},{16,20},{20,16},{24,28},{28,24},{1,5},{5... | collective-permute-start | bytes 98312 | tf_op jit(solution)/shard_map/ppermute | solution.py:247
  13.6 1.3 %collective-permute-start.5 = (bf16[2,128,128]{2,1,0:T(8,128)(2,1)S(1)}, bf16[2,128,128]{2,1,0:T(8,128)(2,1)S(1)}, u32[]{:S(2)}, u32[]{:S(2)}) collective-permute-start(bf16[2,128,128]{2,1,0:T(8,128)(2,1)S(1)} %collective-permute-done.2.refs_3_), channel_id=1, source_target_pairs={{0,4},{4,0},{8,12},{12,8},{16,20},{20,16},{24,28},{28,24},{1,5},{5... | collective-permute-start | bytes 196616 | tf_op jit(solution)/shard_map/ppermute | solution.py:247
  13.7 1.3 %collective-permute-start.6 = (bf16[2,128,128]{2,1,0:T(8,128)(2,1)S(1)}, bf16[2,128,128]{2,1,0:T(8,128)(2,1)S(1)}, u32[]{:S(2)}, u32[]{:S(2)}) collective-permute-start(bf16[2,128,128]{2,1,0:T(8,128)(2,1)S(1)} %collective-permute-done.3.refs_4_), channel_id=1, source_target_pairs={{0,4},{4,0},{8,12},{12,8},{16,20},{20,16},{24,28},{28,24},{1,5},{5... | collective-permute-start | bytes 196616 | tf_op jit(solution)/shard_map/ppermute | solution.py:247
  14.1 1.3 %collective-permute-start.4 = (bf16[2,128,128]{2,1,0:T(8,128)(2,1)S(1)}, bf16[2,128,128]{2,1,0:T(8,128)(2,1)S(1)}, u32[]{:S(2)}, u32[]{:S(2)}) collective-permute-start(bf16[2,128,128]{2,1,0:T(8,128)(2,1)S(1)} %collective-permute-done.refs_2_), channel_id=1, source_target_pairs={{0,4},{4,0},{8,12},{12,8},{16,20},{20,16},{24,28},{28,24},{1,5},{5... | collective-permute-start | bytes 196616 | tf_op jit(solution)/shard_map/ppermute | solution.py:247
  15.9 5.4 %collective-permute-start.7 = (bf16[144,256]{1,0:T(8,128)(2,1)S(1)}, bf16[144,256]{1,0:T(8,128)(2,1)S(1)}, u32[]{:S(2)}, u32[]{:S(2)}) collective-permute-start(bf16[144,256]{1,0:T(8,128)(2,1)S(1)} %get-tuple-element.36), channel_id=1, source_target_pairs={{0,3},{1,2},{2,1},{3,0},{4,7},{5,6},{6,5},{7,4},{8,11},{9,10},{10,... | collective-permute-start | bytes 221192 | tf_op jit(solution)/shard_map/ppermute | solution.py:247
  18.4 4.4 %collective-permute-start.8 = (bf16[144,256]{1,0:T(8,128)(2,1)S(1)}, bf16[144,256]{1,0:T(8,128)(2,1)S(1)}, u32[]{:S(2)}, u32[]{:S(2)}) collective-permute-start(bf16[144,256]{1,0:T(8,128)(2,1)S(1)} %get-tuple-element.37), channel_id=1, source_target_pairs={{0,2},{1,3},{2,0},{3,1},{4,6},{5,7},{6,4},{7,5},{8,10},{9,11},{10,... | collective-permute-start | bytes 221192 | tf_op jit(solution)/shard_map/ppermute | solution.py:247
  19.0 4.4 %collective-permute-start.9 = (bf16[144,256]{1,0:T(8,128)(2,1)S(1)}, bf16[144,256]{1,0:T(8,128)(2,1)S(1)}, u32[]{:S(2)}, u32[]{:S(2)}) collective-permute-start(bf16[144,256]{1,0:T(8,128)(2,1)S(1)} %get-tuple-element.38), channel_id=1, source_target_pairs={{0,1},{1,0},{2,3},{3,2},{4,5},{5,4},{6,7},{7,6},{8,9},{9,8},{10,11... | collective-permute-start | bytes 221192 | tf_op jit(solution)/shard_map/ppermute | solution.py:247

commit v4 on v2

--- a/solution.py
+++ b/solution.py
@@ -11,7 +11,7 @@
 TOP = 128.0
 LEAST = 2.0**-100
 SMALLEST = 2.0**-126
-SPARE = 8
+SPARE = 16
 
 
 def vmem():
@@ -35,6 +35,11 @@
     for n in range(ref.shape[0] // stride):
         found = jnp.where(ref[n * stride] == label, jnp.int32(n), found)
     return found
+
+
+def tabulate(table_ref, ref, stride):
+    for n in range(table_ref.shape[0]):
+        table_ref[ref[n * stride]] = jnp.int32(n)
 
 
 def start_all(sources, targets, sems):
@@ -48,19 +53,15 @@
 def pack_kernel(plan, *refs):
     rows_i, run, c_width, by_partner, tiles_b, groups, steps = plan
     if steps:
-        k_hbm, i_hbm, tile_hbm, t_hbm, j_hbm, w_hbm, *refs = refs
-        *refs, j_ref, w_sems = refs
+        k_ref, j_ref, i_hbm, tile_hbm, t_hbm, w_hbm, *refs = refs
+        *refs, tile_of_ref, w_sems = refs
     else:
-        k_hbm, i_hbm, tile_hbm, t_hbm, *refs = refs
-    *refs, k_ref, i_ref, tile_ref, t_ref, small_sems, t_sems = refs
+        k_ref, i_hbm, tile_hbm, t_hbm, *refs = refs
+    *refs, i_ref, tile_ref, run_of_ref, t_ref, small_sems, t_sems = refs
     out_refs = refs[: len(groups)]
     runs = rows_i // run
     rows = CHUNK // runs
-    sources, targets = [k_hbm, i_hbm, tile_hbm], [k_ref, i_ref, tile_ref]
-    if steps:
-        sources.append(j_hbm)
-        targets.append(j_ref)
-    small_copies = start_all(sources, targets, small_sems)
+    small_copies = start_all((i_hbm, tile_hbm), (i_ref, tile_ref), small_sems)
     me = lax.axis_index("blk") if by_partner else 0
     places = {
         step: (out_ref, spot)
@@ -86,8 +87,10 @@
     own_tile = lax.axis_index("blk") * c_width // TILE
     for copy in small_copies:
         copy.wait()
+    tabulate(run_of_ref, i_ref, run)
     w_copies = []
     if steps:
+        tabulate(tile_of_ref, tile_ref, 1)
         w_ref, choice_ref = refs[len(groups) :]
         side = lax.axis_index("rep") * tiles_b if by_partner else 0
         flip = len(steps) - tiles_b if by_partner else 0
@@ -95,7 +98,7 @@
         spot_row = lax.broadcasted_iota(jnp.int32, choice_ref.shape[1:], 0)
         for n in range(len(steps)):
             b_tile = n ^ flip ^ side
-            c_tile = place_of(tile_ref, 1, label_w ^ tile_ref[b_tile])
+            c_tile = tile_of_ref[label_w ^ tile_ref[b_tile]]
             source = w_hbm.at[
                 pl.ds(pl.multiple_of(c_tile * TILE, TILE), TILE),
                 pl.ds(pl.multiple_of(b_tile * TILE, TILE), TILE),
@@ -112,7 +115,7 @@
     for step in pairs:
         rows_of_pair = []
         for own in (step, step + 1):
-            chosen = place_of(i_ref, run, label ^ tile_ref[me ^ own])
+            chosen = run_of_ref[label ^ tile_ref[me ^ own]]
             rows_of_pair.append(jnp.where(of_run == chosen, 1.0, 0.0).astype(jnp.bfloat16))
         picks.append(jnp.concatenate(rows_of_pair, axis=0))
     swapped = (me & 1) == 1
@@ -162,7 +165,10 @@
         for tile in range(n * each, (n + 1) * each):
             left = jnp.zeros_like(blocks[0])
             for spot, block in enumerate(blocks):
-                left = jnp.where(choice_ref[tile, spot : spot + 1, :] > 0.5, block, left)
+                chosen = choice_ref[tile, spot : spot + 1, :]
+                if block.shape[1] != TILE:
+                    chosen = jnp.broadcast_to(chosen[:, :1], (1, block.shape[1]))
+                left = jnp.where(chosen > 0.5, block, left)
             products.append(
                 lax.dot_general(
                     left,
@@ -258,7 +264,7 @@
     b_width = full_width // rep_count
     deep = c_width * run
     wide = run * a_width
-    by_partner = a_width == TILE and b_width % TILE == 0
+    by_partner = a_width == TILE and b_width % TILE == 0 and run == 1
     steps = list(reversed(range(tiles))) if by_partner else list(range(tiles))
     groups = [[step] for step in steps]
     if by_partner:
@@ -271,34 +277,37 @@
     def pack(some_groups, last):
         pairs = sum(len(group) for group in some_groups) // 2
         plan = (rows_i, run, c_width, by_partner, b_width // TILE, some_groups, steps * last)
-        arguments = [k_irrep, i_irrep, tile_irrep, t_rows]
+        arguments = [i_irrep, tile_irrep, t_rows]
+        scalars = [k_irrep]
         shapes = [
             jax.ShapeDtypeStruct((len(group), deep, TILE), t_slab.dtype) for group in some_groups
         ]
         scratch = [
-            small(k_irrep),
             small(i_irrep),
             small(tile_irrep),
+            small(tile_irrep),
             pltpu.VMEM((pairs, t_rows.shape[0], 2 * TILE), t_slab.dtype),
-            pltpu.SemaphoreType.DMA((3 + last,)),
+            pltpu.SemaphoreType.DMA((2,)),
             pltpu.SemaphoreType.DMA((pairs,)),
         ]
         if last:
-            arguments += [j_irrep, w_cycle.reshape(full_width, full_width)]
+            arguments.append(w_cycle.reshape(full_width, full_width))
+            scalars.append(j_irrep)
             shapes += [
                 jax.ShapeDtypeStruct((TILE, full_width), w_cycle.dtype),
                 jax.ShapeDtypeStruct((tiles, tiles, TILE), jnp.float32),
             ]
-            scratch += [small(j_irrep), pltpu.SemaphoreType.DMA((tiles,))]
+            scratch += [small(tile_irrep), pltpu.SemaphoreType.DMA((tiles,))]
         return pl.pallas_call(
             lambda *refs: pack_kernel(plan, *refs),
-            in_specs=[hbm()] * len(arguments),
+            in_specs=[pl.BlockSpec(memory_space=pltpu.SMEM)] * len(scalars)
+            + [hbm()] * len(arguments),
             out_specs=[vmem()] * len(shapes),
             out_shape=shapes,
             scratch_shapes=scratch,
             compiler_params=limit(52 if last else 62),
             name="pack_near" if last else "pack_far",
-        )(*arguments)
+        )(*scalars, *arguments)
 
     packed = list(pack(groups[:3], False)) if by_partner else []
     *near, chosen_w, choice = pack(groups[len(packed) :], True)

time: 24.3 us -> 24.3 us (level)
  no operation moved by 1% of the time
where the time goes in v4:
time: 24.3 us; the launch traced here: 24.1 us
  starting transfers between devices  9.82 us (40%)
  Pallas kernels  6.4 us (26%)
  waiting for transfers between devices  5.79 us (24%)
  between operations  2.08 us (9%)
    ppermute x10, starting transfers between devices, swap(): lax.ppermute(block, axis, [(n, n ^ step) for n in range(lax.axis_size(axi...  9.82 us
    ppermute x10, waiting for transfers between devices, swap(): lax.ppermute(block, axis, [(n, n ^ step) for n in range(lax.axis_size(axi...  5.79 us
    pallas_call x2, Pallas kernels, pack(): pl.pallas_call(lambda *refs: pack_kernel(plan, *refs), in_specs=[pl.Block...  3.94 us
    pallas_call x1, Pallas kernels, shards(): pl.pallas_call(lambda *refs: scale_kernel(a_width, *refs), in_specs=[hbm(...  1.09 us
    pallas_call x1, Pallas kernels, shards(): pl.pallas_call(lambda *refs: place_kernel(run, *refs), in_specs=[vmem(),...  0.86 us
    pallas_call x1, Pallas kernels, shards(): pl.pallas_call(lambda *refs: multiply_kernel(spots, len(part_shapes), *re...  0.51 us
  transfers between devices with their start and end apart: 10, of which 8 were waited for; matrix products, arithmetic and copies ran while one was open for 0% of the time, Pallas kernels for 11%

profile of v4, /device:TPU:0, one launch (start us, length us, event | category | flops | bytes accessed | tf_op | source)
XLA Modules:
  0.0 24.1 jit_solution(16937930239398452172)
XLA Ops:
  0.7 2.4 %pack_far.1 = (bf16[2,128,128]{2,1,0:T(8,128)(2,1)}, bf16[2,128,128]{2,1,0:T(8,128)(2,1)}, bf16[2,128,128]{2,1,0:T(8,128)(2,1)}) custom-call(s32[1]{0:T(128)S(6)} %copy.12.refs_0_, s32[8]{0:T(128)} %refs_0_.3, s32[8]{0:T(128)} %refs_2_.5, bf16[1024,1024]{1,0:T(8,128)(2,1)} %bitcast.5), custom_call_target="tpu_custom_call" | custom-call | tf_op jit(solution)/shard_map/pack_far/pallas_call | solution.py:301
  3.0 4.1 %collective-permute-start = (bf16[2,128,128]{2,1,0:T(8,128)(2,1)}, bf16[2,128,128]{2,1,0:T(8,128)(2,1)S(1)}, u32[]{:S(2)}, u32[]{:S(2)}) collective-permute-start(bf16[2,128,128]{2,1,0:T(8,128)(2,1)} %get-tuple-element.23), channel_id=1, source_target_pairs={{0,16},{4,20},{8,24},{12,28},{16,0},{20,4},{24,8},{28,12},{1,17},{... | collective-permute-start | bytes 196616 | tf_op jit(solution)/shard_map/ppermute | solution.py:252
  7.1 1.3 %collective-permute-start.2 = (bf16[2,128,128]{2,1,0:T(8,128)(2,1)}, bf16[2,128,128]{2,1,0:T(8,128)(2,1)S(1)}, u32[]{:S(2)}, u32[]{:S(2)}) collective-permute-start(bf16[2,128,128]{2,1,0:T(8,128)(2,1)} %get-tuple-element.28), channel_id=1, source_target_pairs={{0,24},{4,28},{8,16},{12,20},{16,8},{20,12},{24,0},{28,4},{1,25},{... | collective-permute-start | bytes 196616 | tf_op jit(solution)/shard_map/ppermute | solution.py:252
  8.5 0.2 collective-permute-start.3
  9.4 0.0 copy-start.2
  9.4 1.6 %pack_near.1 = (bf16[1,128,128]{2,1,0:T(8,128)(2,1)S(1)}, bf16[1,128,128]{2,1,0:T(8,128)(2,1)S(1)}, bf16[128,1024]{1,0:T(8,128)(2,1)S(1)}, f32[8,8,128]{2,1,0:T(8,128)S(1)}) custom-call(s32[1]{0:T(128)S(6)} %copy.12.refs_0_, s32[1]{0:T(128)S(6)} %copy.13.refs_1_, s32[8]{0:T(128)S(1)} %copy-done, s32[8]{0:T(128)S(1)} %copy-done.1, ...), custom_call_target="tpu_custom_call" | custom-call | tf_op jit(solution)/shard_map/pack_near/pallas_call | solution.py:301
  11.0 0.1 collective-permute-start.1
  11.1 1.2 %collective-permute-done.1.refs_5_ = bf16[1,128,128]{2,1,0:T(8,128)(2,1)S(1)} collective-permute-done((bf16[1,128,128]{2,1,0:T(8,128)(2,1)S(1)}, bf16[1,128,128]{2,1,0:T(8,128)(2,1)S(1)}, u32[]{:S(2)}, u32[]{:S(2)}) %collective-permute-start.1) | collective-permute-done | bytes 32800 | tf_op jit(solution)/shard_map/ppermute | solution.py:252
  12.3 1.3 %collective-permute-done.2.refs_3_ = bf16[2,128,128]{2,1,0:T(8,128)(2,1)S(1)} collective-permute-done((bf16[2,128,128]{2,1,0:T(8,128)(2,1)}, bf16[2,128,128]{2,1,0:T(8,128)(2,1)S(1)}, u32[]{:S(2)}, u32[]{:S(2)}) %collective-permute-start.2) | collective-permute-done | bytes 65568 | tf_op jit(solution)/shard_map/ppermute | solution.py:252
  13.6 0.1 collective-permute-done.3.refs_4_
  13.7 0.4 %collective-permute-start.6 = (bf16[2,128,128]{2,1,0:T(8,128)(2,1)S(1)}, bf16[2,128,128]{2,1,0:T(8,128)(2,1)S(1)}, u32[]{:S(2)}, u32[]{:S(2)}) collective-permute-start(bf16[2,128,128]{2,1,0:T(8,128)(2,1)S(1)} %collective-permute-done.3.refs_4_), channel_id=1, source_target_pairs={{0,4},{4,0},{8,12},{12,8},{16,20},{20,16},{24,28},{28,24},{1,5},{5... | collective-permute-start | bytes 196616 | tf_op jit(solution)/shard_map/ppermute | solution.py:252
  14.1 0.1 collective-permute-start.4
  14.2 0.7 %collective-permute-done.5.refs_8_ = bf16[2,128,128]{2,1,0:T(8,128)(2,1)S(1)} collective-permute-done((bf16[2,128,128]{2,1,0:T(8,128)(2,1)S(1)}, bf16[2,128,128]{2,1,0:T(8,128)(2,1)S(1)}, u32[]{:S(2)}, u32[]{:S(2)}) %collective-permute-start.5) | collective-permute-done | bytes 65568 | tf_op jit(solution)/shard_map/ppermute | solution.py:252
  14.8 0.2 collective-permute-done.6.refs_9_
  15.0 0.4 %collective-permute-done.4.refs_7_ = bf16[2,128,128]{2,1,0:T(8,128)(2,1)S(1)} collective-permute-done((bf16[2,128,128]{2,1,0:T(8,128)(2,1)S(1)}, bf16[2,128,128]{2,1,0:T(8,128)(2,1)S(1)}, u32[]{:S(2)}, u32[]{:S(2)}) %collective-permute-start.4) | collective-permute-done | bytes 65568 | tf_op jit(solution)/shard_map/ppermute | solution.py:252
  15.4 0.5 %multiply.1 = (bf16[144,256]{1,0:T(8,128)(2,1)S(1)}, bf16[144,256]{1,0:T(8,128)(2,1)S(1)}, bf16[144,256]{1,0:T(8,128)(2,1)S(1)}, f32[128,256]{1,0:T(8,128)S(1)}) custom-call(bf16[128,1024]{1,0:T(8,128)(2,1)S(1)} %get-tuple-element.22.refs_0_, f32[8,8,128]{2,1,0:T(8,128)S(1)} %get-tuple-element.26.refs_1_, ...), custom_call_target="tpu_custom_call" | custom-call | tf_op jit(solution)/shard_map/multiply/pallas_call | solution.py:338
  15.9 2.5 %collective-permute-start.7 = (bf16[144,256]{1,0:T(8,128)(2,1)S(1)}, bf16[144,256]{1,0:T(8,128)(2,1)S(1)}, u32[]{:S(2)}, u32[]{:S(2)}) collective-permute-start(bf16[144,256]{1,0:T(8,128)(2,1)S(1)} %get-tuple-element.36), channel_id=1, source_target_pairs={{0,3},{1,2},{2,1},{3,0},{4,7},{5,6},{6,5},{7,4},{8,11},{9,10},{10,... | collective-permute-start | bytes 221192 | tf_op jit(solution)/shard_map/ppermute | solution.py:252
  18.4 0.5 %collective-permute-start.8 = (bf16[144,256]{1,0:T(8,128)(2,1)S(1)}, bf16[144,256]{1,0:T(8,128)(2,1)S(1)}, u32[]{:S(2)}, u32[]{:S(2)}) collective-permute-start(bf16[144,256]{1,0:T(8,128)(2,1)S(1)} %get-tuple-element.37), channel_id=1, source_target_pairs={{0,2},{1,3},{2,0},{3,1},{4,6},{5,7},{6,4},{7,5},{8,10},{9,11},{10,... | collective-permute-start | bytes 221192 | tf_op jit(solution)/shard_map/ppermute | solution.py:252
  18.9 0.5 %collective-permute-start.9 = (bf16[144,256]{1,0:T(8,128)(2,1)S(1)}, bf16[144,256]{1,0:T(8,128)(2,1)S(1)}, u32[]{:S(2)}, u32[]{:S(2)}) collective-permute-start(bf16[144,256]{1,0:T(8,128)(2,1)S(1)} %get-tuple-element.38), channel_id=1, source_target_pairs={{0,1},{1,0},{2,3},{3,2},{4,5},{5,4},{6,7},{7,6},{8,9},{9,8},{10,11... | collective-permute-start | bytes 221192 | tf_op jit(solution)/shard_map/ppermute | solution.py:252
  20.1 1.1 %scale.1 = (f32[128,256]{1,0:T(8,128)S(1)}, f32[8,256]{1,0:T(8,128)S(1)}, f32[8,128,256]{2,1,0:T(8,128)}) custom-call(s32[8]{0:T(128)S(1)} %copy-done, s32[1]{0:T(128)S(6)} %copy.13.refs_1_, s32[8]{0:T(128)S(1)} %copy-done.1, f32[8]{0:T(128)S(1)} %copy-done.3, f32[1]{0:T(128)S(6)} %copy.14.refs_4_, f32[8,128]{1,0:T(8,128)S(1)} %bitcast.4, ...), custom_call_target="tpu_custom_call" | custom-call | tf_op jit(solution)/shard_map/scale/pallas_call | solution.py:348
  21.2 0.0 collective-permute-done.7.refs_3_
  21.2 1.5 %collective-permute-done.8.refs_4_ = bf16[144,256]{1,0:T(8,128)(2,1)S(1)} collective-permute-done((bf16[144,256]{1,0:T(8,128)(2,1)S(1)}, bf16[144,256]{1,0:T(8,128)(2,1)S(1)}, u32[]{:S(2)}, u32[]{:S(2)}) %collective-permute-start.8) | collective-permute-done | bytes 73760 | tf_op jit(solution)/shard_map/ppermute | solution.py:252
  22.8 0.5 %collective-permute-done.9.refs_5_ = bf16[144,256]{1,0:T(8,128)(2,1)S(1)} collective-permute-done((bf16[144,256]{1,0:T(8,128)(2,1)S(1)}, bf16[144,256]{1,0:T(8,128)(2,1)S(1)}, u32[]{:S(2)}, u32[]{:S(2)}) %collective-permute-start.9) | collective-permute-done | bytes 73760 | tf_op jit(solution)/shard_map/ppermute | solution.py:252
  23.2 0.9 %place.1 = f32[8,128,256]{2,1,0:T(8,128)} custom-call(f32[128,256]{1,0:T(8,128)S(1)} %get-tuple-element.33.refs_0_, f32[8,256]{1,0:T(8,128)S(1)} %get-tuple-element.34.refs_1_, f32[8,128,256]{2,1,0:T(8,128)} %get-tuple-element.35.refs_2_, bf16[144,256]{1,0:T(8,128)(2,1)S(1)} %collective-permute-done.7.refs_3_, ...), custom_call_target="tpu_custom_call", output_to_operand_aliasing={{}: (2, {})} | custom-call | tf_op jit(solution)/shard_map/place/pallas_call | solution.py:385
  (9 shorter events, 0.0 us)
Async XLA Ops:
  0.0 9.4 %copy-start.1 = (s32[8]{0:T(128)S(1)}, s32[8]{0:T(128)}, u32[]{:S(2)}) copy-start(s32[8]{0:T(128)} %refs_2_.5) | copy-start | bytes 100
  0.0 9.4 %copy-start = (s32[8]{0:T(128)S(1)}, s32[8]{0:T(128)}, u32[]{:S(2)}) copy-start(s32[8]{0:T(128)} %refs_0_.3) | copy-start | bytes 100
  3.0 9.3 %collective-permute-start = (bf16[2,128,128]{2,1,0:T(8,128)(2,1)}, bf16[2,128,128]{2,1,0:T(8,128)(2,1)S(1)}, u32[]{:S(2)}, u32[]{:S(2)}) collective-permute-start(bf16[2,128,128]{2,1,0:T(8,128)(2,1)} %get-tuple-element.23), channel_id=1, source_target_pairs={{0,16},{4,20},{8,24},{12,28},{16,0},{20,4},{24,8},{28,12},{1,17},{... | collective-permute-start | bytes 196616 | tf_op jit(solution)/shard_map/ppermute | solution.py:252
  7.1 6.4 %collective-permute-start.2 = (bf16[2,128,128]{2,1,0:T(8,128)(2,1)}, bf16[2,128,128]{2,1,0:T(8,128)(2,1)S(1)}, u32[]{:S(2)}, u32[]{:S(2)}) collective-permute-start(bf16[2,128,128]{2,1,0:T(8,128)(2,1)} %get-tuple-element.28), channel_id=1, source_target_pairs={{0,24},{4,28},{8,16},{12,20},{16,8},{20,12},{24,0},{28,4},{1,25},{... | collective-permute-start | bytes 196616 | tf_op jit(solution)/shard_map/ppermute | solution.py:252
  8.5 5.2 %collective-permute-start.3 = (bf16[2,128,128]{2,1,0:T(8,128)(2,1)}, bf16[2,128,128]{2,1,0:T(8,128)(2,1)S(1)}, u32[]{:S(2)}, u32[]{:S(2)}) collective-permute-start(bf16[2,128,128]{2,1,0:T(8,128)(2,1)} %get-tuple-element.29), channel_id=1, source_target_pairs={{0,8},{4,12},{8,0},{12,4},{16,24},{20,28},{24,16},{28,20},{1,9},{5... | collective-permute-start | bytes 196616 | tf_op jit(solution)/shard_map/ppermute | solution.py:252
  9.4 10.7 %copy-start.2 = (f32[1024]{0:T(1024)S(1)}, f32[1024]{0:T(1024)}, u32[]{:S(2)}) copy-start(f32[1024]{0:T(1024)} %param.17) | copy-start | bytes 12292
  9.4 10.7 %copy-start.3 = (f32[8]{0:T(128)S(1)}, f32[8]{0:T(128)}, u32[]{:S(2)}) copy-start(f32[8]{0:T(128)} %refs_3_.3) | copy-start | bytes 100
  11.0 1.3 %collective-permute-start.1 = (bf16[1,128,128]{2,1,0:T(8,128)(2,1)S(1)}, bf16[1,128,128]{2,1,0:T(8,128)(2,1)S(1)}, u32[]{:S(2)}, u32[]{:S(2)}) collective-permute-start(bf16[1,128,128]{2,1,0:T(8,128)(2,1)S(1)} %get-tuple-element.24), channel_id=1, source_target_pairs={{0,4},{4,0},{8,12},{12,8},{16,20},{20,16},{24,28},{28,24},{1,5},{5... | collective-permute-start | bytes 98312 | tf_op jit(solution)/shard_map/ppermute | solution.py:252
  13.6 1.3 %collective-permute-start.5 = (bf16[2,128,128]{2,1,0:T(8,128)(2,1)S(1)}, bf16[2,128,128]{2,1,0:T(8,128)(2,1)S(1)}, u32[]{:S(2)}, u32[]{:S(2)}) collective-permute-start(bf16[2,128,128]{2,1,0:T(8,128)(2,1)S(1)} %collective-permute-done.2.refs_3_), channel_id=1, source_target_pairs={{0,4},{4,0},{8,12},{12,8},{16,20},{20,16},{24,28},{28,24},{1,5},{5... | collective-permute-start | bytes 196616 | tf_op jit(solution)/shard_map/ppermute | solution.py:252
  13.7 1.3 %collective-permute-start.6 = (bf16[2,128,128]{2,1,0:T(8,128)(2,1)S(1)}, bf16[2,128,128]{2,1,0:T(8,128)(2,1)S(1)}, u32[]{:S(2)}, u32[]{:S(2)}) collective-permute-start(bf16[2,128,128]{2,1,0:T(8,128)(2,1)S(1)} %collective-permute-done.3.refs_4_), channel_id=1, source_target_pairs={{0,4},{4,0},{8,12},{12,8},{16,20},{20,16},{24,28},{28,24},{1,5},{5... | collective-permute-start | bytes 196616 | tf_op jit(solution)/shard_map/ppermute | solution.py:252
  14.1 1.3 %collective-permute-start.4 = (bf16[2,128,128]{2,1,0:T(8,128)(2,1)S(1)}, bf16[2,128,128]{2,1,0:T(8,128)(2,1)S(1)}, u32[]{:S(2)}, u32[]{:S(2)}) collective-permute-start(bf16[2,128,128]{2,1,0:T(8,128)(2,1)S(1)} %collective-permute-done.refs_2_), channel_id=1, source_target_pairs={{0,4},{4,0},{8,12},{12,8},{16,20},{20,16},{24,28},{28,24},{1,5},{5... | collective-permute-start | bytes 196616 | tf_op jit(solution)/shard_map/ppermute | solution.py:252
  15.9 5.4 %collective-permute-start.7 = (bf16[144,256]{1,0:T(8,128)(2,1)S(1)}, bf16[144,256]{1,0:T(8,128)(2,1)S(1)}, u32[]{:S(2)}, u32[]{:S(2)}) collective-permute-start(bf16[144,256]{1,0:T(8,128)(2,1)S(1)} %get-tuple-element.36), channel_id=1, source_target_pairs={{0,3},{1,2},{2,1},{3,0},{4,7},{5,6},{6,5},{7,4},{8,11},{9,10},{10,... | collective-permute-start | bytes 221192 | tf_op jit(solution)/shard_map/ppermute | solution.py:252
  18.4 4.4 %collective-permute-start.8 = (bf16[144,256]{1,0:T(8,128)(2,1)S(1)}, bf16[144,256]{1,0:T(8,128)(2,1)S(1)}, u32[]{:S(2)}, u32[]{:S(2)}) collective-permute-start(bf16[144,256]{1,0:T(8,128)(2,1)S(1)} %get-tuple-element.37), channel_id=1, source_target_pairs={{0,2},{1,3},{2,0},{3,1},{4,6},{5,7},{6,4},{7,5},{8,10},{9,11},{10,... | collective-permute-start | bytes 221192 | tf_op jit(solution)/shard_map/ppermute | solution.py:252
  18.9 4.4 %collective-permute-start.9 = (bf16[144,256]{1,0:T(8,128)(2,1)S(1)}, bf16[144,256]{1,0:T(8,128)(2,1)S(1)}, u32[]{:S(2)}, u32[]{:S(2)}) collective-permute-start(bf16[144,256]{1,0:T(8,128)(2,1)S(1)} %get-tuple-element.38), channel_id=1, source_target_pairs={{0,1},{1,0},{2,3},{3,2},{4,5},{5,4},{6,7},{7,6},{8,9},{9,8},{10,11... | collective-permute-start | bytes 221192 | tf_op jit(solution)/shard_map/ppermute | solution.py:252

commit v5 on v2

--- a/solution.py
+++ b/solution.py
@@ -11,7 +11,7 @@
 TOP = 128.0
 LEAST = 2.0**-100
 SMALLEST = 2.0**-126
-SPARE = 8
+SPARE = 16
 
 
 def vmem():
@@ -152,6 +152,10 @@
     return jnp.where(power == 0, 0.0, size)
 
 
+def second_kernel(pair_ref, out_ref):
+    out_ref[...] = pair_ref[1:]
+
+
 def multiply_kernel(spots, out_count, w_ref, choice_ref, *refs):
     out_refs = refs[-out_count:]
     blocks = [refs[n][spot] for n, spot in spots]
@@ -221,6 +225,10 @@
         copy.wait()
 
 
+def add_kernel(part_ref, so_far_ref, out_ref):
+    out_ref[...] = so_far_ref[...] + read_coded(part_ref)
+
+
 def place_kernel(run, denom_ref, run_ref, zero_hbm, *refs):
     parts_refs, out_hbm, block_ref, sems = refs[:-3], refs[-3], refs[-2], refs[-1]
     a_width, width = block_ref.shape[2:]
@@ -258,7 +266,7 @@
     b_width = full_width // rep_count
     deep = c_width * run
     wide = run * a_width
-    by_partner = a_width == TILE and b_width % TILE == 0
+    by_partner = a_width == TILE and b_width % TILE == 0 and run == 1
     steps = list(reversed(range(tiles))) if by_partner else list(range(tiles))
     groups = [[step] for step in steps]
     if by_partner:
@@ -308,11 +316,21 @@
         *far, beside, own = packed
         left = [swap(pair, "blk", group[0]) for pair, group in zip(far, groups)]
         left += [swap(beside, "blk", 1), own]
-        left[0], left[-2], choice = lax.optimization_barrier((left[0], left[-2], choice))
-        handed = [swap(pair, "blk", 1) for pair in left[: len(far)]]
+        left[2], left[-2], choice = lax.optimization_barrier((left[2], left[-2], choice))
+        handed = []
+        for pair in left[: len(far)]:
+            block = pl.pallas_call(
+                second_kernel,
+                in_specs=[vmem()],
+                out_specs=vmem(),
+                out_shape=jax.ShapeDtypeStruct((1,) + pair.shape[1:], pair.dtype),
+                compiler_params=limit(8),
+                name="second",
+            )(pair)
+            handed.append(swap(block, "blk", 1))
         spots = []
         for n in range(len(far)):
-            spots += [(n, 0), (len(left) + n, 1)]
+            spots += [(n, 0), (len(left) + n, 0)]
         spots += [(len(far), 0), (len(far) + 1, 0)]
         left += handed
         part_shapes = [
@@ -367,6 +385,17 @@
         gathered = [
             swap(part, "rep", rep_count - 1 - n) for n, part in enumerate(partials[:-1])
         ] + [partials[-1]]
+        while len(gathered) > 2:
+            first, *gathered, so_far = gathered
+            added = pl.pallas_call(
+                add_kernel,
+                in_specs=[vmem()] * 2,
+                out_specs=vmem(),
+                out_shape=jax.ShapeDtypeStruct(so_far.shape, so_far.dtype),
+                compiler_params=limit(8),
+                name="add",
+            )(first, so_far)
+            gathered.append(added)
     else:
         outgoing = partials[0].reshape(wide, rep_count, b_width).transpose(1, 0, 2)
         arrived = lax.all_to_all(outgoing, "rep", split_axis=0, concat_axis=0, tiled=True)
@@ -375,7 +404,7 @@
     part_width = min(TILE, b_width)
     result = pl.pallas_call(
         lambda *refs: place_kernel(run, *refs),
-        in_specs=[vmem(), vmem(), hbm()] + [vmem()] * rep_count,
+        in_specs=[vmem(), vmem(), hbm()] + [vmem()] * len(gathered),
         out_specs=hbm(),
         out_shape=out_shape,
         input_output_aliases={2: 0},

time: 24.3 us -> 23.9 us (0.984)
  waiting for transfers between devices: 5.71 us -> 4.81 us
  starting transfers between devices: 9.82 us -> 10.3 us
    ppermute x10, waiting for transfers between devices: 5.71 us -> 4.81 us  [swap(): lax.ppermute(block, axis, [(n, n ^ step) for n in range(lax.axis_size(axi...]
    ppermute x10, starting transfers between devices: 9.82 us -> 10.3 us  [swap(): lax.ppermute(block, axis, [(n, n ^ step) for n in range(lax.axis_size(axi...]
  transfers between devices with their start and end apart: 10 -> 10, of which waited for: 8 -> 7; matrix products, arithmetic and copies ran while one was open for 0% -> 0% of each run, Pallas kernels for 11% -> 12%
where the time goes in v5:
time: 23.9 us; the launch traced here: 23.7 us
  starting transfers between devices  10.3 us (43%)
  Pallas kernels  6.51 us (27%)
  waiting for transfers between devices  4.81 us (20%)
  between operations  2.1 us (9%)
    ppermute x10, starting transfers between devices, swap(): lax.ppermute(block, axis, [(n, n ^ step) for n in range(lax.axis_size(axi...  10.3 us
    ppermute x10, waiting for transfers between devices, swap(): lax.ppermute(block, axis, [(n, n ^ step) for n in range(lax.axis_size(axi...  4.81 us
    pallas_call x2, Pallas kernels, pack(): pl.pallas_call(lambda *refs: pack_kernel(plan, *refs), in_specs=[hbm()] *...  3.98 us
    pallas_call x1, Pallas kernels, shards(): pl.pallas_call(lambda *refs: scale_kernel(a_width, *refs), in_specs=[hbm(...  1.09 us
    pallas_call x1, Pallas kernels, shards(): pl.pallas_call(lambda *refs: place_kernel(run, *refs), in_specs=[vmem(),...  0.79 us
    pallas_call x1, Pallas kernels, shards(): pl.pallas_call(lambda *refs: multiply_kernel(spots, len(part_shapes), *re...  0.51 us
  transfers between devices with their start and end apart: 10, of which 7 were waited for; matrix products, arithmetic and copies ran while one was open for 0% of the time, Pallas kernels for 12%

profile of v5, /device:TPU:0, one launch (start us, length us, event | category | flops | bytes accessed | tf_op | source)
XLA Modules:
  0.0 23.7 jit_solution(3682152962550970372)
XLA Ops:
  0.7 2.4 %pack_far.1 = (bf16[2,128,128]{2,1,0:T(8,128)(2,1)}, bf16[2,128,128]{2,1,0:T(8,128)(2,1)}, bf16[2,128,128]{2,1,0:T(8,128)(2,1)}) custom-call(s32[1]{0:T(128)S(6)} %copy.12.refs_0_, s32[8]{0:T(128)} %refs_0_.3, s32[8]{0:T(128)} %refs_2_.5, bf16[1024,1024]{1,0:T(8,128)(2,1)} %bitcast.5), custom_call_target="tpu_custom_call" | custom-call | tf_op jit(solution)/shard_map/pack_far/pallas_call | solution.py:301
  3.1 4.1 %collective-permute-start.2 = (bf16[2,128,128]{2,1,0:T(8,128)(2,1)}, bf16[2,128,128]{2,1,0:T(8,128)(2,1)S(1)}, u32[]{:S(2)}, u32[]{:S(2)}) collective-permute-start(bf16[2,128,128]{2,1,0:T(8,128)(2,1)} %get-tuple-element.27), channel_id=1, source_target_pairs={{0,16},{4,20},{8,24},{12,28},{16,0},{20,4},{24,8},{28,12},{1,17},{... | collective-permute-start | bytes 196616 | tf_op jit(solution)/shard_map/ppermute | solution.py:254
  7.2 1.3 %collective-permute-start.3 = (bf16[2,128,128]{2,1,0:T(8,128)(2,1)}, bf16[2,128,128]{2,1,0:T(8,128)(2,1)S(1)}, u32[]{:S(2)}, u32[]{:S(2)}) collective-permute-start(bf16[2,128,128]{2,1,0:T(8,128)(2,1)} %get-tuple-element.28), channel_id=1, source_target_pairs={{0,24},{4,28},{8,16},{12,20},{16,8},{20,12},{24,0},{28,4},{1,25},{... | collective-permute-start | bytes 196616 | tf_op jit(solution)/shard_map/ppermute | solution.py:254
  8.5 0.2 collective-permute-start
  9.4 0.0 copy-start.2
  9.4 1.6 %pack_near.1 = (bf16[1,128,128]{2,1,0:T(8,128)(2,1)S(1)}, bf16[1,128,128]{2,1,0:T(8,128)(2,1)S(1)}, bf16[128,1024]{1,0:T(8,128)(2,1)S(1)}, f32[8,8,128]{2,1,0:T(8,128)S(1)}) custom-call(s32[1]{0:T(128)S(6)} %copy.12.refs_0_, s32[8]{0:T(128)S(1)} %copy-done, s32[8]{0:T(128)S(1)} %copy-done.1, bf16[1024,1024]{1,0:T(8,128)(2,1)} %bitcast.6, ...), custom_call_target="tpu_custom_call" | custom-call | tf_op jit(solution)/shard_map/pack_near/pallas_call | solution.py:301
  11.1 0.1 collective-permute-start.1
  11.2 0.5 %collective-permute-start.4 = (bf16[1,128,128]{2,1,0:T(8,128)(2,1)S(1)}, bf16[1,128,128]{2,1,0:T(8,128)(2,1)S(1)}, u32[]{:S(2)}, u32[]{:S(2)}) collective-permute-start(bf16[1,128,128]{2,1,0:T(8,128)(2,1)S(1)} %second.3), channel_id=1, source_target_pairs={{0,4},{4,0},{8,12},{12,8},{16,20},{20,16},{24,28},{28,24},{1,5},{5... | collective-permute-start | bytes 98312 | tf_op jit(solution)/shard_map/ppermute | solution.py:254
  11.6 2.0 %collective-permute-done.3.pair_ref.refs_3_ = bf16[2,128,128]{2,1,0:T(8,128)(2,1)S(1)} collective-permute-done((bf16[2,128,128]{2,1,0:T(8,128)(2,1)}, bf16[2,128,128]{2,1,0:T(8,128)(2,1)S(1)}, u32[]{:S(2)}, u32[]{:S(2)}) %collective-permute-start.3) | collective-permute-done | bytes 65568 | tf_op jit(solution)/shard_map/ppermute | solution.py:254
  13.6 0.1 collective-permute-done.pair_ref.refs_4_
  13.7 0.5 %collective-permute-start.6 = (bf16[1,128,128]{2,1,0:T(8,128)(2,1)S(1)}, bf16[1,128,128]{2,1,0:T(8,128)(2,1)S(1)}, u32[]{:S(2)}, u32[]{:S(2)}) collective-permute-start(bf16[1,128,128]{2,1,0:T(8,128)(2,1)S(1)} %second.5), channel_id=1, source_target_pairs={{0,4},{4,0},{8,12},{12,8},{16,20},{20,16},{24,28},{28,24},{1,5},{5... | collective-permute-start | bytes 98312 | tf_op jit(solution)/shard_map/ppermute | solution.py:254
  14.2 0.6 %collective-permute-done.5.refs_8_ = bf16[1,128,128]{2,1,0:T(8,128)(2,1)S(1)} collective-permute-done((bf16[1,128,128]{2,1,0:T(8,128)(2,1)S(1)}, bf16[1,128,128]{2,1,0:T(8,128)(2,1)S(1)}, u32[]{:S(2)}, u32[]{:S(2)}) %collective-permute-start.5) | collective-permute-done | bytes 32800 | tf_op jit(solution)/shard_map/ppermute | solution.py:254
  14.8 0.2 %collective-permute-done.6.refs_9_ = bf16[1,128,128]{2,1,0:T(8,128)(2,1)S(1)} collective-permute-done((bf16[1,128,128]{2,1,0:T(8,128)(2,1)S(1)}, bf16[1,128,128]{2,1,0:T(8,128)(2,1)S(1)}, u32[]{:S(2)}, u32[]{:S(2)}) %collective-permute-start.6) | collective-permute-done | bytes 32800 | tf_op jit(solution)/shard_map/ppermute | solution.py:254
  15.0 0.5 %multiply.1 = (bf16[144,256]{1,0:T(8,128)(2,1)S(1)}, bf16[144,256]{1,0:T(8,128)(2,1)S(1)}, bf16[144,256]{1,0:T(8,128)(2,1)S(1)}, f32[128,256]{1,0:T(8,128)S(1)}) custom-call(bf16[128,1024]{1,0:T(8,128)(2,1)S(1)} %get-tuple-element.22.refs_0_, f32[8,8,128]{2,1,0:T(8,128)S(1)} %get-tuple-element.26.refs_1_, ...), custom_call_target="tpu_custom_call" | custom-call | tf_op jit(solution)/shard_map/multiply/pallas_call | solution.py:347
  15.6 2.5 %collective-permute-start.9 = (bf16[144,256]{1,0:T(8,128)(2,1)S(1)}, bf16[144,256]{1,0:T(8,128)(2,1)S(1)}, u32[]{:S(2)}, u32[]{:S(2)}) collective-permute-start(bf16[144,256]{1,0:T(8,128)(2,1)S(1)} %get-tuple-element.38), channel_id=1, source_target_pairs={{0,3},{1,2},{2,1},{3,0},{4,7},{5,6},{6,5},{7,4},{8,11},{9,10},{10,... | collective-permute-start | bytes 221192 | tf_op jit(solution)/shard_map/ppermute | solution.py:254
  18.1 0.5 %collective-permute-start.8 = (bf16[144,256]{1,0:T(8,128)(2,1)S(1)}, bf16[144,256]{1,0:T(8,128)(2,1)S(1)}, u32[]{:S(2)}, u32[]{:S(2)}) collective-permute-start(bf16[144,256]{1,0:T(8,128)(2,1)S(1)} %get-tuple-element.37), channel_id=1, source_target_pairs={{0,2},{1,3},{2,0},{3,1},{4,6},{5,7},{6,4},{7,5},{8,10},{9,11},{10,... | collective-permute-start | bytes 221192 | tf_op jit(solution)/shard_map/ppermute | solution.py:254
  18.6 0.5 %collective-permute-start.7 = (bf16[144,256]{1,0:T(8,128)(2,1)S(1)}, bf16[144,256]{1,0:T(8,128)(2,1)S(1)}, u32[]{:S(2)}, u32[]{:S(2)}) collective-permute-start(bf16[144,256]{1,0:T(8,128)(2,1)S(1)} %get-tuple-element.36), channel_id=1, source_target_pairs={{0,1},{1,0},{2,3},{3,2},{4,5},{5,4},{6,7},{7,6},{8,9},{9,8},{10,11... | collective-permute-start | bytes 221192 | tf_op jit(solution)/shard_map/ppermute | solution.py:254
  19.8 1.1 %scale.1 = (f32[128,256]{1,0:T(8,128)S(1)}, f32[8,256]{1,0:T(8,128)S(1)}, f32[8,128,256]{2,1,0:T(8,128)}) custom-call(s32[8]{0:T(128)S(1)} %copy-done, s32[1]{0:T(128)S(6)} %copy.13.refs_4_.refs_1_, s32[8]{0:T(128)S(1)} %copy-done.1, f32[8]{0:T(128)S(1)} %copy-done.3, f32[1]{0:T(128)S(6)} %copy.14.refs_4_, f32[8,128]{1,0:T(8,128)S(1)} %bitcast.4, ...), custom_call_target="tpu_custom_call" | custom-call | tf_op jit(solution)/shard_map/scale/pallas_call | solution.py:357
  20.9 0.2 collective-permute-done.9.part_ref
  21.1 0.1 add.2.so_far_ref
  21.2 1.5 %collective-permute-done.8.part_ref = bf16[144,256]{1,0:T(8,128)(2,1)S(1)} collective-permute-done((bf16[144,256]{1,0:T(8,128)(2,1)S(1)}, bf16[144,256]{1,0:T(8,128)(2,1)S(1)}, u32[]{:S(2)}, u32[]{:S(2)}) %collective-permute-start.8) | collective-permute-done | bytes 73760 | tf_op jit(solution)/shard_map/ppermute | solution.py:254
  22.6 0.1 add.3.refs_4_
  22.7 0.2 %collective-permute-done.7.refs_3_ = bf16[144,256]{1,0:T(8,128)(2,1)S(1)} collective-permute-done((bf16[144,256]{1,0:T(8,128)(2,1)S(1)}, bf16[144,256]{1,0:T(8,128)(2,1)S(1)}, u32[]{:S(2)}, u32[]{:S(2)}) %collective-permute-start.7) | collective-permute-done | bytes 73760 | tf_op jit(solution)/shard_map/ppermute | solution.py:254
  22.9 0.8 %place.1 = f32[8,128,256]{2,1,0:T(8,128)} custom-call(f32[128,256]{1,0:T(8,128)S(1)} %get-tuple-element.33.refs_0_, f32[8,256]{1,0:T(8,128)S(1)} %get-tuple-element.34.refs_1_, f32[8,128,256]{2,1,0:T(8,128)} %get-tuple-element.35.refs_2_, bf16[144,256]{1,0:T(8,128)(2,1)S(1)} %collective-permute-done.7.refs_3_, ...), custom_call_target="tpu_custom_call", output_to_operand_aliasing={{}: (2, {})} | custom-call | tf_op jit(solution)/shard_map/place/pallas_call | solution.py:405
  (14 shorter events, 0.0 us)
Async XLA Ops:
  0.0 9.4 %copy-start.1 = (s32[8]{0:T(128)S(1)}, s32[8]{0:T(128)}, u32[]{:S(2)}) copy-start(s32[8]{0:T(128)} %refs_2_.5) | copy-start | bytes 100
  0.0 9.4 %copy-start = (s32[8]{0:T(128)S(1)}, s32[8]{0:T(128)}, u32[]{:S(2)}) copy-start(s32[8]{0:T(128)} %refs_0_.3) | copy-start | bytes 100
  3.1 8.1 %collective-permute-start.2 = (bf16[2,128,128]{2,1,0:T(8,128)(2,1)}, bf16[2,128,128]{2,1,0:T(8,128)(2,1)S(1)}, u32[]{:S(2)}, u32[]{:S(2)}) collective-permute-start(bf16[2,128,128]{2,1,0:T(8,128)(2,1)} %get-tuple-element.27), channel_id=1, source_target_pairs={{0,16},{4,20},{8,24},{12,28},{16,0},{20,4},{24,8},{28,12},{1,17},{... | collective-permute-start | bytes 196616 | tf_op jit(solution)/shard_map/ppermute | solution.py:254
  7.2 6.4 %collective-permute-start.3 = (bf16[2,128,128]{2,1,0:T(8,128)(2,1)}, bf16[2,128,128]{2,1,0:T(8,128)(2,1)S(1)}, u32[]{:S(2)}, u32[]{:S(2)}) collective-permute-start(bf16[2,128,128]{2,1,0:T(8,128)(2,1)} %get-tuple-element.28), channel_id=1, source_target_pairs={{0,24},{4,28},{8,16},{12,20},{16,8},{20,12},{24,0},{28,4},{1,25},{... | collective-permute-start | bytes 196616 | tf_op jit(solution)/shard_map/ppermute | solution.py:254
  8.5 5.2 %collective-permute-start = (bf16[2,128,128]{2,1,0:T(8,128)(2,1)}, bf16[2,128,128]{2,1,0:T(8,128)(2,1)S(1)}, u32[]{:S(2)}, u32[]{:S(2)}) collective-permute-start(bf16[2,128,128]{2,1,0:T(8,128)(2,1)} %get-tuple-element.23), channel_id=1, source_target_pairs={{0,8},{4,12},{8,0},{12,4},{16,24},{20,28},{24,16},{28,20},{1,9},{5... | collective-permute-start | bytes 196616 | tf_op jit(solution)/shard_map/ppermute | solution.py:254
  9.4 10.4 %copy-start.2 = (f32[1024]{0:T(1024)S(1)}, f32[1024]{0:T(1024)}, u32[]{:S(2)}) copy-start(f32[1024]{0:T(1024)} %param.17) | copy-start | bytes 12292
  9.4 10.4 %copy-start.3 = (f32[8]{0:T(128)S(1)}, f32[8]{0:T(128)}, u32[]{:S(2)}) copy-start(f32[8]{0:T(128)} %refs_3_.1) | copy-start | bytes 100
  11.1 2.5 %collective-permute-start.1 = (bf16[1,128,128]{2,1,0:T(8,128)(2,1)S(1)}, bf16[1,128,128]{2,1,0:T(8,128)(2,1)S(1)}, u32[]{:S(2)}, u32[]{:S(2)}) collective-permute-start(bf16[1,128,128]{2,1,0:T(8,128)(2,1)S(1)} %get-tuple-element.24), channel_id=1, source_target_pairs={{0,4},{4,0},{8,12},{12,8},{16,20},{20,16},{24,28},{28,24},{1,5},{5... | collective-permute-start | bytes 98312 | tf_op jit(solution)/shard_map/ppermute | solution.py:254
  11.2 3.0 %collective-permute-start.4 = (bf16[1,128,128]{2,1,0:T(8,128)(2,1)S(1)}, bf16[1,128,128]{2,1,0:T(8,128)(2,1)S(1)}, u32[]{:S(2)}, u32[]{:S(2)}) collective-permute-start(bf16[1,128,128]{2,1,0:T(8,128)(2,1)S(1)} %second.3), channel_id=1, source_target_pairs={{0,4},{4,0},{8,12},{12,8},{16,20},{20,16},{24,28},{28,24},{1,5},{5... | collective-permute-start | bytes 98312 | tf_op jit(solution)/shard_map/ppermute | solution.py:254
  13.6 1.2 %collective-permute-start.5 = (bf16[1,128,128]{2,1,0:T(8,128)(2,1)S(1)}, bf16[1,128,128]{2,1,0:T(8,128)(2,1)S(1)}, u32[]{:S(2)}, u32[]{:S(2)}) collective-permute-start(bf16[1,128,128]{2,1,0:T(8,128)(2,1)S(1)} %second.4), channel_id=1, source_target_pairs={{0,4},{4,0},{8,12},{12,8},{16,20},{20,16},{24,28},{28,24},{1,5},{5... | collective-permute-start | bytes 98312 | tf_op jit(solution)/shard_map/ppermute | solution.py:254
  13.7 1.4 %collective-permute-start.6 = (bf16[1,128,128]{2,1,0:T(8,128)(2,1)S(1)}, bf16[1,128,128]{2,1,0:T(8,128)(2,1)S(1)}, u32[]{:S(2)}, u32[]{:S(2)}) collective-permute-start(bf16[1,128,128]{2,1,0:T(8,128)(2,1)S(1)} %second.5), channel_id=1, source_target_pairs={{0,4},{4,0},{8,12},{12,8},{16,20},{20,16},{24,28},{28,24},{1,5},{5... | collective-permute-start | bytes 98312 | tf_op jit(solution)/shard_map/ppermute | solution.py:254
  15.6 5.5 %collective-permute-start.9 = (bf16[144,256]{1,0:T(8,128)(2,1)S(1)}, bf16[144,256]{1,0:T(8,128)(2,1)S(1)}, u32[]{:S(2)}, u32[]{:S(2)}) collective-permute-start(bf16[144,256]{1,0:T(8,128)(2,1)S(1)} %get-tuple-element.38), channel_id=1, source_target_pairs={{0,3},{1,2},{2,1},{3,0},{4,7},{5,6},{6,5},{7,4},{8,11},{9,10},{10,... | collective-permute-start | bytes 221192 | tf_op jit(solution)/shard_map/ppermute | solution.py:254
  18.1 4.6 %collective-permute-start.8 = (bf16[144,256]{1,0:T(8,128)(2,1)S(1)}, bf16[144,256]{1,0:T(8,128)(2,1)S(1)}, u32[]{:S(2)}, u32[]{:S(2)}) collective-permute-start(bf16[144,256]{1,0:T(8,128)(2,1)S(1)} %get-tuple-element.37), channel_id=1, source_target_pairs={{0,2},{1,3},{2,0},{3,1},{4,6},{5,7},{6,4},{7,5},{8,10},{9,11},{10,... | collective-permute-start | bytes 221192 | tf_op jit(solution)/shard_map/ppermute | solution.py:254
  18.6 4.4 %collective-permute-start.7 = (bf16[144,256]{1,0:T(8,128)(2,1)S(1)}, bf16[144,256]{1,0:T(8,128)(2,1)S(1)}, u32[]{:S(2)}, u32[]{:S(2)}) collective-permute-start(bf16[144,256]{1,0:T(8,128)(2,1)S(1)} %get-tuple-element.36), channel_id=1, source_target_pairs={{0,1},{1,0},{2,3},{3,2},{4,5},{5,4},{6,7},{7,6},{8,9},{9,8},{10,11... | collective-permute-start | bytes 221192 | tf_op jit(solution)/shard_map/ppermute | solution.py:254

commit v6 on v5

--- a/solution.py
+++ b/solution.py
@@ -133,7 +133,7 @@
 
 def write_coded(out_ref, value):
     rows, width = value.shape
-    largest = jnp.max(jnp.max(jnp.abs(value), axis=0, keepdims=True), axis=1, keepdims=True)
+    largest = jnp.max(jnp.abs(value), axis=0, keepdims=True)
     exponent = jnp.ceil(jnp.log2(jnp.maximum(largest, LEAST)))
     scaled = value * (TOP * jnp.exp2(-exponent))
     power = scaled
@@ -232,15 +232,15 @@
 def place_kernel(run, denom_ref, run_ref, zero_hbm, *refs):
     parts_refs, out_hbm, block_ref, sems = refs[:-3], refs[-3], refs[-2], refs[-1]
     a_width, width = block_ref.shape[2:]
+    spans = [slice(n * width, (n + 1) * width) for n in range(block_ref.shape[0])]
+    chosen_runs = [jnp.max(run_ref[:, columns]).astype(jnp.int32) for columns in spans]
     total = parts_refs[-1][...]
     for parts_ref in parts_refs[:-1]:
         coded = parts_ref.dtype != jnp.float32
         total = total + (read_coded(parts_ref) if coded else parts_ref[...])
     scaled = total / denom_ref[...]
     copies = []
-    for part in range(block_ref.shape[0]):
-        columns = slice(part * width, (part + 1) * width)
-        chosen = jnp.max(run_ref[:, columns]).astype(jnp.int32)
+    for part, (columns, chosen) in enumerate(zip(spans, chosen_runs)):
         for m in range(run):
             block_ref[part, m] = scaled[m * a_width : (m + 1) * a_width, columns]
         target = out_hbm.at[pl.ds(chosen * run, run), :, pl.ds(part * width, width)]

time: 23.9 us -> 23.9 us (level)
  no operation moved by 1% of the time
where the time goes in v6:
time: 23.9 us; the launch traced here: 23.7 us
  starting transfers between devices  10.3 us (43%)
  Pallas kernels  6.45 us (27%)
  waiting for transfers between devices  4.81 us (20%)
  between operations  2.1 us (9%)
    ppermute x10, starting transfers between devices, swap(): lax.ppermute(block, axis, [(n, n ^ step) for n in range(lax.axis_size(axi...  10.3 us
    ppermute x10, waiting for transfers between devices, swap(): lax.ppermute(block, axis, [(n, n ^ step) for n in range(lax.axis_size(axi...  4.81 us
    pallas_call x2, Pallas kernels, pack(): pl.pallas_call(lambda *refs: pack_kernel(plan, *refs), in_specs=[hbm()] *...  3.98 us
    pallas_call x1, Pallas kernels, shards(): pl.pallas_call(lambda *refs: scale_kernel(a_width, *refs), in_specs=[hbm(...  1.09 us
    pallas_call x1, Pallas kernels, shards(): pl.pallas_call(lambda *refs: place_kernel(run, *refs), in_specs=[vmem(),...  0.79 us
  transfers between devices with their start and end apart: 10, of which 7 were waited for; matrix products, arithmetic and copies ran while one was open for 0% of the time, Pallas kernels for 12%

profile of v6, /device:TPU:0, one launch (start us, length us, event | category | flops | bytes accessed | tf_op | source)
XLA Modules:
  0.0 23.7 jit_solution(6847326614027026458)
XLA Ops:
  0.7 2.4 %pack_far.1 = (bf16[2,128,128]{2,1,0:T(8,128)(2,1)}, bf16[2,128,128]{2,1,0:T(8,128)(2,1)}, bf16[2,128,128]{2,1,0:T(8,128)(2,1)}) custom-call(s32[1]{0:T(128)S(6)} %copy.12.refs_0_, s32[8]{0:T(128)} %refs_0_.3, s32[8]{0:T(128)} %refs_2_.5, bf16[1024,1024]{1,0:T(8,128)(2,1)} %bitcast.5), custom_call_target="tpu_custom_call" | custom-call | tf_op jit(solution)/shard_map/pack_far/pallas_call | solution.py:301
  3.1 4.1 %collective-permute-start.2 = (bf16[2,128,128]{2,1,0:T(8,128)(2,1)}, bf16[2,128,128]{2,1,0:T(8,128)(2,1)S(1)}, u32[]{:S(2)}, u32[]{:S(2)}) collective-permute-start(bf16[2,128,128]{2,1,0:T(8,128)(2,1)} %get-tuple-element.27), channel_id=1, source_target_pairs={{0,16},{4,20},{8,24},{12,28},{16,0},{20,4},{24,8},{28,12},{1,17},{... | collective-permute-start | bytes 196616 | tf_op jit(solution)/shard_map/ppermute | solution.py:254
  7.2 1.3 %collective-permute-start.3 = (bf16[2,128,128]{2,1,0:T(8,128)(2,1)}, bf16[2,128,128]{2,1,0:T(8,128)(2,1)S(1)}, u32[]{:S(2)}, u32[]{:S(2)}) collective-permute-start(bf16[2,128,128]{2,1,0:T(8,128)(2,1)} %get-tuple-element.28), channel_id=1, source_target_pairs={{0,24},{4,28},{8,16},{12,20},{16,8},{20,12},{24,0},{28,4},{1,25},{... | collective-permute-start | bytes 196616 | tf_op jit(solution)/shard_map/ppermute | solution.py:254
  8.5 0.2 collective-permute-start
  9.4 0.0 copy-start.2
  9.4 1.6 %pack_near.1 = (bf16[1,128,128]{2,1,0:T(8,128)(2,1)S(1)}, bf16[1,128,128]{2,1,0:T(8,128)(2,1)S(1)}, bf16[128,1024]{1,0:T(8,128)(2,1)S(1)}, f32[8,8,128]{2,1,0:T(8,128)S(1)}) custom-call(s32[1]{0:T(128)S(6)} %copy.12.refs_0_, s32[8]{0:T(128)S(1)} %copy-done, s32[8]{0:T(128)S(1)} %copy-done.1, bf16[1024,1024]{1,0:T(8,128)(2,1)} %bitcast.6, ...), custom_call_target="tpu_custom_call" | custom-call | tf_op jit(solution)/shard_map/pack_near/pallas_call | solution.py:301
  11.1 0.1 collective-permute-start.1
  11.2 0.5 %collective-permute-start.4 = (bf16[1,128,128]{2,1,0:T(8,128)(2,1)S(1)}, bf16[1,128,128]{2,1,0:T(8,128)(2,1)S(1)}, u32[]{:S(2)}, u32[]{:S(2)}) collective-permute-start(bf16[1,128,128]{2,1,0:T(8,128)(2,1)S(1)} %second.3), channel_id=1, source_target_pairs={{0,4},{4,0},{8,12},{12,8},{16,20},{20,16},{24,28},{28,24},{1,5},{5... | collective-permute-start | bytes 98312 | tf_op jit(solution)/shard_map/ppermute | solution.py:254
  11.6 2.0 %collective-permute-done.3.pair_ref.refs_3_ = bf16[2,128,128]{2,1,0:T(8,128)(2,1)S(1)} collective-permute-done((bf16[2,128,128]{2,1,0:T(8,128)(2,1)}, bf16[2,128,128]{2,1,0:T(8,128)(2,1)S(1)}, u32[]{:S(2)}, u32[]{:S(2)}) %collective-permute-start.3) | collective-permute-done | bytes 65568 | tf_op jit(solution)/shard_map/ppermute | solution.py:254
  13.6 0.1 collective-permute-done.pair_ref.refs_4_
  13.7 0.5 %collective-permute-start.6 = (bf16[1,128,128]{2,1,0:T(8,128)(2,1)S(1)}, bf16[1,128,128]{2,1,0:T(8,128)(2,1)S(1)}, u32[]{:S(2)}, u32[]{:S(2)}) collective-permute-start(bf16[1,128,128]{2,1,0:T(8,128)(2,1)S(1)} %second.5), channel_id=1, source_target_pairs={{0,4},{4,0},{8,12},{12,8},{16,20},{20,16},{24,28},{28,24},{1,5},{5... | collective-permute-start | bytes 98312 | tf_op jit(solution)/shard_map/ppermute | solution.py:254
  14.2 0.6 %collective-permute-done.5.refs_8_ = bf16[1,128,128]{2,1,0:T(8,128)(2,1)S(1)} collective-permute-done((bf16[1,128,128]{2,1,0:T(8,128)(2,1)S(1)}, bf16[1,128,128]{2,1,0:T(8,128)(2,1)S(1)}, u32[]{:S(2)}, u32[]{:S(2)}) %collective-permute-start.5) | collective-permute-done | bytes 32800 | tf_op jit(solution)/shard_map/ppermute | solution.py:254
  14.8 0.2 %collective-permute-done.6.refs_9_ = bf16[1,128,128]{2,1,0:T(8,128)(2,1)S(1)} collective-permute-done((bf16[1,128,128]{2,1,0:T(8,128)(2,1)S(1)}, bf16[1,128,128]{2,1,0:T(8,128)(2,1)S(1)}, u32[]{:S(2)}, u32[]{:S(2)}) %collective-permute-start.6) | collective-permute-done | bytes 32800 | tf_op jit(solution)/shard_map/ppermute | solution.py:254
  15.0 0.4 %multiply.1 = (bf16[144,256]{1,0:T(8,128)(2,1)S(1)}, bf16[144,256]{1,0:T(8,128)(2,1)S(1)}, bf16[144,256]{1,0:T(8,128)(2,1)S(1)}, f32[128,256]{1,0:T(8,128)S(1)}) custom-call(bf16[128,1024]{1,0:T(8,128)(2,1)S(1)} %get-tuple-element.22.refs_0_, f32[8,8,128]{2,1,0:T(8,128)S(1)} %get-tuple-element.26.refs_1_, ...), custom_call_target="tpu_custom_call" | custom-call | tf_op jit(solution)/shard_map/multiply/pallas_call | solution.py:347
  15.5 2.5 %collective-permute-start.9 = (bf16[144,256]{1,0:T(8,128)(2,1)S(1)}, bf16[144,256]{1,0:T(8,128)(2,1)S(1)}, u32[]{:S(2)}, u32[]{:S(2)}) collective-permute-start(bf16[144,256]{1,0:T(8,128)(2,1)S(1)} %get-tuple-element.38), channel_id=1, source_target_pairs={{0,3},{1,2},{2,1},{3,0},{4,7},{5,6},{6,5},{7,4},{8,11},{9,10},{10,... | collective-permute-start | bytes 221192 | tf_op jit(solution)/shard_map/ppermute | solution.py:254
  18.0 0.5 %collective-permute-start.8 = (bf16[144,256]{1,0:T(8,128)(2,1)S(1)}, bf16[144,256]{1,0:T(8,128)(2,1)S(1)}, u32[]{:S(2)}, u32[]{:S(2)}) collective-permute-start(bf16[144,256]{1,0:T(8,128)(2,1)S(1)} %get-tuple-element.37), channel_id=1, source_target_pairs={{0,2},{1,3},{2,0},{3,1},{4,6},{5,7},{6,4},{7,5},{8,10},{9,11},{10,... | collective-permute-start | bytes 221192 | tf_op jit(solution)/shard_map/ppermute | solution.py:254
  18.5 0.5 %collective-permute-start.7 = (bf16[144,256]{1,0:T(8,128)(2,1)S(1)}, bf16[144,256]{1,0:T(8,128)(2,1)S(1)}, u32[]{:S(2)}, u32[]{:S(2)}) collective-permute-start(bf16[144,256]{1,0:T(8,128)(2,1)S(1)} %get-tuple-element.36), channel_id=1, source_target_pairs={{0,1},{1,0},{2,3},{3,2},{4,5},{5,4},{6,7},{7,6},{8,9},{9,8},{10,11... | collective-permute-start | bytes 221192 | tf_op jit(solution)/shard_map/ppermute | solution.py:254
  19.7 1.1 %scale.1 = (f32[128,256]{1,0:T(8,128)S(1)}, f32[8,256]{1,0:T(8,128)S(1)}, f32[8,128,256]{2,1,0:T(8,128)}) custom-call(s32[8]{0:T(128)S(1)} %copy-done, s32[1]{0:T(128)S(6)} %copy.13.refs_4_.refs_1_, s32[8]{0:T(128)S(1)} %copy-done.1, f32[8]{0:T(128)S(1)} %copy-done.3, f32[1]{0:T(128)S(6)} %copy.14.refs_4_, f32[8,128]{1,0:T(8,128)S(1)} %bitcast.4, ...), custom_call_target="tpu_custom_call" | custom-call | tf_op jit(solution)/shard_map/scale/pallas_call | solution.py:357
  20.8 0.2 collective-permute-done.9.part_ref
  21.0 0.1 add.2.so_far_ref
  21.1 1.5 %collective-permute-done.8.part_ref = bf16[144,256]{1,0:T(8,128)(2,1)S(1)} collective-permute-done((bf16[144,256]{1,0:T(8,128)(2,1)S(1)}, bf16[144,256]{1,0:T(8,128)(2,1)S(1)}, u32[]{:S(2)}, u32[]{:S(2)}) %collective-permute-start.8) | collective-permute-done | bytes 73760 | tf_op jit(solution)/shard_map/ppermute | solution.py:254
  22.6 0.1 add.3.refs_4_
  22.6 0.2 %collective-permute-done.7.refs_3_ = bf16[144,256]{1,0:T(8,128)(2,1)S(1)} collective-permute-done((bf16[144,256]{1,0:T(8,128)(2,1)S(1)}, bf16[144,256]{1,0:T(8,128)(2,1)S(1)}, u32[]{:S(2)}, u32[]{:S(2)}) %collective-permute-start.7) | collective-permute-done | bytes 73760 | tf_op jit(solution)/shard_map/ppermute | solution.py:254
  22.9 0.8 %place.1 = f32[8,128,256]{2,1,0:T(8,128)} custom-call(f32[128,256]{1,0:T(8,128)S(1)} %get-tuple-element.33.refs_0_, f32[8,256]{1,0:T(8,128)S(1)} %get-tuple-element.34.refs_1_, f32[8,128,256]{2,1,0:T(8,128)} %get-tuple-element.35.refs_2_, bf16[144,256]{1,0:T(8,128)(2,1)S(1)} %collective-permute-done.7.refs_3_, ...), custom_call_target="tpu_custom_call", output_to_operand_aliasing={{}: (2, {})} | custom-call | tf_op jit(solution)/shard_map/place/pallas_call | solution.py:405
  (14 shorter events, 0.0 us)
Async XLA Ops:
  0.0 9.4 %copy-start.1 = (s32[8]{0:T(128)S(1)}, s32[8]{0:T(128)}, u32[]{:S(2)}) copy-start(s32[8]{0:T(128)} %refs_2_.5) | copy-start | bytes 100
  0.0 9.4 %copy-start = (s32[8]{0:T(128)S(1)}, s32[8]{0:T(128)}, u32[]{:S(2)}) copy-start(s32[8]{0:T(128)} %refs_0_.3) | copy-start | bytes 100
  3.1 8.1 %collective-permute-start.2 = (bf16[2,128,128]{2,1,0:T(8,128)(2,1)}, bf16[2,128,128]{2,1,0:T(8,128)(2,1)S(1)}, u32[]{:S(2)}, u32[]{:S(2)}) collective-permute-start(bf16[2,128,128]{2,1,0:T(8,128)(2,1)} %get-tuple-element.27), channel_id=1, source_target_pairs={{0,16},{4,20},{8,24},{12,28},{16,0},{20,4},{24,8},{28,12},{1,17},{... | collective-permute-start | bytes 196616 | tf_op jit(solution)/shard_map/ppermute | solution.py:254
  7.2 6.4 %collective-permute-start.3 = (bf16[2,128,128]{2,1,0:T(8,128)(2,1)}, bf16[2,128,128]{2,1,0:T(8,128)(2,1)S(1)}, u32[]{:S(2)}, u32[]{:S(2)}) collective-permute-start(bf16[2,128,128]{2,1,0:T(8,128)(2,1)} %get-tuple-element.28), channel_id=1, source_target_pairs={{0,24},{4,28},{8,16},{12,20},{16,8},{20,12},{24,0},{28,4},{1,25},{... | collective-permute-start | bytes 196616 | tf_op jit(solution)/shard_map/ppermute | solution.py:254
  8.5 5.2 %collective-permute-start = (bf16[2,128,128]{2,1,0:T(8,128)(2,1)}, bf16[2,128,128]{2,1,0:T(8,128)(2,1)S(1)}, u32[]{:S(2)}, u32[]{:S(2)}) collective-permute-start(bf16[2,128,128]{2,1,0:T(8,128)(2,1)} %get-tuple-element.23), channel_id=1, source_target_pairs={{0,8},{4,12},{8,0},{12,4},{16,24},{20,28},{24,16},{28,20},{1,9},{5... | collective-permute-start | bytes 196616 | tf_op jit(solution)/shard_map/ppermute | solution.py:254
  9.4 10.3 %copy-start.2 = (f32[1024]{0:T(1024)S(1)}, f32[1024]{0:T(1024)}, u32[]{:S(2)}) copy-start(f32[1024]{0:T(1024)} %param.17) | copy-start | bytes 12292
  9.4 10.3 %copy-start.3 = (f32[8]{0:T(128)S(1)}, f32[8]{0:T(128)}, u32[]{:S(2)}) copy-start(f32[8]{0:T(128)} %refs_3_.1) | copy-start | bytes 100
  11.1 2.5 %collective-permute-start.1 = (bf16[1,128,128]{2,1,0:T(8,128)(2,1)S(1)}, bf16[1,128,128]{2,1,0:T(8,128)(2,1)S(1)}, u32[]{:S(2)}, u32[]{:S(2)}) collective-permute-start(bf16[1,128,128]{2,1,0:T(8,128)(2,1)S(1)} %get-tuple-element.24), channel_id=1, source_target_pairs={{0,4},{4,0},{8,12},{12,8},{16,20},{20,16},{24,28},{28,24},{1,5},{5... | collective-permute-start | bytes 98312 | tf_op jit(solution)/shard_map/ppermute | solution.py:254
  11.2 3.0 %collective-permute-start.4 = (bf16[1,128,128]{2,1,0:T(8,128)(2,1)S(1)}, bf16[1,128,128]{2,1,0:T(8,128)(2,1)S(1)}, u32[]{:S(2)}, u32[]{:S(2)}) collective-permute-start(bf16[1,128,128]{2,1,0:T(8,128)(2,1)S(1)} %second.3), channel_id=1, source_target_pairs={{0,4},{4,0},{8,12},{12,8},{16,20},{20,16},{24,28},{28,24},{1,5},{5... | collective-permute-start | bytes 98312 | tf_op jit(solution)/shard_map/ppermute | solution.py:254
  13.6 1.2 %collective-permute-start.5 = (bf16[1,128,128]{2,1,0:T(8,128)(2,1)S(1)}, bf16[1,128,128]{2,1,0:T(8,128)(2,1)S(1)}, u32[]{:S(2)}, u32[]{:S(2)}) collective-permute-start(bf16[1,128,128]{2,1,0:T(8,128)(2,1)S(1)} %second.4), channel_id=1, source_target_pairs={{0,4},{4,0},{8,12},{12,8},{16,20},{20,16},{24,28},{28,24},{1,5},{5... | collective-permute-start | bytes 98312 | tf_op jit(solution)/shard_map/ppermute | solution.py:254
  13.7 1.4 %collective-permute-start.6 = (bf16[1,128,128]{2,1,0:T(8,128)(2,1)S(1)}, bf16[1,128,128]{2,1,0:T(8,128)(2,1)S(1)}, u32[]{:S(2)}, u32[]{:S(2)}) collective-permute-start(bf16[1,128,128]{2,1,0:T(8,128)(2,1)S(1)} %second.5), channel_id=1, source_target_pairs={{0,4},{4,0},{8,12},{12,8},{16,20},{20,16},{24,28},{28,24},{1,5},{5... | collective-permute-start | bytes 98312 | tf_op jit(solution)/shard_map/ppermute | solution.py:254
  15.5 5.5 %collective-permute-start.9 = (bf16[144,256]{1,0:T(8,128)(2,1)S(1)}, bf16[144,256]{1,0:T(8,128)(2,1)S(1)}, u32[]{:S(2)}, u32[]{:S(2)}) collective-permute-start(bf16[144,256]{1,0:T(8,128)(2,1)S(1)} %get-tuple-element.38), channel_id=1, source_target_pairs={{0,3},{1,2},{2,1},{3,0},{4,7},{5,6},{6,5},{7,4},{8,11},{9,10},{10,... | collective-permute-start | bytes 221192 | tf_op jit(solution)/shard_map/ppermute | solution.py:254
  18.0 4.6 %collective-permute-start.8 = (bf16[144,256]{1,0:T(8,128)(2,1)S(1)}, bf16[144,256]{1,0:T(8,128)(2,1)S(1)}, u32[]{:S(2)}, u32[]{:S(2)}) collective-permute-start(bf16[144,256]{1,0:T(8,128)(2,1)S(1)} %get-tuple-element.37), channel_id=1, source_target_pairs={{0,2},{1,3},{2,0},{3,1},{4,6},{5,7},{6,4},{7,5},{8,10},{9,11},{10,... | collective-permute-start | bytes 221192 | tf_op jit(solution)/shard_map/ppermute | solution.py:254
  18.5 4.4 %collective-permute-start.7 = (bf16[144,256]{1,0:T(8,128)(2,1)S(1)}, bf16[144,256]{1,0:T(8,128)(2,1)S(1)}, u32[]{:S(2)}, u32[]{:S(2)}) collective-permute-start(bf16[144,256]{1,0:T(8,128)(2,1)S(1)} %get-tuple-element.36), channel_id=1, source_target_pairs={{0,1},{1,0},{2,3},{3,2},{4,5},{5,4},{6,7},{7,6},{8,9},{9,8},{10,11... | collective-permute-start | bytes 221192 | tf_op jit(solution)/shard_map/ppermute | solution.py:254

commit v7 on v6

--- a/solution.py
+++ b/solution.py
@@ -9,6 +9,7 @@
 CHUNK = 256
 POWER = 17
 TOP = 128.0
+ABOVE = 1.01
 LEAST = 2.0**-100
 SMALLEST = 2.0**-126
 SPARE = 16
@@ -134,21 +135,21 @@
 def write_coded(out_ref, value):
     rows, width = value.shape
     largest = jnp.max(jnp.abs(value), axis=0, keepdims=True)
-    exponent = jnp.ceil(jnp.log2(jnp.maximum(largest, LEAST)))
-    scaled = value * (TOP * jnp.exp2(-exponent))
+    scale = jnp.maximum(largest * ABOVE, LEAST).astype(out_ref.dtype)
+    scaled = value * (TOP / scale.astype(jnp.float32))
     power = scaled
     for _ in range(POWER.bit_length() - 1):
         power = power * power
     out_ref[:rows, :] = (power * scaled).astype(out_ref.dtype)
-    out_ref[rows:, :] = jnp.broadcast_to(exponent, (SPARE, width)).astype(out_ref.dtype)
+    out_ref[rows:, :] = jnp.broadcast_to(scale, (SPARE, width))
 
 
 def read_coded(ref):
     rows = ref.shape[0] - SPARE
     power = ref[:rows, :].astype(jnp.float32)
-    exponent = ref[rows:, :].astype(jnp.float32)[:1, :]
+    scale = ref[rows:, :].astype(jnp.float32)[:1, :]
     size = jnp.exp2(jnp.log2(jnp.maximum(jnp.abs(power), SMALLEST)) * (1.0 / POWER))
-    size = jnp.where(power < 0, -size, size) * (jnp.exp2(exponent) * (1.0 / TOP))
+    size = jnp.where(power < 0, -size, size) * (scale * (1.0 / TOP))
     return jnp.where(power == 0, 0.0, size)
 
 

time: 23.9 us -> 23.9 us (level)
  no operation moved by 1% of the time
where the time goes in v7:
time: 23.9 us; the launch traced here: 23.7 us
  starting transfers between devices  10.3 us (43%)
  Pallas kernels  6.44 us (27%)
  waiting for transfers between devices  4.81 us (20%)
  between operations  2.11 us (9%)
    ppermute x10, starting transfers between devices, swap(): lax.ppermute(block, axis, [(n, n ^ step) for n in range(lax.axis_size(axi...  10.3 us
    ppermute x10, waiting for transfers between devices, swap(): lax.ppermute(block, axis, [(n, n ^ step) for n in range(lax.axis_size(axi...  4.81 us
    pallas_call x2, Pallas kernels, pack(): pl.pallas_call(lambda *refs: pack_kernel(plan, *refs), in_specs=[hbm()] *...  3.98 us
    pallas_call x1, Pallas kernels, shards(): pl.pallas_call(lambda *refs: scale_kernel(a_width, *refs), in_specs=[hbm(...  1.09 us
    pallas_call x1, Pallas kernels, shards(): pl.pallas_call(lambda *refs: place_kernel(run, *refs), in_specs=[vmem(),...  0.79 us
  transfers between devices with their start and end apart: 10, of which 7 were waited for; matrix products, arithmetic and copies ran while one was open for 0% of the time, Pallas kernels for 12%

profile of v7, /device:TPU:0, one launch (start us, length us, event | category | flops | bytes accessed | tf_op | source)
XLA Modules:
  0.0 23.7 jit_solution(14282444741211785802)
XLA Ops:
  0.7 2.4 %pack_far.1 = (bf16[2,128,128]{2,1,0:T(8,128)(2,1)}, bf16[2,128,128]{2,1,0:T(8,128)(2,1)}, bf16[2,128,128]{2,1,0:T(8,128)(2,1)}) custom-call(s32[1]{0:T(128)S(6)} %copy.12.refs_0_, s32[8]{0:T(128)} %refs_0_.3, s32[8]{0:T(128)} %refs_2_.5, bf16[1024,1024]{1,0:T(8,128)(2,1)} %bitcast.5), custom_call_target="tpu_custom_call" | custom-call | tf_op jit(solution)/shard_map/pack_far/pallas_call | solution.py:302
  3.1 4.1 %collective-permute-start.2 = (bf16[2,128,128]{2,1,0:T(8,128)(2,1)}, bf16[2,128,128]{2,1,0:T(8,128)(2,1)S(1)}, u32[]{:S(2)}, u32[]{:S(2)}) collective-permute-start(bf16[2,128,128]{2,1,0:T(8,128)(2,1)} %get-tuple-element.27), channel_id=1, source_target_pairs={{0,16},{4,20},{8,24},{12,28},{16,0},{20,4},{24,8},{28,12},{1,17},{... | collective-permute-start | bytes 196616 | tf_op jit(solution)/shard_map/ppermute | solution.py:255
  7.2 1.3 %collective-permute-start.3 = (bf16[2,128,128]{2,1,0:T(8,128)(2,1)}, bf16[2,128,128]{2,1,0:T(8,128)(2,1)S(1)}, u32[]{:S(2)}, u32[]{:S(2)}) collective-permute-start(bf16[2,128,128]{2,1,0:T(8,128)(2,1)} %get-tuple-element.28), channel_id=1, source_target_pairs={{0,24},{4,28},{8,16},{12,20},{16,8},{20,12},{24,0},{28,4},{1,25},{... | collective-permute-start | bytes 196616 | tf_op jit(solution)/shard_map/ppermute | solution.py:255
  8.5 0.2 collective-permute-start
  9.4 0.0 copy-start.3
  9.4 1.6 %pack_near.1 = (bf16[1,128,128]{2,1,0:T(8,128)(2,1)S(1)}, bf16[1,128,128]{2,1,0:T(8,128)(2,1)S(1)}, bf16[128,1024]{1,0:T(8,128)(2,1)S(1)}, f32[8,8,128]{2,1,0:T(8,128)S(1)}) custom-call(s32[1]{0:T(128)S(6)} %copy.12.refs_0_, s32[8]{0:T(128)S(1)} %copy-done, s32[8]{0:T(128)S(1)} %copy-done.1, bf16[1024,1024]{1,0:T(8,128)(2,1)} %bitcast.6, ...), custom_call_target="tpu_custom_call" | custom-call | tf_op jit(solution)/shard_map/pack_near/pallas_call | solution.py:302
  11.1 0.1 collective-permute-start.1
  11.2 0.5 %collective-permute-start.4 = (bf16[1,128,128]{2,1,0:T(8,128)(2,1)S(1)}, bf16[1,128,128]{2,1,0:T(8,128)(2,1)S(1)}, u32[]{:S(2)}, u32[]{:S(2)}) collective-permute-start(bf16[1,128,128]{2,1,0:T(8,128)(2,1)S(1)} %second.3), channel_id=1, source_target_pairs={{0,4},{4,0},{8,12},{12,8},{16,20},{20,16},{24,28},{28,24},{1,5},{5... | collective-permute-start | bytes 98312 | tf_op jit(solution)/shard_map/ppermute | solution.py:255
  11.6 2.0 %collective-permute-done.3.pair_ref.refs_3_ = bf16[2,128,128]{2,1,0:T(8,128)(2,1)S(1)} collective-permute-done((bf16[2,128,128]{2,1,0:T(8,128)(2,1)}, bf16[2,128,128]{2,1,0:T(8,128)(2,1)S(1)}, u32[]{:S(2)}, u32[]{:S(2)}) %collective-permute-start.3) | collective-permute-done | bytes 65568 | tf_op jit(solution)/shard_map/ppermute | solution.py:255
  13.6 0.1 collective-permute-done.pair_ref.refs_4_
  13.7 0.5 %collective-permute-start.6 = (bf16[1,128,128]{2,1,0:T(8,128)(2,1)S(1)}, bf16[1,128,128]{2,1,0:T(8,128)(2,1)S(1)}, u32[]{:S(2)}, u32[]{:S(2)}) collective-permute-start(bf16[1,128,128]{2,1,0:T(8,128)(2,1)S(1)} %second.5), channel_id=1, source_target_pairs={{0,4},{4,0},{8,12},{12,8},{16,20},{20,16},{24,28},{28,24},{1,5},{5... | collective-permute-start | bytes 98312 | tf_op jit(solution)/shard_map/ppermute | solution.py:255
  14.2 0.6 %collective-permute-done.5.refs_8_ = bf16[1,128,128]{2,1,0:T(8,128)(2,1)S(1)} collective-permute-done((bf16[1,128,128]{2,1,0:T(8,128)(2,1)S(1)}, bf16[1,128,128]{2,1,0:T(8,128)(2,1)S(1)}, u32[]{:S(2)}, u32[]{:S(2)}) %collective-permute-start.5) | collective-permute-done | bytes 32800 | tf_op jit(solution)/shard_map/ppermute | solution.py:255
  14.8 0.2 %collective-permute-done.6.refs_9_ = bf16[1,128,128]{2,1,0:T(8,128)(2,1)S(1)} collective-permute-done((bf16[1,128,128]{2,1,0:T(8,128)(2,1)S(1)}, bf16[1,128,128]{2,1,0:T(8,128)(2,1)S(1)}, u32[]{:S(2)}, u32[]{:S(2)}) %collective-permute-start.6) | collective-permute-done | bytes 32800 | tf_op jit(solution)/shard_map/ppermute | solution.py:255
  15.0 0.4 %multiply.1 = (bf16[144,256]{1,0:T(8,128)(2,1)S(1)}, bf16[144,256]{1,0:T(8,128)(2,1)S(1)}, bf16[144,256]{1,0:T(8,128)(2,1)S(1)}, f32[128,256]{1,0:T(8,128)S(1)}) custom-call(bf16[128,1024]{1,0:T(8,128)(2,1)S(1)} %get-tuple-element.22.refs_0_, f32[8,8,128]{2,1,0:T(8,128)S(1)} %get-tuple-element.26.refs_1_, ...), custom_call_target="tpu_custom_call" | custom-call | tf_op jit(solution)/shard_map/multiply/pallas_call | solution.py:348
  15.5 2.5 %collective-permute-start.9 = (bf16[144,256]{1,0:T(8,128)(2,1)S(1)}, bf16[144,256]{1,0:T(8,128)(2,1)S(1)}, u32[]{:S(2)}, u32[]{:S(2)}) collective-permute-start(bf16[144,256]{1,0:T(8,128)(2,1)S(1)} %get-tuple-element.38), channel_id=1, source_target_pairs={{0,3},{1,2},{2,1},{3,0},{4,7},{5,6},{6,5},{7,4},{8,11},{9,10},{10,... | collective-permute-start | bytes 221192 | tf_op jit(solution)/shard_map/ppermute | solution.py:255
  18.0 0.5 %collective-permute-start.8 = (bf16[144,256]{1,0:T(8,128)(2,1)S(1)}, bf16[144,256]{1,0:T(8,128)(2,1)S(1)}, u32[]{:S(2)}, u32[]{:S(2)}) collective-permute-start(bf16[144,256]{1,0:T(8,128)(2,1)S(1)} %get-tuple-element.37), channel_id=1, source_target_pairs={{0,2},{1,3},{2,0},{3,1},{4,6},{5,7},{6,4},{7,5},{8,10},{9,11},{10,... | collective-permute-start | bytes 221192 | tf_op jit(solution)/shard_map/ppermute | solution.py:255
  18.5 0.5 %collective-permute-start.7 = (bf16[144,256]{1,0:T(8,128)(2,1)S(1)}, bf16[144,256]{1,0:T(8,128)(2,1)S(1)}, u32[]{:S(2)}, u32[]{:S(2)}) collective-permute-start(bf16[144,256]{1,0:T(8,128)(2,1)S(1)} %get-tuple-element.36), channel_id=1, source_target_pairs={{0,1},{1,0},{2,3},{3,2},{4,5},{5,4},{6,7},{7,6},{8,9},{9,8},{10,11... | collective-permute-start | bytes 221192 | tf_op jit(solution)/shard_map/ppermute | solution.py:255
  19.7 1.1 %scale.1 = (f32[128,256]{1,0:T(8,128)S(1)}, f32[8,256]{1,0:T(8,128)S(1)}, f32[8,128,256]{2,1,0:T(8,128)}) custom-call(s32[8]{0:T(128)S(1)} %copy-done, s32[1]{0:T(128)S(6)} %copy.13.refs_4_.refs_1_, s32[8]{0:T(128)S(1)} %copy-done.1, f32[8]{0:T(128)S(1)} %copy-done.3, f32[1]{0:T(128)S(6)} %copy.14.refs_4_, f32[8,128]{1,0:T(8,128)S(1)} %bitcast.4, ...), custom_call_target="tpu_custom_call" | custom-call | tf_op jit(solution)/shard_map/scale/pallas_call | solution.py:358
  20.8 0.2 collective-permute-done.9.part_ref
  21.0 0.1 add.2.so_far_ref
  21.1 1.5 %collective-permute-done.8.part_ref = bf16[144,256]{1,0:T(8,128)(2,1)S(1)} collective-permute-done((bf16[144,256]{1,0:T(8,128)(2,1)S(1)}, bf16[144,256]{1,0:T(8,128)(2,1)S(1)}, u32[]{:S(2)}, u32[]{:S(2)}) %collective-permute-start.8) | collective-permute-done | bytes 73760 | tf_op jit(solution)/shard_map/ppermute | solution.py:255
  22.6 0.1 add.3.refs_4_
  22.6 0.2 collective-permute-done.7.refs_3_
  22.9 0.8 %place.1 = f32[8,128,256]{2,1,0:T(8,128)} custom-call(f32[128,256]{1,0:T(8,128)S(1)} %get-tuple-element.33.refs_0_, f32[8,256]{1,0:T(8,128)S(1)} %get-tuple-element.34.refs_1_, f32[8,128,256]{2,1,0:T(8,128)} %get-tuple-element.35.refs_2_, bf16[144,256]{1,0:T(8,128)(2,1)S(1)} %collective-permute-done.7.refs_3_, ...), custom_call_target="tpu_custom_call", output_to_operand_aliasing={{}: (2, {})} | custom-call | tf_op jit(solution)/shard_map/place/pallas_call | solution.py:406
  (14 shorter events, 0.0 us)
Async XLA Ops:
  0.0 9.4 %copy-start.1 = (s32[8]{0:T(128)S(1)}, s32[8]{0:T(128)}, u32[]{:S(2)}) copy-start(s32[8]{0:T(128)} %refs_2_.5) | copy-start | bytes 100
  0.0 9.4 %copy-start = (s32[8]{0:T(128)S(1)}, s32[8]{0:T(128)}, u32[]{:S(2)}) copy-start(s32[8]{0:T(128)} %refs_0_.3) | copy-start | bytes 100
  3.1 8.1 %collective-permute-start.2 = (bf16[2,128,128]{2,1,0:T(8,128)(2,1)}, bf16[2,128,128]{2,1,0:T(8,128)(2,1)S(1)}, u32[]{:S(2)}, u32[]{:S(2)}) collective-permute-start(bf16[2,128,128]{2,1,0:T(8,128)(2,1)} %get-tuple-element.27), channel_id=1, source_target_pairs={{0,16},{4,20},{8,24},{12,28},{16,0},{20,4},{24,8},{28,12},{1,17},{... | collective-permute-start | bytes 196616 | tf_op jit(solution)/shard_map/ppermute | solution.py:255
  7.2 6.4 %collective-permute-start.3 = (bf16[2,128,128]{2,1,0:T(8,128)(2,1)}, bf16[2,128,128]{2,1,0:T(8,128)(2,1)S(1)}, u32[]{:S(2)}, u32[]{:S(2)}) collective-permute-start(bf16[2,128,128]{2,1,0:T(8,128)(2,1)} %get-tuple-element.28), channel_id=1, source_target_pairs={{0,24},{4,28},{8,16},{12,20},{16,8},{20,12},{24,0},{28,4},{1,25},{... | collective-permute-start | bytes 196616 | tf_op jit(solution)/shard_map/ppermute | solution.py:255
  8.5 5.2 %collective-permute-start = (bf16[2,128,128]{2,1,0:T(8,128)(2,1)}, bf16[2,128,128]{2,1,0:T(8,128)(2,1)S(1)}, u32[]{:S(2)}, u32[]{:S(2)}) collective-permute-start(bf16[2,128,128]{2,1,0:T(8,128)(2,1)} %get-tuple-element.23), channel_id=1, source_target_pairs={{0,8},{4,12},{8,0},{12,4},{16,24},{20,28},{24,16},{28,20},{1,9},{5... | collective-permute-start | bytes 196616 | tf_op jit(solution)/shard_map/ppermute | solution.py:255
  9.4 10.3 %copy-start.2 = (f32[1024]{0:T(1024)S(1)}, f32[1024]{0:T(1024)}, u32[]{:S(2)}) copy-start(f32[1024]{0:T(1024)} %param.17) | copy-start | bytes 12292
  9.4 10.3 %copy-start.3 = (f32[8]{0:T(128)S(1)}, f32[8]{0:T(128)}, u32[]{:S(2)}) copy-start(f32[8]{0:T(128)} %refs_3_.1) | copy-start | bytes 100
  11.1 2.5 %collective-permute-start.1 = (bf16[1,128,128]{2,1,0:T(8,128)(2,1)S(1)}, bf16[1,128,128]{2,1,0:T(8,128)(2,1)S(1)}, u32[]{:S(2)}, u32[]{:S(2)}) collective-permute-start(bf16[1,128,128]{2,1,0:T(8,128)(2,1)S(1)} %get-tuple-element.24), channel_id=1, source_target_pairs={{0,4},{4,0},{8,12},{12,8},{16,20},{20,16},{24,28},{28,24},{1,5},{5... | collective-permute-start | bytes 98312 | tf_op jit(solution)/shard_map/ppermute | solution.py:255
  11.2 3.0 %collective-permute-start.4 = (bf16[1,128,128]{2,1,0:T(8,128)(2,1)S(1)}, bf16[1,128,128]{2,1,0:T(8,128)(2,1)S(1)}, u32[]{:S(2)}, u32[]{:S(2)}) collective-permute-start(bf16[1,128,128]{2,1,0:T(8,128)(2,1)S(1)} %second.3), channel_id=1, source_target_pairs={{0,4},{4,0},{8,12},{12,8},{16,20},{20,16},{24,28},{28,24},{1,5},{5... | collective-permute-start | bytes 98312 | tf_op jit(solution)/shard_map/ppermute | solution.py:255
  13.6 1.2 %collective-permute-start.5 = (bf16[1,128,128]{2,1,0:T(8,128)(2,1)S(1)}, bf16[1,128,128]{2,1,0:T(8,128)(2,1)S(1)}, u32[]{:S(2)}, u32[]{:S(2)}) collective-permute-start(bf16[1,128,128]{2,1,0:T(8,128)(2,1)S(1)} %second.4), channel_id=1, source_target_pairs={{0,4},{4,0},{8,12},{12,8},{16,20},{20,16},{24,28},{28,24},{1,5},{5... | collective-permute-start | bytes 98312 | tf_op jit(solution)/shard_map/ppermute | solution.py:255
  13.7 1.4 %collective-permute-start.6 = (bf16[1,128,128]{2,1,0:T(8,128)(2,1)S(1)}, bf16[1,128,128]{2,1,0:T(8,128)(2,1)S(1)}, u32[]{:S(2)}, u32[]{:S(2)}) collective-permute-start(bf16[1,128,128]{2,1,0:T(8,128)(2,1)S(1)} %second.5), channel_id=1, source_target_pairs={{0,4},{4,0},{8,12},{12,8},{16,20},{20,16},{24,28},{28,24},{1,5},{5... | collective-permute-start | bytes 98312 | tf_op jit(solution)/shard_map/ppermute | solution.py:255
  15.5 5.5 %collective-permute-start.9 = (bf16[144,256]{1,0:T(8,128)(2,1)S(1)}, bf16[144,256]{1,0:T(8,128)(2,1)S(1)}, u32[]{:S(2)}, u32[]{:S(2)}) collective-permute-start(bf16[144,256]{1,0:T(8,128)(2,1)S(1)} %get-tuple-element.38), channel_id=1, source_target_pairs={{0,3},{1,2},{2,1},{3,0},{4,7},{5,6},{6,5},{7,4},{8,11},{9,10},{10,... | collective-permute-start | bytes 221192 | tf_op jit(solution)/shard_map/ppermute | solution.py:255
  18.0 4.6 %collective-permute-start.8 = (bf16[144,256]{1,0:T(8,128)(2,1)S(1)}, bf16[144,256]{1,0:T(8,128)(2,1)S(1)}, u32[]{:S(2)}, u32[]{:S(2)}) collective-permute-start(bf16[144,256]{1,0:T(8,128)(2,1)S(1)} %get-tuple-element.37), channel_id=1, source_target_pairs={{0,2},{1,3},{2,0},{3,1},{4,6},{5,7},{6,4},{7,5},{8,10},{9,11},{10,... | collective-permute-start | bytes 221192 | tf_op jit(solution)/shard_map/ppermute | solution.py:255
  18.5 4.4 %collective-permute-start.7 = (bf16[144,256]{1,0:T(8,128)(2,1)S(1)}, bf16[144,256]{1,0:T(8,128)(2,1)S(1)}, u32[]{:S(2)}, u32[]{:S(2)}) collective-permute-start(bf16[144,256]{1,0:T(8,128)(2,1)S(1)} %get-tuple-element.36), channel_id=1, source_target_pairs={{0,1},{1,0},{2,3},{3,2},{4,5},{5,4},{6,7},{7,6},{8,9},{9,8},{10,11... | collective-permute-start | bytes 221192 | tf_op jit(solution)/shard_map/ppermute | solution.py:255

commit v8 on v6

--- a/solution.py
+++ b/solution.py
@@ -183,7 +183,7 @@
 
 
 def scale_kernel(
-    a_width, i_hbm, j_hbm, tile_hbm, ei_hbm, ej_hbm, ev_ref, after_hbm, denom_ref, run_ref,
+    a_width, i_hbm, j_hbm, tile_hbm, ei_hbm, ej_hbm, ev_ref, after_hbm, inverse_ref, run_ref,
     zero_hbm, i_ref, j_ref, tile_ref, ei_ref, ej_ref, column_ref, zero_ref, sems, zero_sems,
 ):
     copies = start_all(
@@ -218,7 +218,7 @@
         run_ref[:, columns] = jnp.full((run_ref.shape[0], width), chosen.astype(jnp.float32))
         sum_ab = a_energy[:, :width] + b_row
         for m in range(run):
-            denom_ref[m * a_width : (m + 1) * a_width, columns] = (
+            inverse_ref[m * a_width : (m + 1) * a_width, columns] = 1.0 / (
                 sum_ab - ei_ref[chosen * run + m] - ej_ref[0]
             )
     for copy in zero_copies:
@@ -229,7 +229,7 @@
     out_ref[...] = so_far_ref[...] + read_coded(part_ref)
 
 
-def place_kernel(run, denom_ref, run_ref, zero_hbm, *refs):
+def place_kernel(run, inverse_ref, run_ref, zero_hbm, *refs):
     parts_refs, out_hbm, block_ref, sems = refs[:-3], refs[-3], refs[-2], refs[-1]
     a_width, width = block_ref.shape[2:]
     spans = [slice(n * width, (n + 1) * width) for n in range(block_ref.shape[0])]
@@ -238,7 +238,7 @@
     for parts_ref in parts_refs[:-1]:
         coded = parts_ref.dtype != jnp.float32
         total = total + (read_coded(parts_ref) if coded else parts_ref[...])
-    scaled = total / denom_ref[...]
+    scaled = total * inverse_ref[...]
     copies = []
     for part, (columns, chosen) in enumerate(zip(spans, chosen_runs)):
         for m in range(run):
@@ -354,7 +354,7 @@
     )(chosen_w, choice, *left)
 
     out_shape = jax.ShapeDtypeStruct((rows_i, a_width, b_width), jnp.float32)
-    denom, run_row, zeros = pl.pallas_call(
+    inverse, run_row, zeros = pl.pallas_call(
         lambda *refs: scale_kernel(a_width, *refs),
         in_specs=[hbm()] * 5 + [vmem(), pl.BlockSpec(memory_space=pl.ANY)],
         out_specs=[vmem(), vmem(), hbm()],
@@ -414,7 +414,7 @@
         ],
         compiler_params=limit(16),
         name="place",
-    )(denom, run_row, zeros, *gathered)
+    )(inverse, run_row, zeros, *gathered)
     return result.reshape(rows_j, rows_i, a_width, b_width)
 
 

time: 23.9 us -> 23.9 us (level)
  no operation moved by 1% of the time
where the time goes in v8:
time: 23.9 us; the launch traced here: 23.7 us
  starting transfers between devices  10.3 us (43%)
  Pallas kernels  6.44 us (27%)
  waiting for transfers between devices  4.81 us (20%)
  between operations  2.1 us (9%)
    ppermute x10, starting transfers between devices, swap(): lax.ppermute(block, axis, [(n, n ^ step) for n in range(lax.axis_size(axi...  10.3 us
    ppermute x10, waiting for transfers between devices, swap(): lax.ppermute(block, axis, [(n, n ^ step) for n in range(lax.axis_size(axi...  4.81 us
    pallas_call x2, Pallas kernels, pack(): pl.pallas_call(lambda *refs: pack_kernel(plan, *refs), in_specs=[hbm()] *...  3.98 us
    pallas_call x1, Pallas kernels, shards(): pl.pallas_call(lambda *refs: scale_kernel(a_width, *refs), in_specs=[hbm(...  1.09 us
    pallas_call x1, Pallas kernels, shards(): pl.pallas_call(lambda *refs: place_kernel(run, *refs), in_specs=[vmem(),...  0.79 us
  transfers between devices with their start and end apart: 10, of which 7 were waited for; matrix products, arithmetic and copies ran while one was open for 0% of the time, Pallas kernels for 12%

profile of v8, /device:TPU:0, one launch (start us, length us, event | category | flops | bytes accessed | tf_op | source)
XLA Modules:
  0.0 23.7 jit_solution(16021442769225004325)
XLA Ops:
  0.7 2.4 %pack_far.1 = (bf16[2,128,128]{2,1,0:T(8,128)(2,1)}, bf16[2,128,128]{2,1,0:T(8,128)(2,1)}, bf16[2,128,128]{2,1,0:T(8,128)(2,1)}) custom-call(s32[1]{0:T(128)S(6)} %copy.12.refs_0_, s32[8]{0:T(128)} %refs_0_.3, s32[8]{0:T(128)} %refs_2_.5, bf16[1024,1024]{1,0:T(8,128)(2,1)} %bitcast.5), custom_call_target="tpu_custom_call" | custom-call | tf_op jit(solution)/shard_map/pack_far/pallas_call | solution.py:301
  3.1 4.1 %collective-permute-start.2 = (bf16[2,128,128]{2,1,0:T(8,128)(2,1)}, bf16[2,128,128]{2,1,0:T(8,128)(2,1)S(1)}, u32[]{:S(2)}, u32[]{:S(2)}) collective-permute-start(bf16[2,128,128]{2,1,0:T(8,128)(2,1)} %get-tuple-element.27), channel_id=1, source_target_pairs={{0,16},{4,20},{8,24},{12,28},{16,0},{20,4},{24,8},{28,12},{1,17},{... | collective-permute-start | bytes 196616 | tf_op jit(solution)/shard_map/ppermute | solution.py:254
  7.2 1.3 %collective-permute-start.3 = (bf16[2,128,128]{2,1,0:T(8,128)(2,1)}, bf16[2,128,128]{2,1,0:T(8,128)(2,1)S(1)}, u32[]{:S(2)}, u32[]{:S(2)}) collective-permute-start(bf16[2,128,128]{2,1,0:T(8,128)(2,1)} %get-tuple-element.28), channel_id=1, source_target_pairs={{0,24},{4,28},{8,16},{12,20},{16,8},{20,12},{24,0},{28,4},{1,25},{... | collective-permute-start | bytes 196616 | tf_op jit(solution)/shard_map/ppermute | solution.py:254
  8.5 0.2 collective-permute-start
  9.4 0.0 copy-start.2
  9.4 1.6 %pack_near.1 = (bf16[1,128,128]{2,1,0:T(8,128)(2,1)S(1)}, bf16[1,128,128]{2,1,0:T(8,128)(2,1)S(1)}, bf16[128,1024]{1,0:T(8,128)(2,1)S(1)}, f32[8,8,128]{2,1,0:T(8,128)S(1)}) custom-call(s32[1]{0:T(128)S(6)} %copy.12.refs_0_, s32[8]{0:T(128)S(1)} %copy-done, s32[8]{0:T(128)S(1)} %copy-done.1, bf16[1024,1024]{1,0:T(8,128)(2,1)} %bitcast.6, ...), custom_call_target="tpu_custom_call" | custom-call | tf_op jit(solution)/shard_map/pack_near/pallas_call | solution.py:301
  11.1 0.1 collective-permute-start.1
  11.2 0.5 %collective-permute-start.4 = (bf16[1,128,128]{2,1,0:T(8,128)(2,1)S(1)}, bf16[1,128,128]{2,1,0:T(8,128)(2,1)S(1)}, u32[]{:S(2)}, u32[]{:S(2)}) collective-permute-start(bf16[1,128,128]{2,1,0:T(8,128)(2,1)S(1)} %second.3), channel_id=1, source_target_pairs={{0,4},{4,0},{8,12},{12,8},{16,20},{20,16},{24,28},{28,24},{1,5},{5... | collective-permute-start | bytes 98312 | tf_op jit(solution)/shard_map/ppermute | solution.py:254
  11.6 2.0 %collective-permute-done.3.pair_ref.refs_3_ = bf16[2,128,128]{2,1,0:T(8,128)(2,1)S(1)} collective-permute-done((bf16[2,128,128]{2,1,0:T(8,128)(2,1)}, bf16[2,128,128]{2,1,0:T(8,128)(2,1)S(1)}, u32[]{:S(2)}, u32[]{:S(2)}) %collective-permute-start.3) | collective-permute-done | bytes 65568 | tf_op jit(solution)/shard_map/ppermute | solution.py:254
  13.6 0.1 collective-permute-done.pair_ref.refs_4_
  13.7 0.5 %collective-permute-start.6 = (bf16[1,128,128]{2,1,0:T(8,128)(2,1)S(1)}, bf16[1,128,128]{2,1,0:T(8,128)(2,1)S(1)}, u32[]{:S(2)}, u32[]{:S(2)}) collective-permute-start(bf16[1,128,128]{2,1,0:T(8,128)(2,1)S(1)} %second.5), channel_id=1, source_target_pairs={{0,4},{4,0},{8,12},{12,8},{16,20},{20,16},{24,28},{28,24},{1,5},{5... | collective-permute-start | bytes 98312 | tf_op jit(solution)/shard_map/ppermute | solution.py:254
  14.2 0.6 %collective-permute-done.5.refs_8_ = bf16[1,128,128]{2,1,0:T(8,128)(2,1)S(1)} collective-permute-done((bf16[1,128,128]{2,1,0:T(8,128)(2,1)S(1)}, bf16[1,128,128]{2,1,0:T(8,128)(2,1)S(1)}, u32[]{:S(2)}, u32[]{:S(2)}) %collective-permute-start.5) | collective-permute-done | bytes 32800 | tf_op jit(solution)/shard_map/ppermute | solution.py:254
  14.8 0.2 %collective-permute-done.6.refs_9_ = bf16[1,128,128]{2,1,0:T(8,128)(2,1)S(1)} collective-permute-done((bf16[1,128,128]{2,1,0:T(8,128)(2,1)S(1)}, bf16[1,128,128]{2,1,0:T(8,128)(2,1)S(1)}, u32[]{:S(2)}, u32[]{:S(2)}) %collective-permute-start.6) | collective-permute-done | bytes 32800 | tf_op jit(solution)/shard_map/ppermute | solution.py:254
  15.0 0.4 %multiply.1 = (bf16[144,256]{1,0:T(8,128)(2,1)S(1)}, bf16[144,256]{1,0:T(8,128)(2,1)S(1)}, bf16[144,256]{1,0:T(8,128)(2,1)S(1)}, f32[128,256]{1,0:T(8,128)S(1)}) custom-call(bf16[128,1024]{1,0:T(8,128)(2,1)S(1)} %get-tuple-element.22.refs_0_, f32[8,8,128]{2,1,0:T(8,128)S(1)} %get-tuple-element.26.refs_1_, ...), custom_call_target="tpu_custom_call" | custom-call | tf_op jit(solution)/shard_map/multiply/pallas_call | solution.py:347
  15.5 2.5 %collective-permute-start.9 = (bf16[144,256]{1,0:T(8,128)(2,1)S(1)}, bf16[144,256]{1,0:T(8,128)(2,1)S(1)}, u32[]{:S(2)}, u32[]{:S(2)}) collective-permute-start(bf16[144,256]{1,0:T(8,128)(2,1)S(1)} %get-tuple-element.38), channel_id=1, source_target_pairs={{0,3},{1,2},{2,1},{3,0},{4,7},{5,6},{6,5},{7,4},{8,11},{9,10},{10,... | collective-permute-start | bytes 221192 | tf_op jit(solution)/shard_map/ppermute | solution.py:254
  18.0 0.5 %collective-permute-start.8 = (bf16[144,256]{1,0:T(8,128)(2,1)S(1)}, bf16[144,256]{1,0:T(8,128)(2,1)S(1)}, u32[]{:S(2)}, u32[]{:S(2)}) collective-permute-start(bf16[144,256]{1,0:T(8,128)(2,1)S(1)} %get-tuple-element.37), channel_id=1, source_target_pairs={{0,2},{1,3},{2,0},{3,1},{4,6},{5,7},{6,4},{7,5},{8,10},{9,11},{10,... | collective-permute-start | bytes 221192 | tf_op jit(solution)/shard_map/ppermute | solution.py:254
  18.5 0.5 %collective-permute-start.7 = (bf16[144,256]{1,0:T(8,128)(2,1)S(1)}, bf16[144,256]{1,0:T(8,128)(2,1)S(1)}, u32[]{:S(2)}, u32[]{:S(2)}) collective-permute-start(bf16[144,256]{1,0:T(8,128)(2,1)S(1)} %get-tuple-element.36), channel_id=1, source_target_pairs={{0,1},{1,0},{2,3},{3,2},{4,5},{5,4},{6,7},{7,6},{8,9},{9,8},{10,11... | collective-permute-start | bytes 221192 | tf_op jit(solution)/shard_map/ppermute | solution.py:254
  19.7 1.1 %scale.1 = (f32[128,256]{1,0:T(8,128)S(1)}, f32[8,256]{1,0:T(8,128)S(1)}, f32[8,128,256]{2,1,0:T(8,128)}) custom-call(s32[8]{0:T(128)S(1)} %copy-done, s32[1]{0:T(128)S(6)} %copy.13.refs_4_.refs_1_, s32[8]{0:T(128)S(1)} %copy-done.1, f32[8]{0:T(128)S(1)} %copy-done.3, f32[1]{0:T(128)S(6)} %copy.14.refs_4_, f32[8,128]{1,0:T(8,128)S(1)} %bitcast.4, ...), custom_call_target="tpu_custom_call" | custom-call | tf_op jit(solution)/shard_map/scale/pallas_call | solution.py:357
  20.8 0.2 collective-permute-done.9.part_ref
  21.0 0.1 add.2.so_far_ref
  21.1 1.5 %collective-permute-done.8.part_ref = bf16[144,256]{1,0:T(8,128)(2,1)S(1)} collective-permute-done((bf16[144,256]{1,0:T(8,128)(2,1)S(1)}, bf16[144,256]{1,0:T(8,128)(2,1)S(1)}, u32[]{:S(2)}, u32[]{:S(2)}) %collective-permute-start.8) | collective-permute-done | bytes 73760 | tf_op jit(solution)/shard_map/ppermute | solution.py:254
  22.6 0.1 add.3.refs_4_
  22.6 0.2 %collective-permute-done.7.refs_3_ = bf16[144,256]{1,0:T(8,128)(2,1)S(1)} collective-permute-done((bf16[144,256]{1,0:T(8,128)(2,1)S(1)}, bf16[144,256]{1,0:T(8,128)(2,1)S(1)}, u32[]{:S(2)}, u32[]{:S(2)}) %collective-permute-start.7) | collective-permute-done | bytes 73760 | tf_op jit(solution)/shard_map/ppermute | solution.py:254
  22.9 0.8 %place.1 = f32[8,128,256]{2,1,0:T(8,128)} custom-call(f32[128,256]{1,0:T(8,128)S(1)} %get-tuple-element.33.refs_0_, f32[8,256]{1,0:T(8,128)S(1)} %get-tuple-element.34.refs_1_, f32[8,128,256]{2,1,0:T(8,128)} %get-tuple-element.35.refs_2_, bf16[144,256]{1,0:T(8,128)(2,1)S(1)} %collective-permute-done.7.refs_3_, ...), custom_call_target="tpu_custom_call", output_to_operand_aliasing={{}: (2, {})} | custom-call | tf_op jit(solution)/shard_map/place/pallas_call | solution.py:405
  (14 shorter events, 0.0 us)
Async XLA Ops:
  0.0 9.4 %copy-start.1 = (s32[8]{0:T(128)S(1)}, s32[8]{0:T(128)}, u32[]{:S(2)}) copy-start(s32[8]{0:T(128)} %refs_2_.5) | copy-start | bytes 100
  0.0 9.4 %copy-start = (s32[8]{0:T(128)S(1)}, s32[8]{0:T(128)}, u32[]{:S(2)}) copy-start(s32[8]{0:T(128)} %refs_0_.3) | copy-start | bytes 100
  3.1 8.1 %collective-permute-start.2 = (bf16[2,128,128]{2,1,0:T(8,128)(2,1)}, bf16[2,128,128]{2,1,0:T(8,128)(2,1)S(1)}, u32[]{:S(2)}, u32[]{:S(2)}) collective-permute-start(bf16[2,128,128]{2,1,0:T(8,128)(2,1)} %get-tuple-element.27), channel_id=1, source_target_pairs={{0,16},{4,20},{8,24},{12,28},{16,0},{20,4},{24,8},{28,12},{1,17},{... | collective-permute-start | bytes 196616 | tf_op jit(solution)/shard_map/ppermute | solution.py:254
  7.2 6.4 %collective-permute-start.3 = (bf16[2,128,128]{2,1,0:T(8,128)(2,1)}, bf16[2,128,128]{2,1,0:T(8,128)(2,1)S(1)}, u32[]{:S(2)}, u32[]{:S(2)}) collective-permute-start(bf16[2,128,128]{2,1,0:T(8,128)(2,1)} %get-tuple-element.28), channel_id=1, source_target_pairs={{0,24},{4,28},{8,16},{12,20},{16,8},{20,12},{24,0},{28,4},{1,25},{... | collective-permute-start | bytes 196616 | tf_op jit(solution)/shard_map/ppermute | solution.py:254
  8.5 5.2 %collective-permute-start = (bf16[2,128,128]{2,1,0:T(8,128)(2,1)}, bf16[2,128,128]{2,1,0:T(8,128)(2,1)S(1)}, u32[]{:S(2)}, u32[]{:S(2)}) collective-permute-start(bf16[2,128,128]{2,1,0:T(8,128)(2,1)} %get-tuple-element.23), channel_id=1, source_target_pairs={{0,8},{4,12},{8,0},{12,4},{16,24},{20,28},{24,16},{28,20},{1,9},{5... | collective-permute-start | bytes 196616 | tf_op jit(solution)/shard_map/ppermute | solution.py:254
  9.4 10.3 %copy-start.2 = (f32[1024]{0:T(1024)S(1)}, f32[1024]{0:T(1024)}, u32[]{:S(2)}) copy-start(f32[1024]{0:T(1024)} %param.17) | copy-start | bytes 12292
  9.4 10.3 %copy-start.3 = (f32[8]{0:T(128)S(1)}, f32[8]{0:T(128)}, u32[]{:S(2)}) copy-start(f32[8]{0:T(128)} %refs_3_.1) | copy-start | bytes 100
  11.1 2.5 %collective-permute-start.1 = (bf16[1,128,128]{2,1,0:T(8,128)(2,1)S(1)}, bf16[1,128,128]{2,1,0:T(8,128)(2,1)S(1)}, u32[]{:S(2)}, u32[]{:S(2)}) collective-permute-start(bf16[1,128,128]{2,1,0:T(8,128)(2,1)S(1)} %get-tuple-element.24), channel_id=1, source_target_pairs={{0,4},{4,0},{8,12},{12,8},{16,20},{20,16},{24,28},{28,24},{1,5},{5... | collective-permute-start | bytes 98312 | tf_op jit(solution)/shard_map/ppermute | solution.py:254
  11.2 3.0 %collective-permute-start.4 = (bf16[1,128,128]{2,1,0:T(8,128)(2,1)S(1)}, bf16[1,128,128]{2,1,0:T(8,128)(2,1)S(1)}, u32[]{:S(2)}, u32[]{:S(2)}) collective-permute-start(bf16[1,128,128]{2,1,0:T(8,128)(2,1)S(1)} %second.3), channel_id=1, source_target_pairs={{0,4},{4,0},{8,12},{12,8},{16,20},{20,16},{24,28},{28,24},{1,5},{5... | collective-permute-start | bytes 98312 | tf_op jit(solution)/shard_map/ppermute | solution.py:254
  13.6 1.2 %collective-permute-start.5 = (bf16[1,128,128]{2,1,0:T(8,128)(2,1)S(1)}, bf16[1,128,128]{2,1,0:T(8,128)(2,1)S(1)}, u32[]{:S(2)}, u32[]{:S(2)}) collective-permute-start(bf16[1,128,128]{2,1,0:T(8,128)(2,1)S(1)} %second.4), channel_id=1, source_target_pairs={{0,4},{4,0},{8,12},{12,8},{16,20},{20,16},{24,28},{28,24},{1,5},{5... | collective-permute-start | bytes 98312 | tf_op jit(solution)/shard_map/ppermute | solution.py:254
  13.7 1.4 %collective-permute-start.6 = (bf16[1,128,128]{2,1,0:T(8,128)(2,1)S(1)}, bf16[1,128,128]{2,1,0:T(8,128)(2,1)S(1)}, u32[]{:S(2)}, u32[]{:S(2)}) collective-permute-start(bf16[1,128,128]{2,1,0:T(8,128)(2,1)S(1)} %second.5), channel_id=1, source_target_pairs={{0,4},{4,0},{8,12},{12,8},{16,20},{20,16},{24,28},{28,24},{1,5},{5... | collective-permute-start | bytes 98312 | tf_op jit(solution)/shard_map/ppermute | solution.py:254
  15.5 5.5 %collective-permute-start.9 = (bf16[144,256]{1,0:T(8,128)(2,1)S(1)}, bf16[144,256]{1,0:T(8,128)(2,1)S(1)}, u32[]{:S(2)}, u32[]{:S(2)}) collective-permute-start(bf16[144,256]{1,0:T(8,128)(2,1)S(1)} %get-tuple-element.38), channel_id=1, source_target_pairs={{0,3},{1,2},{2,1},{3,0},{4,7},{5,6},{6,5},{7,4},{8,11},{9,10},{10,... | collective-permute-start | bytes 221192 | tf_op jit(solution)/shard_map/ppermute | solution.py:254
  18.0 4.6 %collective-permute-start.8 = (bf16[144,256]{1,0:T(8,128)(2,1)S(1)}, bf16[144,256]{1,0:T(8,128)(2,1)S(1)}, u32[]{:S(2)}, u32[]{:S(2)}) collective-permute-start(bf16[144,256]{1,0:T(8,128)(2,1)S(1)} %get-tuple-element.37), channel_id=1, source_target_pairs={{0,2},{1,3},{2,0},{3,1},{4,6},{5,7},{6,4},{7,5},{8,10},{9,11},{10,... | collective-permute-start | bytes 221192 | tf_op jit(solution)/shard_map/ppermute | solution.py:254
  18.5 4.4 %collective-permute-start.7 = (bf16[144,256]{1,0:T(8,128)(2,1)S(1)}, bf16[144,256]{1,0:T(8,128)(2,1)S(1)}, u32[]{:S(2)}, u32[]{:S(2)}) collective-permute-start(bf16[144,256]{1,0:T(8,128)(2,1)S(1)} %get-tuple-element.36), channel_id=1, source_target_pairs={{0,1},{1,0},{2,3},{3,2},{4,5},{5,4},{6,7},{7,6},{8,9},{9,8},{10,11... | collective-permute-start | bytes 221192 | tf_op jit(solution)/shard_map/ppermute | solution.py:254
